TPU v7x, 256 devices: a whole 4x4x8 slice. The times are simulated.
256 devices in a mesh: dp: 64 (over x, z, y_hi), space: 4 (over y_lo, core).
Axes of the slice: x: 4, y: 4 (y_hi: 2, y_lo: 2; y = y_hi * 2 + y_lo), z: 8, core: 2. Of those that a mesh axis runs over, the one named last changes fastest.
Arguments:
- section_input: bfloat16 [64, 2, 4, 64, 640], P('dp', None, 'space'), may hold values from -6 to 6
- target: bfloat16 [64, 2, 4, 64, 640], P('dp', None, 'space'), may hold values from -6 to 6
- conv_weight: bfloat16 [3, 3, 640, 640], replicated, may hold values from -0.078125 to 0.078125
- conv_bias: float32 [640], replicated, may hold values from -3 to 3
- norm_gain: float32 [640], replicated, may hold values from 0.5 to 1.5
- qkv_weight: bfloat16 [640, 1920], replicated, may hold values from -1 to 1
- out_weight: bfloat16 [640, 640], replicated, may hold values from -0.25 to 0.25
- time_weight: bfloat16 [320, 640], replicated, may hold values from -0.3125 to 0.3125
- timesteps: int32 [64], P('dp'), may hold values from 0 to 999
- labels: int32 [64], P('dp'), may hold values from 0 to 1
- ref_error: float32 [64, 2], P('dp'), may hold values from 4 to 6
Outputs:
- input_grad: bfloat16 [64, 2, 4, 64, 640], P('dp', None, 'space')
- conv_weight_grad: float32 [3, 3, 640, 640], P(None, None, None, 'dp')
- qkv_weight_grad: float32 [640, 1920], P(None, 'dp')
- out_weight_grad: float32 [640, 640], P(None, 'dp')
- time_weight_grad: float32 [320, 640], P(None, 'dp')
- gain_grad: float32 [640], P('dp')
- bias_grad: float32 [640], P('dp')
- pair_loss: float32 [64], P('dp')
All inputs are finite; a program needn't handle non-finite values.
Results may differ from a plain program's by a relative error of at most 0.027.
Values may be sent and summed in bfloat16 or wider, within the bound.
No kernel may reach another device: no remote copies, remote signals or barrier semaphores. Data moves between devices by JAX's collectives and lax.ppermute only.
A program may use at most 128 MiB of HBM per device.

v0:
```python
import math

import jax
import jax.numpy as jnp
import numpy as np
from jax import lax
from jax.experimental import pallas as pl
from jax.experimental.pallas import tpu as pltpu
from jax.sharding import Mesh
from jax.sharding import PartitionSpec as P

HEADS = 10
GROUPS = 32
TDIM = 320
C = 640
COLS = 64
ROWS = 4
TOK = 2 * ROWS * COLS
IMG = ROWS * COLS
BAND = 2 * COLS
HEAD_PAIRS = HEADS // 2
GROUP_COUNT = ROWS * COLS * (C // GROUPS)
SCALE = 1.0 / math.sqrt(C // HEADS)
EPS = 1e-05
BETA = 2.0

PAIR_AXES = ("x", "z", "y_hi")
SPACE_AXES = ("y_lo", "core")
MESH_AXES = ("x", "z", "y_hi", "y_lo", "core")
MESH_SHAPE = (4, 8, 2, 2, 2)
OWN = C // 64
TAP_BLOCKS = 12
BLOCKS = 5 + TAP_BLOCKS
WIDTH = BLOCKS * 128
CHUNK = 176
MIB = 1024 * 1024

f32 = jnp.float32
bf16 = jnp.bfloat16

NN = (((1,), (0,)), ((), ()))
NT = (((1,), (1,)), ((), ()))
TN = (((0,), (0,)), ((), ()))


def dot(a, b, dims=NN):
    return lax.dot_general(a, b, dims, preferred_element_type=f32)


def owner_columns():
    n = np.arange(C)
    x, y, z, j = n // 160, (n % 160) // 80, (n % 80) // OWN, n % OWN
    owner = 16 * x + 2 * z + y
    table = np.zeros((8, C), np.int32)
    table[0] = 3 * OWN * owner + j
    table[1] = OWN * owner + j
    return table


def frequencies():
    half = TDIM // 2
    return np.exp(-math.log(10000.0) * (np.arange(TDIM) % half) / half).astype(np.float32)[None]


def row(i):
    return pl.ds(i, 1)


def group_sums(rows):
    a = lax.broadcasted_iota(jnp.int32, (C, C), 0)
    b = lax.broadcasted_iota(jnp.int32, (C, C), 1)
    same = ((a * 3277) >> 16) == ((b * 3277) >> 16)
    ones = jnp.where(same, 1.0, 0.0).astype(bf16)
    high = rows.astype(bf16).astype(f32)
    rest = rows - high
    middle = rest.astype(bf16).astype(f32)
    low = rest - middle
    stack = jnp.concatenate([high, middle, low, jnp.zeros_like(rows)], axis=0).astype(bf16)
    sums = dot(stack, ones)
    return sums[0:4] + sums[4:8] + sums[8:12]


def sigmoid(v):
    return 1.0 / (1.0 + jnp.exp(-v))


def blocks():
    return [(r, m, (2 * r + m) * COLS) for r in range(ROWS) for m in range(2)]


def shifted(v, step):
    at = lax.broadcasted_iota(jnp.int32, (COLS, C), 0)
    if step == 1:
        return jnp.where(at == 0, 0.0, pltpu.roll(v, 1, 0))
    return jnp.where(at == COLS - 1, 0.0, pltpu.roll(v, COLS - 1, 0))


def head_halves(v):
    lane = lax.broadcasted_iota(jnp.int32, (1, 128), 1)
    first = jnp.where(lane < 64, 1.0, 0.0).astype(bf16)
    second = jnp.where(lane < 64, 0.0, 1.0).astype(bf16)
    return jnp.concatenate([v * first, v * second], axis=0)


def head_join(v):
    lane = lax.broadcasted_iota(jnp.int32, (IMG, 128), 1)
    return jnp.where(lane < 64, v[:IMG], v[IMG:])


def pair_kernel(
    part_ref,
    step_ref,
    label_ref,
    error_ref,
    x_ref,
    t_ref,
    conv_ref,
    bias_ref,
    gain_ref,
    qkvw_ref,
    outw_ref,
    timew_ref,
    freq_ref,
    table_ref,
    wire_ref,
    cg_ref,
    own_ref,
    stat_ref,
    margin_ref,
    acat,
    acc,
    resid,
    qkv,
    probs,
    attended,
    dev,
    gall,
    dattn,
    asel,
    feats_s,
):
    part = part_ref[0]
    sums, squares = [], []
    for m in range(2):
        total = jnp.zeros((1, C), f32)
        square = jnp.zeros((1, C), f32)
        for r in range(ROWS):
            v = x_ref[pl.ds((2 * r + m) * COLS, COLS), :].astype(f32)
            total = total + jnp.sum(v, axis=0, keepdims=True)
            square = square + jnp.sum(v * v, axis=0, keepdims=True)
        sums.append(total)
        squares.append(square)
    moments = group_sums(jnp.concatenate(sums + squares, axis=0)) / GROUP_COUNT
    mean = moments[0:2]
    inv = lax.rsqrt(moments[2:4] - mean * mean + EPS)
    stat_ref[...] = jnp.concatenate([mean, inv, jnp.zeros((4, C), f32)], axis=0)
    gain = gain_ref[...]
    acat[0:BAND, :] = jnp.zeros((BAND, 3 * C), bf16)
    acat[pl.ds(BAND + TOK, BAND), :] = jnp.zeros((BAND, 3 * C), bf16)
    for r, m, at in blocks():
        v = x_ref[pl.ds(at, COLS), :].astype(f32)
        a = (v - mean[m : m + 1]) * inv[m : m + 1] * gain
        act = a * sigmoid(a)
        here = pl.ds(BAND + at, COLS)
        acat[here, 0:C] = shifted(act, 1).astype(bf16)
        acat[here, C : 2 * C] = act.astype(bf16)
        acat[here, 2 * C : 3 * C] = shifted(act, -1).astype(bf16)
    angle = step_ref[0].astype(f32) * freq_ref[...]
    lane = lax.broadcasted_iota(jnp.int32, (1, TDIM), 1)
    feats = jnp.where(lane < TDIM // 2, jnp.cos(angle), jnp.sin(angle))
    feats_s[...] = jnp.zeros((8, 384), f32)
    feats_s[0:1, 0:TDIM] = feats
    feats_s[0:1, TDIM : TDIM + 1] = jnp.ones((1, 1), f32)
    shift = dot(jnp.broadcast_to(feats, (16, TDIM)).astype(bf16), timew_ref[...])[0:1]
    offset = shift + bias_ref[...]
    acc[...] = dot(acat[0:TOK, :], conv_ref[0])
    acc[...] += dot(acat[pl.ds(BAND, TOK), :], conv_ref[1])
    acc[...] += dot(acat[pl.ds(2 * BAND, TOK), :], conv_ref[2])
    resid[...] = (x_ref[...].astype(f32) + acc[...] + offset).astype(bf16)
    for third in range(3):
        cols = pl.ds(third * C, C)
        proj = dot(resid[...], qkvw_ref[:, cols]).astype(bf16)
        for r, m, at in blocks():
            qkv[m, pl.ds(r * COLS, COLS), cols] = proj[at : at + COLS]
    for m in range(2):
        for h in range(HEAD_PAIRS):
            q2 = head_halves(qkv[m, :, pl.ds(h * 128, 128)])
            k = qkv[m, :, pl.ds(C + h * 128, 128)]
            v = qkv[m, :, pl.ds(2 * C + h * 128, 128)]
            scores = dot(k, q2, NT) * SCALE
            exps = jnp.exp(scores - jnp.max(scores, axis=0, keepdims=True))
            p = exps * (1.0 / jnp.sum(exps, axis=0, keepdims=True))
            probs[m * HEAD_PAIRS + h] = p
            joined = head_join(dot(p.astype(bf16), v, TN)).astype(bf16)
            for r in range(ROWS):
                attended[pl.ds((2 * r + m) * COLS, COLS), pl.ds(h * 128, 128)] = joined[
                    r * COLS : (r + 1) * COLS
                ]
    dev[...] = (
        resid[...].astype(f32) + dot(attended[...], outw_ref[...]) - t_ref[...].astype(f32)
    )
    margin = jnp.zeros((1, 1), f32)
    signs = []
    for m in range(2):
        total = jnp.zeros((1, C), f32)
        for r in range(ROWS):
            d = dev[pl.ds((2 * r + m) * COLS, COLS), :]
            total = total + jnp.sum(d * d, axis=0, keepdims=True)
        error = jnp.sum(total, axis=1, keepdims=True) / (IMG * C)
        sign = jnp.where(label_ref[0] == m, 1.0, -1.0)
        signs.append(sign)
        margin = margin + sign * (error - error_ref[0, m])
    margin_ref[...] = jnp.broadcast_to(margin, (8, 128))
    slope = BETA * sigmoid(BETA * margin)
    for r, m, at in blocks():
        here = pl.ds(at, COLS)
        gall[here, 3 * C : 4 * C] = (signs[m] * slope * dev[here, :]).astype(bf16)
    out_grad = gall[:, 3 * C : 4 * C]
    da = dot(out_grad, outw_ref[...], NT).astype(bf16)
    for r, m, at in blocks():
        dattn[m, pl.ds(r * COLS, COLS), :] = da[at : at + COLS]
    for m in range(2):
        for h in range(HEAD_PAIRS):
            q2 = head_halves(qkv[m, :, pl.ds(h * 128, 128)])
            k = qkv[m, :, pl.ds(C + h * 128, 128)]
            v = qkv[m, :, pl.ds(2 * C + h * 128, 128)]
            da2 = head_halves(dattn[m, :, pl.ds(h * 128, 128)])
            p = probs[m * HEAD_PAIRS + h]
            dp = dot(v, da2, NT)
            dots = jnp.sum(p * dp, axis=0, keepdims=True)
            ds = (p * (dp - dots) * SCALE).astype(bf16)
            dq = head_join(dot(ds, k, TN)).astype(bf16)
            dk = dot(ds, q2).astype(bf16)
            dv = dot(p.astype(bf16), da2).astype(bf16)
            for r in range(ROWS):
                here = pl.ds((2 * r + m) * COLS, COLS)
                rows = slice(r * COLS, (r + 1) * COLS)
                gall[here, pl.ds(h * 128, 128)] = dq[rows]
                gall[here, pl.ds(C + h * 128, 128)] = dk[rows]
                gall[here, pl.ds(2 * C + h * 128, 128)] = dv[rows]
    acc[...] = out_grad.astype(f32) + dot(gall[:, 0 : 3 * C], qkvw_ref[...], NT)
    cg_ref[...] = acc[...].astype(bf16)
    own_ref[...] = acc[pl.ds(pl.multiple_of(part * BAND, BAND), BAND), :]
    at_row = lax.broadcasted_iota(jnp.int32, (C, C), 0)
    pick = jnp.where(at_row == table_ref[1:2, :], 1.0, 0.0).astype(bf16)
    conv_grad = dot(cg_ref[...], pick).astype(bf16)
    for k in range(TAP_BLOCKS):
        place = part * TAP_BLOCKS + k
        cols = slice(k * 128, (k + 1) * 128)

        def tap(place=place, cols=cols):
            up = place // 15
            lane = pl.multiple_of((place - 15 * up) * 128, 128)
            asel[:, cols] = acat[pl.ds(pl.multiple_of(up * BAND, BAND), TOK), pl.ds(lane, 128)]

        if k < 9:
            tap()
        else:
            pl.when(part < 3)(tap)

            @pl.when(part == 3)
            def _(k=k, cols=cols):
                f = feats_s[0:1, (k - 9) * 128 : (k - 8) * 128]
                asel[:, cols] = jnp.broadcast_to(f, (TOK, 128)).astype(bf16)

    wire_ref[:, C:] = dot(conv_grad, asel[...], TN).astype(bf16)

    @pl.when(part < 3)
    def _():
        rows = lax.broadcasted_iota(jnp.int32, (3 * C, C), 0)
        third = jnp.where(rows == table_ref[0:1, :] + OWN * part, 1.0, 0.0).astype(bf16)
        g = dot(gall[:, 0 : 3 * C], third).astype(bf16)
        wire_ref[:, 0:C] = dot(g, resid[...], TN).astype(bf16)

    @pl.when(part == 3)
    def _():
        g = dot(gall[:, 3 * C : 4 * C], pick).astype(bf16)
        wire_ref[:, 0:C] = dot(g, attended[...], TN).astype(bf16)


def pair_call(part, steps, labels, errors, x, t, conv, bias, gain, qkvw, outw, timew):
    smem = pl.BlockSpec(memory_space=pltpu.SMEM)
    vmem = pl.BlockSpec(memory_space=pltpu.VMEM)
    return pl.pallas_call(
        pair_kernel,
        out_shape=(
            jax.ShapeDtypeStruct((C, WIDTH), bf16),
            jax.ShapeDtypeStruct((TOK, C), bf16),
            jax.ShapeDtypeStruct((BAND, C), f32),
            jax.ShapeDtypeStruct((8, C), f32),
            jax.ShapeDtypeStruct((8, 128), f32),
        ),
        in_specs=[smem] * 4 + [vmem] * 10,
        out_specs=[vmem] * 5,
        scratch_shapes=[
            pltpu.VMEM((TOK + 2 * BAND, 3 * C), bf16),
            pltpu.VMEM((TOK, C), f32),
            pltpu.VMEM((TOK, C), bf16),
            pltpu.VMEM((2, IMG, 3 * C), bf16),
            pltpu.VMEM((2 * HEAD_PAIRS, IMG, 2 * IMG), f32),
            pltpu.VMEM((TOK, C), bf16),
            pltpu.VMEM((TOK, C), f32),
            pltpu.VMEM((TOK, 4 * C), bf16),
            pltpu.VMEM((2, IMG, C), bf16),
            pltpu.VMEM((TOK, TAP_BLOCKS * 128), bf16),
            pltpu.VMEM((8, 384), f32),
        ],
        compiler_params=pltpu.CompilerParams(vmem_limit_bytes=56 * MIB),
        name="pair",
    )(
        part,
        steps,
        labels,
        errors,
        x,
        t,
        conv,
        bias,
        gain,
        qkvw,
        outw,
        timew,
        frequencies(),
        owner_columns(),
    )


def input_kernel(
    part_ref, x_ref, cg_ref, own_ref, stat_ref, gain_ref, conv_ref, in_ref, gg_ref, gcat, acc
):
    part = part_ref[0]
    gcat[0:BAND, :] = jnp.zeros((BAND, 3 * C), bf16)
    gcat[pl.ds(BAND + TOK, BAND), :] = jnp.zeros((BAND, 3 * C), bf16)
    for r, m, at in blocks():
        g = cg_ref[pl.ds(at, COLS), :]
        here = pl.ds(BAND + at, COLS)
        gcat[here, 0:C] = shifted(g.astype(f32), -1).astype(bf16)
        gcat[here, C : 2 * C] = g
        gcat[here, 2 * C : 3 * C] = shifted(g.astype(f32), 1).astype(bf16)
    for i in range(3):
        for j in range(3):
            term = dot(
                gcat[pl.ds((2 - i) * BAND, TOK), j * C : (j + 1) * C],
                conv_ref[i, j * C : (j + 1) * C, :],
                NT,
            )
            if i == 0 and j == 0:
                acc[...] = term
            else:
                acc[...] += term
    gain = gain_ref[...]
    gain_sum = jnp.zeros((1, C), f32)
    ones = [jnp.zeros((1, C), f32) for _ in range(2)]
    twos = [jnp.zeros((1, C), f32) for _ in range(2)]
    for r, m, at in blocks():
        here = pl.ds(at, COLS)
        normed = (x_ref[here, :].astype(f32) - stat_ref[row(m), :]) * stat_ref[row(2 + m), :]
        a = normed * gain
        s = sigmoid(a)
        pre = acc[here, :] * (s * (1.0 + a * (1.0 - s)))
        gain_sum = gain_sum + jnp.sum(pre * normed, axis=0, keepdims=True)
        scaled = pre * gain
        acc[here, :] = scaled
        ones[m] = ones[m] + jnp.sum(scaled, axis=0, keepdims=True)
        twos[m] = twos[m] + jnp.sum(scaled * normed, axis=0, keepdims=True)
    gg_ref[...] = jnp.broadcast_to(gain_sum, (8, C))
    means = group_sums(jnp.concatenate(ones + twos, axis=0)) / GROUP_COUNT
    for m in range(2):
        here = pl.ds(pl.multiple_of(part * BAND + m * COLS, COLS), COLS)
        inv = stat_ref[row(2 + m), :]
        normed = (x_ref[here, :].astype(f32) - stat_ref[row(m), :]) * inv
        inner = inv * (acc[here, :] - means[m : m + 1] - normed * means[2 + m : 3 + m])
        mine = slice(m * COLS, (m + 1) * COLS)
        in_ref[mine, :] = (own_ref[mine, :] + inner).astype(bf16)


def input_call(part, x, cg, own, stat, gain, conv):
    smem = pl.BlockSpec(memory_space=pltpu.SMEM)
    vmem = pl.BlockSpec(memory_space=pltpu.VMEM)
    return pl.pallas_call(
        input_kernel,
        out_shape=(
            jax.ShapeDtypeStruct((BAND, C), bf16),
            jax.ShapeDtypeStruct((8, C), f32),
        ),
        in_specs=[smem] + [vmem] * 6,
        out_specs=[vmem] * 2,
        scratch_shapes=[
            pltpu.VMEM((TOK + 2 * BAND, 3 * C), bf16),
            pltpu.VMEM((TOK, C), f32),
        ],
        compiler_params=pltpu.CompilerParams(vmem_limit_bytes=40 * MIB),
        cost_estimate=pl.CostEstimate(
            flops=2 * TOK * 9 * C * C, bytes_accessed=9 * C * C * 2, transcendentals=TOK * C
        ),
        name="input",
    )(part, x, cg, own, stat, gain, conv)


def half_kernel(a_ref, gain_ref, out_ref, acc, mid):
    total = a_ref[0].astype(f32)
    for i in range(1, 8):
        total = total + a_ref[i].astype(f32)
    acc[...] = total
    mid[:, OWN * BLOCKS :, :] = jnp.zeros((8, CHUNK - OWN * BLOCKS, 128), f32)
    for i in range(8):
        for k in range(BLOCKS):
            mid[i, OWN * k : OWN * (k + 1), :] = acc[
                OWN * i : OWN * (i + 1), 128 * k : 128 * (k + 1)
            ]
        mid[i, OWN * BLOCKS : OWN * BLOCKS + 1, :] = gain_ref[i : i + 1, :]
    out_ref[...] = mid[...].astype(bf16)


def half_call(a, gains):
    vmem = pl.BlockSpec(memory_space=pltpu.VMEM)
    return pl.pallas_call(
        half_kernel,
        out_shape=jax.ShapeDtypeStruct((8, CHUNK, 128), bf16),
        in_specs=[vmem] * 2,
        out_specs=vmem,
        scratch_shapes=[
            pltpu.VMEM((80, WIDTH), f32),
            pltpu.VMEM((8, CHUNK, 128), f32),
        ],
        compiler_params=pltpu.CompilerParams(vmem_limit_bytes=32 * MIB),
        name="half",
    )(a, gains)


def total_kernel(a_ref, out_ref):
    total = a_ref[0].astype(f32)
    for i in range(1, 8):
        total = total + a_ref[i].astype(f32)
    out_ref[...] = total


def total_call(a):
    vmem = pl.BlockSpec(memory_space=pltpu.VMEM)
    return pl.pallas_call(
        total_kernel,
        out_shape=jax.ShapeDtypeStruct((CHUNK, 128), f32),
        in_specs=[vmem],
        out_specs=vmem,
        compiler_params=pltpu.CompilerParams(vmem_limit_bytes=16 * MIB),
        name="total",
    )(a)


def unpack(whole):
    rest = whole[:, : 5 * OWN].reshape(4, 5, OWN, 128)
    qkv = rest[:3].transpose(1, 3, 0, 2).reshape(C, 3 * OWN)
    out = rest[3].transpose(0, 2, 1).reshape(C, OWN)
    taps = whole[:, 5 * OWN : OWN * BLOCKS].reshape(4 * TAP_BLOCKS, OWN, 128)
    conv = taps[:45].reshape(3, 3, 5, OWN, 128).transpose(0, 1, 2, 4, 3).reshape(3, 3, C, OWN)
    tail = taps[45:].transpose(0, 2, 1).reshape(3 * 128, OWN)
    return conv, qkv, out, tail[:TDIM], whole[0, OWN * BLOCKS, :OWN], tail[TDIM]


def on_device(
    section_input,
    target,
    conv_weight,
    conv_bias,
    norm_gain,
    qkv_weight,
    out_weight,
    time_weight,
    timesteps,
    labels,
    ref_error,
):
    part = lax.axis_index(SPACE_AXES).astype(jnp.int32).reshape(1)
    x = lax.all_gather(section_input.reshape(BAND, C), SPACE_AXES, axis=0, tiled=True)
    t = lax.all_gather(target.reshape(BAND, C), SPACE_AXES, axis=0, tiled=True)
    conv = conv_weight.reshape(3, 3 * C, C)
    gain = norm_gain.reshape(1, C)
    wire, cg, own, stat, margin = pair_call(
        part,
        timesteps,
        labels,
        ref_error,
        x,
        t,
        conv,
        conv_bias.reshape(1, C),
        gain,
        qkv_weight,
        out_weight,
        time_weight,
    )
    moved = lax.all_to_all(wire.reshape(8, 80, WIDTH), ("x", "y_hi"), 0, 0)
    input_grad, gains = input_call(part, x, cg, own, stat, gain, conv)
    gains = lax.psum(gains[0], ("x", "y_hi")).reshape(4, 8, 2, OWN)
    gains = lax.dynamic_slice_in_dim(gains, lax.axis_index("x"), 1, 0)
    gains = lax.dynamic_slice_in_dim(gains, lax.axis_index("y_hi"), 1, 2).reshape(8, OWN)
    gains = jnp.pad(gains, ((0, 0), (0, 128 - OWN)))
    moved = lax.all_to_all(half_call(moved, gains), "z", 0, 0)
    whole = lax.all_gather(total_call(moved), SPACE_AXES, axis=0, tiled=False)
    conv_out, qkv_out, out_out, time_out, gain_out, bias_out = unpack(whole)
    pair_loss = jax.nn.softplus(BETA * margin[0, 0:1])
    return (
        input_grad.reshape(section_input.shape),
        conv_out,
        qkv_out,
        out_out,
        time_out,
        gain_out,
        bias_out,
        pair_loss,
    )


def solution(mesh):
    fine = Mesh(mesh.devices.reshape(MESH_SHAPE), MESH_AXES)
    pairs = P(PAIR_AXES)
    rows = P(PAIR_AXES, None, SPACE_AXES, None, None)
    return jax.shard_map(
        on_device,
        mesh=fine,
        in_specs=(rows, rows, P(), P(), P(), P(), P(), P(), pairs, pairs, pairs),
        out_specs=(
            rows,
            P(None, None, None, PAIR_AXES),
            P(None, PAIR_AXES),
            P(None, PAIR_AXES),
            P(None, PAIR_AXES),
            pairs,
            pairs,
            pairs,
        ),
        check_vma=False,
    )
```

profile of v0, /device:TPU:1, one launch (start us, length us, event | category | flops | bytes accessed | tf_op | source)
XLA Modules:
  0.0 165.0 jit_solution(16069646907305296361)
XLA Ops:
  1.9 1.3 reshape.75.gain_ref
  3.2 1.3 reshape.74.bias_ref
  4.5 10.9 %all_gather.12.x_ref = bf16[512,640]{1,0:T(8,128)(2,1)} all-gather(bf16[128,640]{1,0:T(8,128)(2,1)} %bitcast.59), channel_id=1, replica_groups=mesh['x'=4,'z'=8,'y_hi'=2,'y_lo'=2,'core'=2] {'y_lo','core'}, dimensions={0}, use_global_device_ids=true | all-gather | bytes 819200 | tf_op jit(solution)/shard_map/all_gather | solution.py:474
  15.4 9.8 %all_gather.13.t_ref = bf16[512,640]{1,0:T(8,128)(2,1)} all-gather(bf16[128,640]{1,0:T(8,128)(2,1)} %bitcast.60), channel_id=1, replica_groups=mesh['x'=4,'z'=8,'y_hi'=2,'y_lo'=2,'core'=2] {'y_lo','core'}, dimensions={0}, use_global_device_ids=true | all-gather | bytes 819200 | tf_op jit(solution)/shard_map/all_gather | solution.py:475
  25.1 30.7 %pair.1 = (bf16[640,2176]{1,0:T(8,128)(2,1)}, bf16[512,640]{1,0:T(8,128)(2,1)}, f32[128,640]{1,0:T(8,128)}, f32[8,640]{1,0:T(8,128)}, f32[8,128]{1,0:T(8,128)}) custom-call(s32[1]{0:T(128)} %bitcast.part_ref, s32[1]{0:T(128)S(6)} %copy.47.step_ref, s32[1]{0:T(128)S(6)} %copy.48.label_ref, f32[1,2]{1,0:T(1,128)} %error_ref.1, ...), custom_call_target="tpu_custom_call" | custom-call | tf_op jit(solution)/shard_map/pair/pallas_call | solution.py:284
  55.8 0.0 copy-start.1
  55.8 0.0 copy-start.2
  55.8 0.0 copy-start.5
  55.8 6.0 %all-to-all-start = ((bf16[8,80,2176]{2,1,0:T(8,128)(2,1)}), bf16[8,80,2176]{2,1,0:T(8,128)(2,1)S(1)}, u32[]{:S(2)}, u32[]{:S(2)}) async-start(bf16[8,80,2176]{2,1,0:T(8,128)(2,1)} %bitcast.47), calls=%async_computation | async-start | bytes 5570560 | tf_op jit(solution)/shard_map/all_to_all | solution.py:492
  61.8 0.0 copy-done.1
  61.8 0.0 copy-done.2
  61.8 0.0 copy-done.5
  61.8 0.0 copy-start
  61.8 3.1 %copy-done = bf16[3,3,640,640]{3,2,1,0:T(8,128)(2,1)S(1)} copy-done((bf16[3,3,640,640]{3,2,1,0:T(8,128)(2,1)S(1)}, bf16[3,3,640,640]{3,2,1,0:T(8,128)(2,1)}, u32[]{:S(2)}) %copy-start) | copy-done | bytes 7372824
  64.9 0.0 copy-start.3
  64.9 1.1 copy-done.3
  66.0 0.0 copy-start.4
  66.0 1.0 copy-done.4
  67.0 7.1 %input.1 = (bf16[128,640]{1,0:T(8,128)(2,1)}, f32[8,640]{1,0:T(8,128)S(1)}) custom-call(s32[1]{0:T(128)} %bitcast.part_ref, bf16[512,640]{1,0:T(8,128)(2,1)S(1)} %copy-done.1, bf16[512,640]{1,0:T(8,128)(2,1)S(1)} %copy-done.3, f32[128,640]{1,0:T(8,128)S(1)} %copy-done.4, f32[8,640]{1,0:T(8,128)S(1)} %copy-done.5, f32[1,640]{1,0:T(1,128)S(1)} %copy-done.2, ...), custom_call_target="tpu_custom_call" | custom-call | flops 3774873600 | bytes 7372800 | tf_op jit(solution)/shard_map/input/pallas_call | solution.py:380
  74.1 0.2 reshape.78
  74.3 51.1 %psum.7 = f32[4,8,2,10]{3,1,2,0:T(8,128)S(1)} all-reduce(f32[4,8,2,10]{3,1,2,0:T(8,128)S(1)} %copy.31), channel_id=1, replica_groups=mesh['x'=4,'z'=8,'y_hi'=2,'y_lo'=2,'core'=2] {'x','y_hi'}, use_global_device_ids=true, to_apply=%region_0.0 | all-reduce | flops 640 | bytes 5120 | tf_op jit(solution)/shard_map/psum | solution.py:494
  125.4 0.0 all-to-all-done.a_ref
  125.4 1.4 half.1
  126.8 8.2 %all-to-all-start.1 = ((bf16[8,176,128]{2,1,0:T(8,128)(2,1)}), bf16[8,176,128]{2,1,0:T(8,128)(2,1)S(1)}, u32[]{:S(2)}, u32[]{:S(2)}) async-start(bf16[8,176,128]{2,1,0:T(8,128)(2,1)} %half.1), calls=%async_computation.1 | async-start | bytes 720896 | tf_op jit(solution)/shard_map/all_to_all | solution.py:498
  135.0 1.2 slice.47
  136.9 8.4 %all-to-all-done.1.a_ref = bf16[8,176,128]{2,1,0:T(8,128)(2,1)S(1)} async-done(((bf16[8,176,128]{2,1,0:T(8,128)(2,1)}), bf16[8,176,128]{2,1,0:T(8,128)(2,1)S(1)}, u32[]{:S(2)}, u32[]{:S(2)}) %all-to-all-start.1) | async-done | bytes 360480 | tf_op jit(solution)/shard_map/all_to_all | solution.py:498
  145.4 14.7 %all-gather = f32[704,128]{1,0:T(8,128)S(1)} all-gather(f32[176,128]{1,0:T(8,128)S(1)} %total.1), channel_id=2, replica_groups=mesh['x'=4,'z'=8,'y_hi'=2,'y_lo'=2,'core'=2] {'y_lo','core'}, dimensions={0}, use_global_device_ids=true | all-gather | bytes 450560 | tf_op jit(solution)/shard_map/all_gather | solution.py:499
  160.1 0.5 slice_bitcast_fusion.1
  160.8 0.6 copy.41
  161.5 0.7 copy.40
  162.2 0.1 copy.33
  162.3 0.8 reshape.82
  163.1 0.0 copy-start.6
  163.1 0.7 slice_reduce_fusion
  163.8 0.0 copy-done.6
  (20 shorter events, 0.3 us)
Async XLA Ops:
  55.8 6.0 %copy-start.1 = (bf16[512,640]{1,0:T(8,128)(2,1)S(1)}, bf16[512,640]{1,0:T(8,128)(2,1)}, u32[]{:S(2)}) copy-start(bf16[512,640]{1,0:T(8,128)(2,1)} %all_gather.12.x_ref) | copy-start | bytes 1966084
  55.8 6.0 %copy-start.2 = (f32[1,640]{1,0:T(1,128)S(1)}, f32[1,640]{1,0:T(1,128)}, u32[]{:S(2)}) copy-start(f32[1,640]{1,0:T(1,128)} %reshape.75.gain_ref) | copy-start | bytes 7684
  55.8 6.0 %copy-start.5 = (f32[8,640]{1,0:T(8,128)S(1)}, f32[8,640]{1,0:T(8,128)}, u32[]{:S(2)}) copy-start(f32[8,640]{1,0:T(8,128)} %get-tuple-element.17.stat_ref) | copy-start | bytes 61444
  55.8 69.6 %all-to-all-start = ((bf16[8,80,2176]{2,1,0:T(8,128)(2,1)}), bf16[8,80,2176]{2,1,0:T(8,128)(2,1)S(1)}, u32[]{:S(2)}, u32[]{:S(2)}) async-start(bf16[8,80,2176]{2,1,0:T(8,128)(2,1)} %bitcast.47), calls=%async_computation | async-start | bytes 5570560 | tf_op jit(solution)/shard_map/all_to_all | solution.py:492
  61.8 3.1 %copy-start = (bf16[3,3,640,640]{3,2,1,0:T(8,128)(2,1)S(1)}, bf16[3,3,640,640]{3,2,1,0:T(8,128)(2,1)}, u32[]{:S(2)}) copy-start(bf16[3,3,640,640]{3,2,1,0:T(8,128)(2,1)} %param.15) | copy-start | bytes 22118404
  64.9 1.1 copy-start.3
  66.0 1.0 copy-start.4
  126.8 18.6 %all-to-all-start.1 = ((bf16[8,176,128]{2,1,0:T(8,128)(2,1)}), bf16[8,176,128]{2,1,0:T(8,128)(2,1)S(1)}, u32[]{:S(2)}, u32[]{:S(2)}) async-start(bf16[8,176,128]{2,1,0:T(8,128)(2,1)} %half.1), calls=%async_computation.1 | async-start | bytes 720896 | tf_op jit(solution)/shard_map/all_to_all | solution.py:498
  163.1 0.7 copy-start.6
where the time goes:
time: 166 us; the launch traced here: 165 us
  blocking collectives  86.4 us (52%)
  Pallas kernels  39.3 us (24%)
  starting transfers between devices  14.2 us (9%)
  local copies, waits for them, and re-layouts  12.7 us (8%)
  waiting for transfers between devices  8.45 us (5%)
  between operations  3.99 us (2%)
    psum x1, blocking collectives, on_device(): gains = lax.psum(gains[0], ('x', 'y_hi')).reshape(4, 8, 2, OWN)  51.1 us
    pallas_call x1, Pallas kernels, pair_call(): pl.pallas_call(pair_kernel, out_shape=(jax.ShapeDtypeStruct((C, WIDTH), b...  30.7 us
    all_gather x1, blocking collectives, on_device(): whole = lax.all_gather(total_call(moved), SPACE_AXES, axis=0, tiled=False)  14.7 us
    all_gather x1, blocking collectives, on_device(): lax.all_gather(section_input.reshape(BAND, C), SPACE_AXES, axis=0, tiled=...  10.9 us
    all_gather x1, blocking collectives, on_device(): t = lax.all_gather(target.reshape(BAND, C), SPACE_AXES, axis=0, tiled=True)  9.75 us
    all_to_all x1, waiting for transfers between devices, on_device(): moved = lax.all_to_all(half_call(moved, gains), 'z', 0, 0)  8.45 us
    all_to_all x1, starting transfers between devices, on_device(): moved = lax.all_to_all(half_call(moved, gains), 'z', 0, 0)  8.19 us
    pallas_call x1, Pallas kernels, input_call(): pl.pallas_call(input_kernel, out_shape=(jax.ShapeDtypeStruct((BAND, C), b...  7.11 us
  transfers between devices with their start and end apart: 2, of which 1 were waited for; matrix products, arithmetic and copies ran while one was open for 1% of the time, Pallas kernels for 4%

commit v1 on v0

--- a/solution.py
+++ b/solution.py
@@ -34,6 +34,7 @@
 WIDTH = BLOCKS * 128
 CHUNK = 176
 MIB = 1024 * 1024
+LIMIT = 40
 
 f32 = jnp.float32
 bf16 = jnp.bfloat16
@@ -47,19 +48,17 @@
     return lax.dot_general(a, b, dims, preferred_element_type=f32)
 
 
-def owner_columns():
-    n = np.arange(C)
-    x, y, z, j = n // 160, (n % 160) // 80, (n % 80) // OWN, n % OWN
-    owner = 16 * x + 2 * z + y
-    table = np.zeros((8, C), np.int32)
-    table[0] = 3 * OWN * owner + j
-    table[1] = OWN * owner + j
-    return table
-
-
 def frequencies():
     half = TDIM // 2
     return np.exp(-math.log(10000.0) * (np.arange(TDIM) % half) / half).astype(np.float32)[None]
+
+
+def wire_columns(step, width):
+    n = lax.broadcasted_iota(jnp.int32, (160, width), 0)
+    y = jnp.where(n >= 80, 1, 0)
+    rest = n - 80 * y
+    z = (rest * 6554) >> 16
+    return 2 * step * z + step * y + rest - OWN * z
 
 
 def row(i):
@@ -121,7 +120,6 @@
     outw_ref,
     timew_ref,
     freq_ref,
-    table_ref,
     wire_ref,
     cg_ref,
     own_ref,
@@ -138,6 +136,7 @@
     dattn,
     asel,
     feats_s,
+    turned,
 ):
     part = part_ref[0]
     sums, squares = [], []
@@ -154,7 +153,7 @@
     mean = moments[0:2]
     inv = lax.rsqrt(moments[2:4] - mean * mean + EPS)
     stat_ref[...] = jnp.concatenate([mean, inv, jnp.zeros((4, C), f32)], axis=0)
-    gain = gain_ref[...]
+    gain = gain_ref[...].reshape(1, C)
     acat[0:BAND, :] = jnp.zeros((BAND, 3 * C), bf16)
     acat[pl.ds(BAND + TOK, BAND), :] = jnp.zeros((BAND, 3 * C), bf16)
     for r, m, at in blocks():
@@ -170,9 +169,8 @@
     feats = jnp.where(lane < TDIM // 2, jnp.cos(angle), jnp.sin(angle))
     feats_s[...] = jnp.zeros((8, 384), f32)
     feats_s[0:1, 0:TDIM] = feats
-    feats_s[0:1, TDIM : TDIM + 1] = jnp.ones((1, 1), f32)
     shift = dot(jnp.broadcast_to(feats, (16, TDIM)).astype(bf16), timew_ref[...])[0:1]
-    offset = shift + bias_ref[...]
+    offset = shift + bias_ref[...].reshape(1, C)
     acc[...] = dot(acat[0:TOK, :], conv_ref[0])
     acc[...] += dot(acat[pl.ds(BAND, TOK), :], conv_ref[1])
     acc[...] += dot(acat[pl.ds(2 * BAND, TOK), :], conv_ref[2])
@@ -241,9 +239,12 @@
     acc[...] = out_grad.astype(f32) + dot(gall[:, 0 : 3 * C], qkvw_ref[...], NT)
     cg_ref[...] = acc[...].astype(bf16)
     own_ref[...] = acc[pl.ds(pl.multiple_of(part * BAND, BAND), BAND), :]
-    at_row = lax.broadcasted_iota(jnp.int32, (C, C), 0)
-    pick = jnp.where(at_row == table_ref[1:2, :], 1.0, 0.0).astype(bf16)
-    conv_grad = dot(cg_ref[...], pick).astype(bf16)
+    lane = lax.broadcasted_iota(jnp.int32, (160, 2 * IMG), 1)
+    own_cols = wire_columns(OWN, 2 * IMG)[:, 0:IMG]
+    for x in range(4):
+        low = 128 * x
+        pick = jnp.where(lane[:, 0:IMG] == own_cols + 32 * x, 1.0, 0.0).astype(bf16)
+        turned[160 * x : 160 * (x + 1), :] = dot(pick, cg_ref[:, low : low + IMG], NT).astype(bf16)
     for k in range(TAP_BLOCKS):
         place = part * TAP_BLOCKS + k
         cols = slice(k * 128, (k + 1) * 128)
@@ -263,19 +264,26 @@
                 f = feats_s[0:1, (k - 9) * 128 : (k - 8) * 128]
                 asel[:, cols] = jnp.broadcast_to(f, (TOK, 128)).astype(bf16)
 
-    wire_ref[:, C:] = dot(conv_grad, asel[...], TN).astype(bf16)
+    wire_ref[:, C:] = dot(turned[...], asel[...]).astype(bf16)
 
     @pl.when(part < 3)
     def _():
-        rows = lax.broadcasted_iota(jnp.int32, (3 * C, C), 0)
-        third = jnp.where(rows == table_ref[0:1, :] + OWN * part, 1.0, 0.0).astype(bf16)
-        g = dot(gall[:, 0 : 3 * C], third).astype(bf16)
-        wire_ref[:, 0:C] = dot(g, resid[...], TN).astype(bf16)
+        at = lax.broadcasted_iota(jnp.int32, (160, C), 1)
+        cols = wire_columns(3 * OWN, C) + OWN * part
+        for x, low in enumerate((0, 384, 896, 1280)):
+            pick = jnp.where(at == cols + (480 * x - low), 1.0, 0.0).astype(bf16)
+            turned[160 * x : 160 * (x + 1), :] = dot(pick, gall[:, low : low + C], NT).astype(bf16)
+        wire_ref[:, 0:C] = dot(turned[...], resid[...]).astype(bf16)
 
     @pl.when(part == 3)
     def _():
-        g = dot(gall[:, 3 * C : 4 * C], pick).astype(bf16)
-        wire_ref[:, 0:C] = dot(g, attended[...], TN).astype(bf16)
+        for x in range(4):
+            low = 3 * C + 128 * x
+            pick = jnp.where(lane[:, 0:IMG] == own_cols + 32 * x, 1.0, 0.0).astype(bf16)
+            turned[160 * x : 160 * (x + 1), :] = dot(pick, gall[:, low : low + IMG], NT).astype(
+                bf16
+            )
+        wire_ref[:, 0:C] = dot(turned[...], attended[...]).astype(bf16)
 
 
 def pair_call(part, steps, labels, errors, x, t, conv, bias, gain, qkvw, outw, timew):
@@ -290,7 +298,7 @@
             jax.ShapeDtypeStruct((8, C), f32),
             jax.ShapeDtypeStruct((8, 128), f32),
         ),
-        in_specs=[smem] * 4 + [vmem] * 10,
+        in_specs=[smem] * 4 + [vmem] * 9,
         out_specs=[vmem] * 5,
         scratch_shapes=[
             pltpu.VMEM((TOK + 2 * BAND, 3 * C), bf16),
@@ -304,8 +312,9 @@
             pltpu.VMEM((2, IMG, C), bf16),
             pltpu.VMEM((TOK, TAP_BLOCKS * 128), bf16),
             pltpu.VMEM((8, 384), f32),
+            pltpu.VMEM((C, TOK), bf16),
         ],
-        compiler_params=pltpu.CompilerParams(vmem_limit_bytes=56 * MIB),
+        compiler_params=pltpu.CompilerParams(vmem_limit_bytes=LIMIT * MIB),
         name="pair",
     )(
         part,
@@ -321,7 +330,6 @@
         outw,
         timew,
         frequencies(),
-        owner_columns(),
     )
 
 
@@ -348,7 +356,7 @@
                 acc[...] = term
             else:
                 acc[...] += term
-    gain = gain_ref[...]
+    gain = gain_ref[...].reshape(1, C)
     gain_sum = jnp.zeros((1, C), f32)
     ones = [jnp.zeros((1, C), f32) for _ in range(2)]
     twos = [jnp.zeros((1, C), f32) for _ in range(2)]
@@ -363,7 +371,8 @@
         acc[here, :] = scaled
         ones[m] = ones[m] + jnp.sum(scaled, axis=0, keepdims=True)
         twos[m] = twos[m] + jnp.sum(scaled * normed, axis=0, keepdims=True)
-    gg_ref[...] = jnp.broadcast_to(gain_sum, (8, C))
+    bias_sum = jnp.sum(cg_ref[...].astype(f32), axis=0, keepdims=True)
+    gg_ref[...] = jnp.concatenate([gain_sum, bias_sum], axis=0)
     means = group_sums(jnp.concatenate(ones + twos, axis=0)) / GROUP_COUNT
     for m in range(2):
         here = pl.ds(pl.multiple_of(part * BAND + m * COLS, COLS), COLS)
@@ -381,7 +390,7 @@
         input_kernel,
         out_shape=(
             jax.ShapeDtypeStruct((BAND, C), bf16),
-            jax.ShapeDtypeStruct((8, C), f32),
+            jax.ShapeDtypeStruct((2, C), f32),
         ),
         in_specs=[smem] + [vmem] * 6,
         out_specs=[vmem] * 2,
@@ -397,7 +406,7 @@
     )(part, x, cg, own, stat, gain, conv)
 
 
-def half_kernel(a_ref, gain_ref, out_ref, acc, mid):
+def half_kernel(a_ref, out_ref, acc, mid):
     total = a_ref[0].astype(f32)
     for i in range(1, 8):
         total = total + a_ref[i].astype(f32)
@@ -408,16 +417,15 @@
             mid[i, OWN * k : OWN * (k + 1), :] = acc[
                 OWN * i : OWN * (i + 1), 128 * k : 128 * (k + 1)
             ]
-        mid[i, OWN * BLOCKS : OWN * BLOCKS + 1, :] = gain_ref[i : i + 1, :]
     out_ref[...] = mid[...].astype(bf16)
 
 
-def half_call(a, gains):
+def half_call(a):
     vmem = pl.BlockSpec(memory_space=pltpu.VMEM)
     return pl.pallas_call(
         half_kernel,
         out_shape=jax.ShapeDtypeStruct((8, CHUNK, 128), bf16),
-        in_specs=[vmem] * 2,
+        in_specs=[vmem],
         out_specs=vmem,
         scratch_shapes=[
             pltpu.VMEM((80, WIDTH), f32),
@@ -425,7 +433,7 @@
         ],
         compiler_params=pltpu.CompilerParams(vmem_limit_bytes=32 * MIB),
         name="half",
-    )(a, gains)
+    )(a)
 
 
 def total_kernel(a_ref, out_ref):
@@ -447,14 +455,42 @@
     )(a)
 
 
-def unpack(whole):
-    rest = whole[:, : 5 * OWN].reshape(4, 5, OWN, 128)
-    qkv = rest[:3].transpose(1, 3, 0, 2).reshape(C, 3 * OWN)
-    out = rest[3].transpose(0, 2, 1).reshape(C, OWN)
-    taps = whole[:, 5 * OWN : OWN * BLOCKS].reshape(4 * TAP_BLOCKS, OWN, 128)
-    conv = taps[:45].reshape(3, 3, 5, OWN, 128).transpose(0, 1, 2, 4, 3).reshape(3, 3, C, OWN)
-    tail = taps[45:].transpose(0, 2, 1).reshape(3 * 128, OWN)
-    return conv, qkv, out, tail[:TDIM], whole[0, OWN * BLOCKS, :OWN], tail[TDIM]
+def unpack_kernel(all_ref, conv_ref, qkv_ref, out_ref, time_ref):
+    for part in range(4):
+        for k in range(5):
+            rows = all_ref[part, OWN * k : OWN * (k + 1), :]
+            cols = slice(128 * k, 128 * (k + 1))
+            if part < 3:
+                qkv_ref[OWN * part : OWN * (part + 1), cols] = rows
+            else:
+                out_ref[:, cols] = rows
+        for k in range(TAP_BLOCKS):
+            rows = all_ref[part, OWN * (5 + k) : OWN * (6 + k), :]
+            place = part * TAP_BLOCKS + k
+            tap, block = place // 5, place % 5
+            if place < 45:
+                conv_ref[tap // 3, :, tap % 3, 128 * block : 128 * (block + 1)] = rows
+            else:
+                wide = min(128, TDIM - 128 * (place - 45))
+                low = 128 * (place - 45)
+                time_ref[:, low : low + wide] = rows[:, 0:wide]
+
+
+def unpack_call(whole):
+    vmem = pl.BlockSpec(memory_space=pltpu.VMEM)
+    return pl.pallas_call(
+        unpack_kernel,
+        out_shape=(
+            jax.ShapeDtypeStruct((3, OWN, 3, C), f32),
+            jax.ShapeDtypeStruct((3 * OWN, C), f32),
+            jax.ShapeDtypeStruct((OWN, C), f32),
+            jax.ShapeDtypeStruct((OWN, TDIM), f32),
+        ),
+        in_specs=[vmem],
+        out_specs=[vmem] * 4,
+        compiler_params=pltpu.CompilerParams(vmem_limit_bytes=16 * MIB),
+        name="unpack",
+    )(whole)
 
 
 def on_device(
@@ -474,7 +510,6 @@
     x = lax.all_gather(section_input.reshape(BAND, C), SPACE_AXES, axis=0, tiled=True)
     t = lax.all_gather(target.reshape(BAND, C), SPACE_AXES, axis=0, tiled=True)
     conv = conv_weight.reshape(3, 3 * C, C)
-    gain = norm_gain.reshape(1, C)
     wire, cg, own, stat, margin = pair_call(
         part,
         timesteps,
@@ -483,30 +518,29 @@
         x,
         t,
         conv,
-        conv_bias.reshape(1, C),
-        gain,
+        conv_bias,
+        norm_gain,
         qkv_weight,
         out_weight,
         time_weight,
     )
     moved = lax.all_to_all(wire.reshape(8, 80, WIDTH), ("x", "y_hi"), 0, 0)
-    input_grad, gains = input_call(part, x, cg, own, stat, gain, conv)
-    gains = lax.psum(gains[0], ("x", "y_hi")).reshape(4, 8, 2, OWN)
-    gains = lax.dynamic_slice_in_dim(gains, lax.axis_index("x"), 1, 0)
-    gains = lax.dynamic_slice_in_dim(gains, lax.axis_index("y_hi"), 1, 2).reshape(8, OWN)
-    gains = jnp.pad(gains, ((0, 0), (0, 128 - OWN)))
-    moved = lax.all_to_all(half_call(moved, gains), "z", 0, 0)
+    input_grad, gains = input_call(part, x, cg, own, stat, norm_gain, conv)
+    gains = lax.psum(gains, "z")
+    moved = lax.all_to_all(half_call(moved), "z", 0, 0)
+    gains = lax.psum(gains, ("x", "y_hi"))
+    gains = lax.dynamic_slice_in_dim(gains, lax.axis_index(PAIR_AXES) * OWN, OWN, 1)
     whole = lax.all_gather(total_call(moved), SPACE_AXES, axis=0, tiled=False)
-    conv_out, qkv_out, out_out, time_out, gain_out, bias_out = unpack(whole)
+    conv_out, qkv_out, out_out, time_out = unpack_call(whole)
     pair_loss = jax.nn.softplus(BETA * margin[0, 0:1])
     return (
         input_grad.reshape(section_input.shape),
-        conv_out,
-        qkv_out,
-        out_out,
-        time_out,
-        gain_out,
-        bias_out,
+        conv_out.transpose(0, 2, 3, 1),
+        qkv_out.T,
+        out_out.T,
+        time_out.T,
+        gains[0],
+        gains[1],
         pair_loss,
     )
 

time: 166 us -> 174 us (1.048)
  waiting for transfers between devices: 8.45 us -> 39 us
  blocking collectives: 86.4 us -> 65.9 us
  Pallas kernels: 39.3 us -> 33.9 us
  local copies, waits for them, and re-layouts: 12.7 us -> 16.7 us
    all_to_all x1, waiting for transfers between devices: 0.01 us -> 39 us  [on_device(): moved = lax.all_to_all(wire.reshape(8, 80, WIDTH), ('x', 'y_hi'), 0, 0)]
    psum x1 -> x2, blocking collectives: 51.1 us -> 32.4 us  [the longest x1 18.8 us: on_device(): gains = lax.psum(gains, ('x', 'y_hi'))]
    unnamed x20 -> x30, local copies, waits for them, and re-layouts: 6.48 us -> 15.5 us
    all_to_all x1, waiting for transfers between devices: 8.45 us -> 0.01 us  [on_device(): moved = lax.all_to_all(half_call(moved), 'z', 0, 0)]
    pallas_call x1, Pallas kernels: 30.7 us -> 25.1 us  [pair_call(): pl.pallas_call(pair_kernel, out_shape=(jax.ShapeDtypeStruct((C, WIDTH), b...]
    reshape x7 -> x0, local copies, waits for them, and re-layouts: 3.56 us -> none  [the longest x1 1.27 us: on_device(): gain = norm_gain.reshape(1, C)]
where the time goes in v1:
time: 174 us; the launch traced here: 173 us
  blocking collectives  65.9 us (38%)
  waiting for transfers between devices  39 us (22%)
  Pallas kernels  33.9 us (19%)
  local copies, waits for them, and re-layouts  16.7 us (10%)
  starting transfers between devices  13.9 us (8%)
  between operations  3.89 us (2%)
    all_to_all x1, waiting for transfers between devices, on_device(): moved = lax.all_to_all(wire.reshape(8, 80, WIDTH), ('x', 'y_hi'), 0, 0)  39 us
    pallas_call x1, Pallas kernels, pair_call(): pl.pallas_call(pair_kernel, out_shape=(jax.ShapeDtypeStruct((C, WIDTH), b...  25.1 us
    psum x1, blocking collectives, on_device(): gains = lax.psum(gains, ('x', 'y_hi'))  18.8 us
    unnamed x30, local copies, waits for them, and re-layouts  15.5 us
    all_gather x1, blocking collectives, on_device(): whole = lax.all_gather(total_call(moved), SPACE_AXES, axis=0, tiled=False)  15.2 us
    psum x1, blocking collectives, on_device(): gains = lax.psum(gains, 'z')  13.6 us
    all_gather x1, blocking collectives, on_device(): lax.all_gather(section_input.reshape(BAND, C), SPACE_AXES, axis=0, tiled=...  10.2 us
    all_gather x1, blocking collectives, on_device(): t = lax.all_gather(target.reshape(BAND, C), SPACE_AXES, axis=0, tiled=True)  8.2 us
  transfers between devices with their start and end apart: 2, of which 1 were waited for; matrix products, arithmetic and copies ran while one was open for 1% of the time, Pallas kernels for 4%

profile of v1, /device:TPU:1, one launch (start us, length us, event | category | flops | bytes accessed | tf_op | source)
XLA Modules:
  0.0 173.3 jit_solution(6798692996032085947)
XLA Ops:
  1.9 10.2 %all_gather.12.x_ref = bf16[512,640]{1,0:T(8,128)(2,1)S(1)} all-gather(bf16[128,640]{1,0:T(8,128)(2,1)} %bitcast.22), channel_id=1, replica_groups=mesh['x'=4,'z'=8,'y_hi'=2,'y_lo'=2,'core'=2] {'y_lo','core'}, dimensions={0}, use_global_device_ids=true | all-gather | bytes 819200 | tf_op jit(solution)/shard_map/all_gather | solution.py:510
  12.1 8.2 %all_gather.13.t_ref = bf16[512,640]{1,0:T(8,128)(2,1)S(1)} all-gather(bf16[128,640]{1,0:T(8,128)(2,1)} %bitcast.23), channel_id=1, replica_groups=mesh['x'=4,'z'=8,'y_hi'=2,'y_lo'=2,'core'=2] {'y_lo','core'}, dimensions={0}, use_global_device_ids=true | all-gather | bytes 819200 | tf_op jit(solution)/shard_map/all_gather | solution.py:511
  20.3 0.0 copy-start.2
  20.3 1.7 copy-done.2
  22.0 0.0 copy-start.4
  22.0 1.1 copy-done.4
  23.1 0.0 copy-start.5
  23.1 1.0 copy-done.5
  24.1 0.0 copy-start.6
  24.1 0.7 copy-done.6
  24.8 0.0 copy-start.7
  24.8 0.7 copy-done.7
  25.5 0.0 copy-start.9
  25.5 0.7 copy-done.9
  26.2 0.0 copy-start.10
  26.2 0.7 copy-done.10
  26.9 25.1 %pair.1 = (bf16[640,2176]{1,0:T(8,128)(2,1)S(1)}, bf16[512,640]{1,0:T(8,128)(2,1)S(1)}, f32[128,640]{1,0:T(8,128)S(1)}, f32[8,640]{1,0:T(8,128)S(1)}, f32[8,128]{1,0:T(8,128)S(1)}) custom-call(s32[1]{0:T(128)} %bitcast.part_ref, s32[1]{0:T(128)S(6)} %copy.21.step_ref, s32[1]{0:T(128)S(6)} %copy.22.label_ref, f32[1,2]{1,0:T(1,128)S(1)} %copy-done.10, ...), custom_call_target="tpu_custom_call" | custom-call | tf_op jit(solution)/shard_map/pair/pallas_call | solution.py:292
  52.0 0.0 copy-start.1
  52.0 1.6 copy-done.1
  53.5 0.0 copy-start.11
  53.5 0.8 copy-done.11
  54.4 0.0 copy-start.13
  54.4 0.7 copy-done.13
  55.1 5.7 %all-to-all-start = ((bf16[8,80,2176]{2,1,0:T(8,128)(2,1)}), bf16[8,80,2176]{2,1,0:T(8,128)(2,1)S(1)}, u32[]{:S(2)}, u32[]{:S(2)}) async-start(bf16[8,80,2176]{2,1,0:T(8,128)(2,1)} %bitcast.20), calls=%async_computation | async-start | bytes 5570560 | tf_op jit(solution)/shard_map/all_to_all | solution.py:527
  60.8 0.0 copy-start.8
  60.8 0.5 slice.11
  62.1 39.0 %all-to-all-done.a_ref = bf16[8,80,2176]{2,1,0:T(8,128)(2,1)S(1)} async-done(((bf16[8,80,2176]{2,1,0:T(8,128)(2,1)}), bf16[8,80,2176]{2,1,0:T(8,128)(2,1)S(1)}, u32[]{:S(2)}, u32[]{:S(2)}) %all-to-all-start) | async-done | bytes 2785312 | tf_op jit(solution)/shard_map/all_to_all | solution.py:527
  101.1 0.7 half.1
  101.8 0.0 copy-start.3
  101.8 0.7 copy-done.3
  102.5 8.2 %all-to-all-start.1 = ((bf16[8,176,128]{2,1,0:T(8,128)(2,1)}), bf16[8,176,128]{2,1,0:T(8,128)(2,1)S(1)}, u32[]{:S(2)}, u32[]{:S(2)}) async-start(bf16[8,176,128]{2,1,0:T(8,128)(2,1)} %copy-done.3), calls=%async_computation.1 | async-start | bytes 720896 | tf_op jit(solution)/shard_map/all_to_all | solution.py:530
  110.7 0.0 copy-done.8
  110.7 0.0 copy-start
  110.7 3.1 %copy-done = bf16[3,3,640,640]{3,2,1,0:T(8,128)(2,1)S(1)} copy-done((bf16[3,3,640,640]{3,2,1,0:T(8,128)(2,1)S(1)}, bf16[3,3,640,640]{3,2,1,0:T(8,128)(2,1)}, u32[]{:S(2)}) %copy-start) | copy-done | bytes 7372824
  113.8 0.0 copy-start.12
  113.8 1.1 copy-done.12
  114.9 0.0 copy-start.14
  114.9 1.0 copy-done.14
  115.9 7.1 %input.1 = (bf16[128,640]{1,0:T(8,128)(2,1)}, f32[2,640]{1,0:T(2,128)S(1)}) custom-call(s32[1]{0:T(128)} %bitcast.part_ref, bf16[512,640]{1,0:T(8,128)(2,1)S(1)} %all_gather.12.x_ref, bf16[512,640]{1,0:T(8,128)(2,1)S(1)} %copy-done.12, f32[128,640]{1,0:T(8,128)S(1)} %copy-done.14, f32[8,640]{1,0:T(8,128)S(1)} %get-tuple-element.21.stat_ref, ...), custom_call_target="tpu_custom_call" | custom-call | flops 3774873600 | bytes 7372800 | tf_op jit(solution)/shard_map/input/pallas_call | solution.py:389
  123.0 13.6 %psum.14 = f32[2,640]{1,0:T(2,128)S(1)} all-reduce(f32[2,640]{1,0:T(2,128)S(1)} %get-tuple-element.28), channel_id=1, replica_groups=mesh['x'=4,'z'=8,'y_hi'=2,'y_lo'=2,'core'=2] {'z'}, use_global_device_ids=true, to_apply=%region_0.0 | all-reduce | flops 1280 | bytes 10240 | tf_op jit(solution)/shard_map/psum | solution.py:529
  136.6 18.8 %psum.15 = f32[2,640]{1,0:T(2,128)S(1)} all-reduce(f32[2,640]{1,0:T(2,128)S(1)} %psum.14), channel_id=1, replica_groups=mesh['x'=4,'z'=8,'y_hi'=2,'y_lo'=2,'core'=2] {'x','y_hi'}, use_global_device_ids=true, to_apply=%region_1.0 | all-reduce | flops 1280 | bytes 10240 | tf_op jit(solution)/shard_map/psum | solution.py:531
  155.4 0.1 constant_dynamic-slice_fusion
  155.5 0.5 slice_bitcast_fusion
  156.0 0.0 all-to-all-done.1.a_ref
  156.1 15.2 %all-gather = f32[704,128]{1,0:T(8,128)S(1)} all-gather(f32[176,128]{1,0:T(8,128)S(1)} %total.1), channel_id=2, replica_groups=mesh['x'=4,'z'=8,'y_hi'=2,'y_lo'=2,'core'=2] {'y_lo','core'}, dimensions={0}, use_global_device_ids=true | all-gather | bytes 450560 | tf_op jit(solution)/shard_map/all_gather | solution.py:533
  171.3 0.9 unpack.1
  (1 shorter events, 0.0 us)
Async XLA Ops:
  20.3 1.7 copy-start.2
  22.0 1.1 copy-start.4
  23.1 1.0 copy-start.5
  24.1 0.7 copy-start.6
  24.8 0.7 copy-start.7
  25.5 0.7 copy-start.9
  26.2 0.7 copy-start.10
  52.0 1.6 copy-start.1
  53.5 0.8 copy-start.11
  54.4 0.7 copy-start.13
  55.1 46.0 %all-to-all-start = ((bf16[8,80,2176]{2,1,0:T(8,128)(2,1)}), bf16[8,80,2176]{2,1,0:T(8,128)(2,1)S(1)}, u32[]{:S(2)}, u32[]{:S(2)}) async-start(bf16[8,80,2176]{2,1,0:T(8,128)(2,1)} %bitcast.20), calls=%async_computation | async-start | bytes 5570560 | tf_op jit(solution)/shard_map/all_to_all | solution.py:527
  60.8 49.9 %copy-start.8 = (f32[640]{0:T(1024)S(1)}, f32[640]{0:T(1024)}, u32[]{:S(2)}) copy-start(f32[640]{0:T(1024)} %gain_ref.3) | copy-start | bytes 7684
  101.8 0.7 copy-start.3
  102.5 53.5 %all-to-all-start.1 = ((bf16[8,176,128]{2,1,0:T(8,128)(2,1)}), bf16[8,176,128]{2,1,0:T(8,128)(2,1)S(1)}, u32[]{:S(2)}, u32[]{:S(2)}) async-start(bf16[8,176,128]{2,1,0:T(8,128)(2,1)} %copy-done.3), calls=%async_computation.1 | async-start | bytes 720896 | tf_op jit(solution)/shard_map/all_to_all | solution.py:530
  110.7 3.1 %copy-start = (bf16[3,3,640,640]{3,2,1,0:T(8,128)(2,1)S(1)}, bf16[3,3,640,640]{3,2,1,0:T(8,128)(2,1)}, u32[]{:S(2)}) copy-start(bf16[3,3,640,640]{3,2,1,0:T(8,128)(2,1)} %param.14) | copy-start | bytes 22118404
  113.8 1.1 copy-start.12
  114.9 1.0 copy-start.14

commit v2 on v1

--- a/solution.py
+++ b/solution.py
@@ -34,7 +34,7 @@
 WIDTH = BLOCKS * 128
 CHUNK = 176
 MIB = 1024 * 1024
-LIMIT = 40
+LIMIT = 56
 
 f32 = jnp.float32
 bf16 = jnp.bfloat16
@@ -137,8 +137,25 @@
     asel,
     feats_s,
     turned,
+    wire_s,
+    cg_s,
+    own_s,
+    t_s,
+    conv_s,
+    qkvw_s,
+    outw_s,
+    timew_s,
+    sems,
 ):
     part = part_ref[0]
+    taps = [pltpu.make_async_copy(conv_ref.at[i], conv_s.at[i], sems.at[i]) for i in range(3)]
+    load_time = pltpu.make_async_copy(timew_ref, timew_s, sems.at[3])
+    load_qkv = pltpu.make_async_copy(qkvw_ref, qkvw_s, sems.at[4])
+    load_out = pltpu.make_async_copy(outw_ref, outw_s, sems.at[5])
+    load_t = pltpu.make_async_copy(t_ref, t_s, sems.at[6])
+    taps[0].start()
+    load_time.start()
+    taps[1].start()
     sums, squares = [], []
     for m in range(2):
         total = jnp.zeros((1, C), f32)
@@ -169,15 +186,24 @@
     feats = jnp.where(lane < TDIM // 2, jnp.cos(angle), jnp.sin(angle))
     feats_s[...] = jnp.zeros((8, 384), f32)
     feats_s[0:1, 0:TDIM] = feats
-    shift = dot(jnp.broadcast_to(feats, (16, TDIM)).astype(bf16), timew_ref[...])[0:1]
+    load_time.wait()
+    shift = dot(jnp.broadcast_to(feats, (16, TDIM)).astype(bf16), timew_s[...])[0:1]
     offset = shift + bias_ref[...].reshape(1, C)
-    acc[...] = dot(acat[0:TOK, :], conv_ref[0])
-    acc[...] += dot(acat[pl.ds(BAND, TOK), :], conv_ref[1])
-    acc[...] += dot(acat[pl.ds(2 * BAND, TOK), :], conv_ref[2])
+    taps[0].wait()
+    taps[2].start()
+    load_qkv.start()
+    acc[...] = dot(acat[0:TOK, :], conv_s[0])
+    taps[1].wait()
+    acc[...] += dot(acat[pl.ds(BAND, TOK), :], conv_s[1])
+    taps[2].wait()
+    acc[...] += dot(acat[pl.ds(2 * BAND, TOK), :], conv_s[2])
     resid[...] = (x_ref[...].astype(f32) + acc[...] + offset).astype(bf16)
+    load_qkv.wait()
+    load_out.start()
+    load_t.start()
     for third in range(3):
         cols = pl.ds(third * C, C)
-        proj = dot(resid[...], qkvw_ref[:, cols]).astype(bf16)
+        proj = dot(resid[...], qkvw_s[:, cols]).astype(bf16)
         for r, m, at in blocks():
             qkv[m, pl.ds(r * COLS, COLS), cols] = proj[at : at + COLS]
     for m in range(2):
@@ -194,8 +220,10 @@
                 attended[pl.ds((2 * r + m) * COLS, COLS), pl.ds(h * 128, 128)] = joined[
                     r * COLS : (r + 1) * COLS
                 ]
+    load_out.wait()
+    load_t.wait()
     dev[...] = (
-        resid[...].astype(f32) + dot(attended[...], outw_ref[...]) - t_ref[...].astype(f32)
+        resid[...].astype(f32) + dot(attended[...], outw_s[...]) - t_s[...].astype(f32)
     )
     margin = jnp.zeros((1, 1), f32)
     signs = []
@@ -214,7 +242,7 @@
         here = pl.ds(at, COLS)
         gall[here, 3 * C : 4 * C] = (signs[m] * slope * dev[here, :]).astype(bf16)
     out_grad = gall[:, 3 * C : 4 * C]
-    da = dot(out_grad, outw_ref[...], NT).astype(bf16)
+    da = dot(out_grad, outw_s[...], NT).astype(bf16)
     for r, m, at in blocks():
         dattn[m, pl.ds(r * COLS, COLS), :] = da[at : at + COLS]
     for m in range(2):
@@ -236,15 +264,21 @@
                 gall[here, pl.ds(h * 128, 128)] = dq[rows]
                 gall[here, pl.ds(C + h * 128, 128)] = dk[rows]
                 gall[here, pl.ds(2 * C + h * 128, 128)] = dv[rows]
-    acc[...] = out_grad.astype(f32) + dot(gall[:, 0 : 3 * C], qkvw_ref[...], NT)
-    cg_ref[...] = acc[...].astype(bf16)
-    own_ref[...] = acc[pl.ds(pl.multiple_of(part * BAND, BAND), BAND), :]
+    acc[...] = out_grad.astype(f32) + dot(gall[:, 0 : 3 * C], qkvw_s[...], NT)
+    cg_s[...] = acc[...].astype(bf16)
+    own_s[...] = acc[pl.ds(pl.multiple_of(part * BAND, BAND), BAND), :]
+    stores = [
+        pltpu.make_async_copy(cg_s, cg_ref, sems.at[7]),
+        pltpu.make_async_copy(own_s, own_ref, sems.at[8]),
+    ]
+    for store in stores:
+        store.start()
     lane = lax.broadcasted_iota(jnp.int32, (160, 2 * IMG), 1)
     own_cols = wire_columns(OWN, 2 * IMG)[:, 0:IMG]
     for x in range(4):
         low = 128 * x
         pick = jnp.where(lane[:, 0:IMG] == own_cols + 32 * x, 1.0, 0.0).astype(bf16)
-        turned[160 * x : 160 * (x + 1), :] = dot(pick, cg_ref[:, low : low + IMG], NT).astype(bf16)
+        turned[160 * x : 160 * (x + 1), :] = dot(pick, cg_s[:, low : low + IMG], NT).astype(bf16)
     for k in range(TAP_BLOCKS):
         place = part * TAP_BLOCKS + k
         cols = slice(k * 128, (k + 1) * 128)
@@ -264,7 +298,12 @@
                 f = feats_s[0:1, (k - 9) * 128 : (k - 8) * 128]
                 asel[:, cols] = jnp.broadcast_to(f, (TOK, 128)).astype(bf16)
 
-    wire_ref[:, C:] = dot(turned[...], asel[...]).astype(bf16)
+    for i, low in enumerate((C, C + 768)):
+        cols = slice(low, low + 768)
+        wire_s[:, cols] = dot(turned[...], asel[:, low - C : low - C + 768]).astype(bf16)
+        store = pltpu.make_async_copy(wire_s.at[:, cols], wire_ref.at[:, cols], sems.at[9 + i])
+        store.start()
+        stores.append(store)
 
     @pl.when(part < 3)
     def _():
@@ -273,7 +312,7 @@
         for x, low in enumerate((0, 384, 896, 1280)):
             pick = jnp.where(at == cols + (480 * x - low), 1.0, 0.0).astype(bf16)
             turned[160 * x : 160 * (x + 1), :] = dot(pick, gall[:, low : low + C], NT).astype(bf16)
-        wire_ref[:, 0:C] = dot(turned[...], resid[...]).astype(bf16)
+        wire_s[:, 0:C] = dot(turned[...], resid[...]).astype(bf16)
 
     @pl.when(part == 3)
     def _():
@@ -283,12 +322,18 @@
             turned[160 * x : 160 * (x + 1), :] = dot(pick, gall[:, low : low + IMG], NT).astype(
                 bf16
             )
-        wire_ref[:, 0:C] = dot(turned[...], attended[...]).astype(bf16)
+        wire_s[:, 0:C] = dot(turned[...], attended[...]).astype(bf16)
+
+    store = pltpu.make_async_copy(wire_s.at[:, 0:C], wire_ref.at[:, 0:C], sems.at[11])
+    store.start()
+    for each in stores + [store]:
+        each.wait()
 
 
 def pair_call(part, steps, labels, errors, x, t, conv, bias, gain, qkvw, outw, timew):
     smem = pl.BlockSpec(memory_space=pltpu.SMEM)
     vmem = pl.BlockSpec(memory_space=pltpu.VMEM)
+    hbm = pl.BlockSpec(memory_space=pl.ANY)
     return pl.pallas_call(
         pair_kernel,
         out_shape=(
@@ -298,8 +343,8 @@
             jax.ShapeDtypeStruct((8, C), f32),
             jax.ShapeDtypeStruct((8, 128), f32),
         ),
-        in_specs=[smem] * 4 + [vmem] * 9,
-        out_specs=[vmem] * 5,
+        in_specs=[smem] * 4 + [vmem, hbm, hbm, vmem, vmem, hbm, hbm, hbm, vmem],
+        out_specs=[hbm] * 3 + [vmem] * 2,
         scratch_shapes=[
             pltpu.VMEM((TOK + 2 * BAND, 3 * C), bf16),
             pltpu.VMEM((TOK, C), f32),
@@ -313,6 +358,15 @@
             pltpu.VMEM((TOK, TAP_BLOCKS * 128), bf16),
             pltpu.VMEM((8, 384), f32),
             pltpu.VMEM((C, TOK), bf16),
+            pltpu.VMEM((C, WIDTH), bf16),
+            pltpu.VMEM((TOK, C), bf16),
+            pltpu.VMEM((BAND, C), f32),
+            pltpu.VMEM((TOK, C), bf16),
+            pltpu.VMEM((3, 3 * C, C), bf16),
+            pltpu.VMEM((C, 3 * C), bf16),
+            pltpu.VMEM((C, C), bf16),
+            pltpu.VMEM((TDIM, C), bf16),
+            pltpu.SemaphoreType.DMA((12,)),
         ],
         compiler_params=pltpu.CompilerParams(vmem_limit_bytes=LIMIT * MIB),
         name="pair",
@@ -527,6 +581,7 @@
     moved = lax.all_to_all(wire.reshape(8, 80, WIDTH), ("x", "y_hi"), 0, 0)
     input_grad, gains = input_call(part, x, cg, own, stat, norm_gain, conv)
     gains = lax.psum(gains, "z")
+    moved, gains = lax.optimization_barrier((moved, gains))
     moved = lax.all_to_all(half_call(moved), "z", 0, 0)
     gains = lax.psum(gains, ("x", "y_hi"))
     gains = lax.dynamic_slice_in_dim(gains, lax.axis_index(PAIR_AXES) * OWN, OWN, 1)

time: 174 us -> 142 us (0.82)
  waiting for transfers between devices: 39 us -> 10.3 us
  local copies, waits for them, and re-layouts: 16.7 us -> 6.96 us
  Pallas kernels: 33.9 us -> 37.6 us
  blocking collectives: 65.9 us -> 68.3 us
    all_to_all x1, waiting for transfers between devices: 39 us -> 10.3 us  [on_device(): moved = lax.all_to_all(wire.reshape(8, 80, WIDTH), ('x', 'y_hi'), 0, 0)]
    unnamed x30 -> x12, local copies, waits for them, and re-layouts: 15.5 us -> 5.16 us
    all_gather x1, blocking collectives: 15.2 us -> 11.1 us  [on_device(): whole = lax.all_gather(total_call(moved), SPACE_AXES, axis=0, tiled=False)]
    psum x1, blocking collectives: 13.6 us -> 17.6 us  [on_device(): gains = lax.psum(gains, 'z')]
    pallas_call x1, Pallas kernels: 25.1 us -> 28.1 us  [pair_call(): pl.pallas_call(pair_kernel, out_shape=(jax.ShapeDtypeStruct((C, WIDTH), b...]
  transfers between devices with their start and end apart: 2 -> 2, of which waited for: 1 -> 1; matrix products, arithmetic and copies ran while one was open for 1% -> 1% of each run, Pallas kernels for 4% -> 5%
where the time goes in v2:
time: 142 us; the launch traced here: 141 us
  blocking collectives  68.3 us (48%)
  Pallas kernels  37.6 us (26%)
  starting transfers between devices  14.2 us (10%)
  waiting for transfers between devices  10.3 us (7%)
  local copies, waits for them, and re-layouts  6.96 us (5%)
  between operations  3.9 us (3%)
    pallas_call x1, Pallas kernels, pair_call(): pl.pallas_call(pair_kernel, out_shape=(jax.ShapeDtypeStruct((C, WIDTH), b...  28.1 us
    psum x1, blocking collectives, on_device(): gains = lax.psum(gains, ('x', 'y_hi'))  18.9 us
    psum x1, blocking collectives, on_device(): gains = lax.psum(gains, 'z')  17.6 us
    all_gather x1, blocking collectives, on_device(): whole = lax.all_gather(total_call(moved), SPACE_AXES, axis=0, tiled=False)  11.1 us
    all_gather x1, blocking collectives, on_device(): lax.all_gather(section_input.reshape(BAND, C), SPACE_AXES, axis=0, tiled=...  10.9 us
    all_to_all x1, waiting for transfers between devices, on_device(): moved = lax.all_to_all(wire.reshape(8, 80, WIDTH), ('x', 'y_hi'), 0, 0)  10.3 us
    all_gather x1, blocking collectives, on_device(): t = lax.all_gather(target.reshape(BAND, C), SPACE_AXES, axis=0, tiled=True)  9.77 us
    all_to_all x1, starting transfers between devices, on_device(): moved = lax.all_to_all(half_call(moved), 'z', 0, 0)  8.19 us
  transfers between devices with their start and end apart: 2, of which 1 were waited for; matrix products, arithmetic and copies ran while one was open for 1% of the time, Pallas kernels for 5%

profile of v2, /device:TPU:1, one launch (start us, length us, event | category | flops | bytes accessed | tf_op | source)
XLA Modules:
  0.0 141.2 jit_solution(5259987126344876257)
XLA Ops:
  1.9 10.9 %all_gather.12.x_ref = bf16[512,640]{1,0:T(8,128)(2,1)} all-gather(bf16[128,640]{1,0:T(8,128)(2,1)} %bitcast.22), channel_id=1, replica_groups=mesh['x'=4,'z'=8,'y_hi'=2,'y_lo'=2,'core'=2] {'y_lo','core'}, dimensions={0}, use_global_device_ids=true | all-gather | bytes 819200 | tf_op jit(solution)/shard_map/all_gather | solution.py:564
  12.8 9.8 %all_gather.13.t_ref = bf16[512,640]{1,0:T(8,128)(2,1)} all-gather(bf16[128,640]{1,0:T(8,128)(2,1)} %bitcast.23), channel_id=1, replica_groups=mesh['x'=4,'z'=8,'y_hi'=2,'y_lo'=2,'core'=2] {'y_lo','core'}, dimensions={0}, use_global_device_ids=true | all-gather | bytes 819200 | tf_op jit(solution)/shard_map/all_gather | solution.py:565
  22.6 28.1 %pair.1 = (bf16[640,2176]{1,0:T(8,128)(2,1)}, bf16[512,640]{1,0:T(8,128)(2,1)}, f32[128,640]{1,0:T(8,128)}, f32[8,640]{1,0:T(8,128)}, f32[8,128]{1,0:T(8,128)}) custom-call(s32[1]{0:T(128)} %bitcast.part_ref, s32[1]{0:T(128)S(6)} %copy.21.step_ref, s32[1]{0:T(128)S(6)} %copy.22.label_ref, f32[1,2]{1,0:T(1,128)} %error_ref.1, ...), custom_call_target="tpu_custom_call" | custom-call | tf_op jit(solution)/shard_map/pair/pallas_call | solution.py:337
  50.7 0.0 copy-start.1
  50.7 0.0 copy-start.2
  50.7 0.0 copy-start.5
  50.7 6.0 %all-to-all-start = ((bf16[8,80,2176]{2,1,0:T(8,128)(2,1)}), bf16[8,80,2176]{2,1,0:T(8,128)(2,1)S(1)}, u32[]{:S(2)}, u32[]{:S(2)}) async-start(bf16[8,80,2176]{2,1,0:T(8,128)(2,1)} %bitcast.21), calls=%async_computation | async-start | bytes 5570560 | tf_op jit(solution)/shard_map/all_to_all | solution.py:581
  56.7 0.0 copy-done.1
  56.7 0.0 copy-done.2
  56.7 0.0 copy-done.5
  56.7 0.0 copy-start
  56.7 3.1 %copy-done = bf16[3,3,640,640]{3,2,1,0:T(8,128)(2,1)S(1)} copy-done((bf16[3,3,640,640]{3,2,1,0:T(8,128)(2,1)S(1)}, bf16[3,3,640,640]{3,2,1,0:T(8,128)(2,1)}, u32[]{:S(2)}) %copy-start) | copy-done | bytes 7372824
  59.8 0.0 copy-start.3
  59.8 1.1 copy-done.3
  60.9 0.0 copy-start.4
  60.9 1.0 copy-done.4
  61.9 7.1 %input.1 = (bf16[128,640]{1,0:T(8,128)(2,1)}, f32[2,640]{1,0:T(2,128)S(1)}) custom-call(s32[1]{0:T(128)} %bitcast.part_ref, bf16[512,640]{1,0:T(8,128)(2,1)S(1)} %copy-done.1, bf16[512,640]{1,0:T(8,128)(2,1)S(1)} %copy-done.3, f32[128,640]{1,0:T(8,128)S(1)} %copy-done.4, f32[8,640]{1,0:T(8,128)S(1)} %copy-done.5, f32[640]{0:T(1024)S(1)} %copy-done.2, ...), custom_call_target="tpu_custom_call" | custom-call | flops 3774873600 | bytes 7372800 | tf_op jit(solution)/shard_map/input/pallas_call | solution.py:443
  69.0 17.6 %psum.14 = f32[2,640]{1,0:T(2,128)S(1)} all-reduce(f32[2,640]{1,0:T(2,128)S(1)} %get-tuple-element.26), channel_id=1, replica_groups=mesh['x'=4,'z'=8,'y_hi'=2,'y_lo'=2,'core'=2] {'z'}, use_global_device_ids=true, to_apply=%region_0.0 | all-reduce | flops 1280 | bytes 10240 | tf_op jit(solution)/shard_map/psum | solution.py:583
  86.7 10.3 %all-to-all-done.a_ref = bf16[8,80,2176]{2,1,0:T(8,128)(2,1)S(1)} async-done(((bf16[8,80,2176]{2,1,0:T(8,128)(2,1)}), bf16[8,80,2176]{2,1,0:T(8,128)(2,1)S(1)}, u32[]{:S(2)}, u32[]{:S(2)}) %all-to-all-start) | async-done | bytes 2785312 | tf_op jit(solution)/shard_map/all_to_all | solution.py:581
  97.0 1.4 %half.1 = bf16[8,176,128]{2,1,0:T(8,128)(2,1)} custom-call(bf16[8,80,2176]{2,1,0:T(8,128)(2,1)S(1)} %all-to-all-done.a_ref), custom_call_target="tpu_custom_call" | custom-call | tf_op jit(solution)/shard_map/half/pallas_call | solution.py:479
  98.4 8.2 %all-to-all-start.1 = ((bf16[8,176,128]{2,1,0:T(8,128)(2,1)}), bf16[8,176,128]{2,1,0:T(8,128)(2,1)S(1)}, u32[]{:S(2)}, u32[]{:S(2)}) async-start(bf16[8,176,128]{2,1,0:T(8,128)(2,1)} %half.1), calls=%async_computation.1 | async-start | bytes 720896 | tf_op jit(solution)/shard_map/all_to_all | solution.py:585
  106.6 1.2 slice.11
  108.5 18.9 %psum.15 = f32[2,640]{1,0:T(2,128)S(1)} all-reduce(f32[2,640]{1,0:T(2,128)S(1)} %psum.14), channel_id=1, replica_groups=mesh['x'=4,'z'=8,'y_hi'=2,'y_lo'=2,'core'=2] {'x','y_hi'}, use_global_device_ids=true, to_apply=%region_1.0 | all-reduce | flops 1280 | bytes 10240 | tf_op jit(solution)/shard_map/psum | solution.py:586
  127.5 0.1 constant_dynamic-slice_fusion
  127.5 0.5 slice_bitcast_fusion
  128.1 0.0 all-to-all-done.1.a_ref
  128.1 11.1 %all-gather = f32[704,128]{1,0:T(8,128)S(1)} all-gather(f32[176,128]{1,0:T(8,128)S(1)} %total.1), channel_id=2, replica_groups=mesh['x'=4,'z'=8,'y_hi'=2,'y_lo'=2,'core'=2] {'y_lo','core'}, dimensions={0}, use_global_device_ids=true | all-gather | bytes 450560 | tf_op jit(solution)/shard_map/all_gather | solution.py:588
  139.2 0.9 unpack.1
  (1 shorter events, 0.0 us)
Async XLA Ops:
  50.7 6.0 %copy-start.1 = (bf16[512,640]{1,0:T(8,128)(2,1)S(1)}, bf16[512,640]{1,0:T(8,128)(2,1)}, u32[]{:S(2)}) copy-start(bf16[512,640]{1,0:T(8,128)(2,1)} %all_gather.12.x_ref) | copy-start | bytes 1966084
  50.7 6.0 %copy-start.2 = (f32[640]{0:T(1024)S(1)}, f32[640]{0:T(1024)}, u32[]{:S(2)}) copy-start(f32[640]{0:T(1024)} %gain_ref.3) | copy-start | bytes 7684
  50.7 6.0 %copy-start.5 = (f32[8,640]{1,0:T(8,128)S(1)}, f32[8,640]{1,0:T(8,128)}, u32[]{:S(2)}) copy-start(f32[8,640]{1,0:T(8,128)} %get-tuple-element.23.stat_ref) | copy-start | bytes 61444
  50.7 46.3 %all-to-all-start = ((bf16[8,80,2176]{2,1,0:T(8,128)(2,1)}), bf16[8,80,2176]{2,1,0:T(8,128)(2,1)S(1)}, u32[]{:S(2)}, u32[]{:S(2)}) async-start(bf16[8,80,2176]{2,1,0:T(8,128)(2,1)} %bitcast.21), calls=%async_computation | async-start | bytes 5570560 | tf_op jit(solution)/shard_map/all_to_all | solution.py:581
  56.7 3.1 %copy-start = (bf16[3,3,640,640]{3,2,1,0:T(8,128)(2,1)S(1)}, bf16[3,3,640,640]{3,2,1,0:T(8,128)(2,1)}, u32[]{:S(2)}) copy-start(bf16[3,3,640,640]{3,2,1,0:T(8,128)(2,1)} %param.14) | copy-start | bytes 22118404
  59.8 1.1 copy-start.3
  60.9 1.0 copy-start.4
  98.4 29.7 %all-to-all-start.1 = ((bf16[8,176,128]{2,1,0:T(8,128)(2,1)}), bf16[8,176,128]{2,1,0:T(8,128)(2,1)S(1)}, u32[]{:S(2)}, u32[]{:S(2)}) async-start(bf16[8,176,128]{2,1,0:T(8,128)(2,1)} %half.1), calls=%async_computation.1 | async-start | bytes 720896 | tf_op jit(solution)/shard_map/all_to_all | solution.py:585

commit v3 on v2

--- a/solution.py
+++ b/solution.py
@@ -111,8 +111,10 @@
     step_ref,
     label_ref,
     error_ref,
-    x_ref,
-    t_ref,
+    own_xt_ref,
+    y_xt_ref,
+    core_xt_ref,
+    far_xt_ref,
     conv_ref,
     bias_ref,
     gain_ref,
@@ -121,6 +123,7 @@
     timew_ref,
     freq_ref,
     wire_ref,
+    x_ref,
     cg_ref,
     own_ref,
     stat_ref,
@@ -140,6 +143,7 @@
     wire_s,
     cg_s,
     own_s,
+    x_s,
     t_s,
     conv_s,
     qkvw_s,
@@ -152,16 +156,31 @@
     load_time = pltpu.make_async_copy(timew_ref, timew_s, sems.at[3])
     load_qkv = pltpu.make_async_copy(qkvw_ref, qkvw_s, sems.at[4])
     load_out = pltpu.make_async_copy(outw_ref, outw_s, sems.at[5])
-    load_t = pltpu.make_async_copy(t_ref, t_s, sems.at[6])
+    load_x, load_t = [], []
+    for i, (ref, way) in enumerate(
+        ((own_xt_ref, 0), (core_xt_ref, 1), (y_xt_ref, 2), (far_xt_ref, 3))
+    ):
+        rows = pl.ds(pl.multiple_of((part ^ way) * BAND, BAND), BAND)
+        load_x.append(
+            pltpu.make_async_copy(ref.at[pl.ds(0, BAND)], x_s.at[rows], sems.at[12 + i])
+        )
+        load_t.append(
+            pltpu.make_async_copy(ref.at[pl.ds(BAND, BAND)], t_s.at[rows], sems.at[16 + i])
+        )
+    for load in load_x:
+        load.start()
     taps[0].start()
     load_time.start()
     taps[1].start()
+    for load in load_x:
+        load.wait()
+    stores = [pltpu.make_async_copy(x_s, x_ref, sems.at[6])]
     sums, squares = [], []
     for m in range(2):
         total = jnp.zeros((1, C), f32)
         square = jnp.zeros((1, C), f32)
         for r in range(ROWS):
-            v = x_ref[pl.ds((2 * r + m) * COLS, COLS), :].astype(f32)
+            v = x_s[pl.ds((2 * r + m) * COLS, COLS), :].astype(f32)
             total = total + jnp.sum(v, axis=0, keepdims=True)
             square = square + jnp.sum(v * v, axis=0, keepdims=True)
         sums.append(total)
@@ -174,7 +193,7 @@
     acat[0:BAND, :] = jnp.zeros((BAND, 3 * C), bf16)
     acat[pl.ds(BAND + TOK, BAND), :] = jnp.zeros((BAND, 3 * C), bf16)
     for r, m, at in blocks():
-        v = x_ref[pl.ds(at, COLS), :].astype(f32)
+        v = x_s[pl.ds(at, COLS), :].astype(f32)
         a = (v - mean[m : m + 1]) * inv[m : m + 1] * gain
         act = a * sigmoid(a)
         here = pl.ds(BAND + at, COLS)
@@ -192,15 +211,17 @@
     taps[0].wait()
     taps[2].start()
     load_qkv.start()
+    stores[0].start()
     acc[...] = dot(acat[0:TOK, :], conv_s[0])
     taps[1].wait()
     acc[...] += dot(acat[pl.ds(BAND, TOK), :], conv_s[1])
     taps[2].wait()
     acc[...] += dot(acat[pl.ds(2 * BAND, TOK), :], conv_s[2])
-    resid[...] = (x_ref[...].astype(f32) + acc[...] + offset).astype(bf16)
+    resid[...] = (x_s[...].astype(f32) + acc[...] + offset).astype(bf16)
     load_qkv.wait()
     load_out.start()
-    load_t.start()
+    for load in load_t:
+        load.start()
     for third in range(3):
         cols = pl.ds(third * C, C)
         proj = dot(resid[...], qkvw_s[:, cols]).astype(bf16)
@@ -221,7 +242,8 @@
                     r * COLS : (r + 1) * COLS
                 ]
     load_out.wait()
-    load_t.wait()
+    for load in load_t:
+        load.wait()
     dev[...] = (
         resid[...].astype(f32) + dot(attended[...], outw_s[...]) - t_s[...].astype(f32)
     )
@@ -267,11 +289,9 @@
     acc[...] = out_grad.astype(f32) + dot(gall[:, 0 : 3 * C], qkvw_s[...], NT)
     cg_s[...] = acc[...].astype(bf16)
     own_s[...] = acc[pl.ds(pl.multiple_of(part * BAND, BAND), BAND), :]
-    stores = [
-        pltpu.make_async_copy(cg_s, cg_ref, sems.at[7]),
-        pltpu.make_async_copy(own_s, own_ref, sems.at[8]),
-    ]
-    for store in stores:
+    stores.append(pltpu.make_async_copy(cg_s, cg_ref, sems.at[7]))
+    stores.append(pltpu.make_async_copy(own_s, own_ref, sems.at[8]))
+    for store in stores[1:]:
         store.start()
     lane = lax.broadcasted_iota(jnp.int32, (160, 2 * IMG), 1)
     own_cols = wire_columns(OWN, 2 * IMG)[:, 0:IMG]
@@ -330,7 +350,7 @@
         each.wait()
 
 
-def pair_call(part, steps, labels, errors, x, t, conv, bias, gain, qkvw, outw, timew):
+def pair_call(part, steps, labels, errors, own, near, core, far, conv, bias, gain, qkvw, outw, timew):
     smem = pl.BlockSpec(memory_space=pltpu.SMEM)
     vmem = pl.BlockSpec(memory_space=pltpu.VMEM)
     hbm = pl.BlockSpec(memory_space=pl.ANY)
@@ -339,12 +359,13 @@
         out_shape=(
             jax.ShapeDtypeStruct((C, WIDTH), bf16),
             jax.ShapeDtypeStruct((TOK, C), bf16),
+            jax.ShapeDtypeStruct((TOK, C), bf16),
             jax.ShapeDtypeStruct((BAND, C), f32),
             jax.ShapeDtypeStruct((8, C), f32),
             jax.ShapeDtypeStruct((8, 128), f32),
         ),
-        in_specs=[smem] * 4 + [vmem, hbm, hbm, vmem, vmem, hbm, hbm, hbm, vmem],
-        out_specs=[hbm] * 3 + [vmem] * 2,
+        in_specs=[smem] * 4 + [vmem] * 4 + [hbm] + [vmem] * 2 + [hbm] * 3 + [vmem],
+        out_specs=[hbm] * 4 + [vmem] * 2,
         scratch_shapes=[
             pltpu.VMEM((TOK + 2 * BAND, 3 * C), bf16),
             pltpu.VMEM((TOK, C), f32),
@@ -362,11 +383,12 @@
             pltpu.VMEM((TOK, C), bf16),
             pltpu.VMEM((BAND, C), f32),
             pltpu.VMEM((TOK, C), bf16),
+            pltpu.VMEM((TOK, C), bf16),
             pltpu.VMEM((3, 3 * C, C), bf16),
             pltpu.VMEM((C, 3 * C), bf16),
             pltpu.VMEM((C, C), bf16),
             pltpu.VMEM((TDIM, C), bf16),
-            pltpu.SemaphoreType.DMA((12,)),
+            pltpu.SemaphoreType.DMA((20,)),
         ],
         compiler_params=pltpu.CompilerParams(vmem_limit_bytes=LIMIT * MIB),
         name="pair",
@@ -375,8 +397,10 @@
         steps,
         labels,
         errors,
-        x,
-        t,
+        own,
+        near,
+        core,
+        far,
         conv,
         bias,
         gain,
@@ -561,16 +585,21 @@
     ref_error,
 ):
     part = lax.axis_index(SPACE_AXES).astype(jnp.int32).reshape(1)
-    x = lax.all_gather(section_input.reshape(BAND, C), SPACE_AXES, axis=0, tiled=True)
-    t = lax.all_gather(target.reshape(BAND, C), SPACE_AXES, axis=0, tiled=True)
+    swap = [(0, 1), (1, 0)]
+    own_xt = jnp.concatenate([section_input.reshape(BAND, C), target.reshape(BAND, C)], axis=0)
+    near = lax.ppermute(own_xt, "y_lo", swap)
+    core = lax.ppermute(own_xt, "core", swap)
+    far = lax.ppermute(near, "core", swap)
     conv = conv_weight.reshape(3, 3 * C, C)
-    wire, cg, own, stat, margin = pair_call(
+    wire, x, cg, own, stat, margin = pair_call(
         part,
         timesteps,
         labels,
         ref_error,
-        x,
-        t,
+        own_xt,
+        near,
+        core,
+        far,
         conv,
         conv_bias,
         norm_gain,
@@ -582,8 +611,11 @@
     input_grad, gains = input_call(part, x, cg, own, stat, norm_gain, conv)
     gains = lax.psum(gains, "z")
     moved, gains = lax.optimization_barrier((moved, gains))
-    moved = lax.all_to_all(half_call(moved), "z", 0, 0)
-    gains = lax.psum(gains, ("x", "y_hi"))
+    half, gains = lax.optimization_barrier((half_call(moved), gains))
+    moved = lax.all_to_all(half, "z", 0, 0)
+    gains = gains + lax.ppermute(gains, "y_hi", swap)
+    gains = gains + lax.ppermute(gains, "x", [(0, 1), (1, 0), (2, 3), (3, 2)])
+    gains = gains + lax.ppermute(gains, "x", [(0, 3), (3, 0), (1, 2), (2, 1)])
     gains = lax.dynamic_slice_in_dim(gains, lax.axis_index(PAIR_AXES) * OWN, OWN, 1)
     whole = lax.all_gather(total_call(moved), SPACE_AXES, axis=0, tiled=False)
     conv_out, qkv_out, out_out, time_out = unpack_call(whole)

time: 142 us -> 126 us (0.89)
  blocking collectives: 68.3 us -> 27.6 us
  waiting for transfers between devices: 10.3 us -> 21.6 us
  starting transfers between devices: 14.2 us -> 23.9 us
  Pallas kernels: 37.6 us -> 39.7 us
    all_gather x2 -> x0, blocking collectives: 20.7 us -> none  [the longest x1 10.9 us: on_device(): lax.all_gather(section_input.reshape(BAND, C), SPACE_AXES, axis=0, tiled=...]
    psum x1 -> x0, blocking collectives: 18.9 us -> none  [on_device(): gains = lax.psum(gains, ('x', 'y_hi'))]
    ppermute x0 -> x6, waiting for transfers between devices: none -> 10.9 us  [the longest x1 4.97 us: on_device(): near = lax.ppermute(own_xt, 'y_lo', swap)]
    ppermute x0 -> x6, starting transfers between devices: none -> 8.72 us  [the longest x1 2.48 us: on_device(): far = lax.ppermute(near, 'core', swap)]
    pallas_call x1, Pallas kernels: 28.1 us -> 30.2 us  [pair_call(): pl.pallas_call(pair_kernel, out_shape=(jax.ShapeDtypeStruct((C, WIDTH), b...]
    unnamed x12 -> x20, local copies, waits for them, and re-layouts: 5.16 us -> 5.98 us
  transfers between devices with their start and end apart: 2 -> 8, of which waited for: 1 -> 6; matrix products, arithmetic and copies ran while one was open for 1% -> 1% of each run, Pallas kernels for 5% -> 6%
where the time goes in v3:
time: 126 us
  Pallas kernels  39.7 us (32%)
  blocking collectives  27.6 us (22%)
  starting transfers between devices  23.9 us (19%)
  waiting for transfers between devices  21.6 us (17%)
  local copies, waits for them, and re-layouts  7.7 us (6%)
  between operations  3.96 us (3%)
    pallas_call x1, Pallas kernels, pair_call(): pl.pallas_call(pair_kernel, out_shape=(jax.ShapeDtypeStruct((C, WIDTH), b...  30.2 us
    psum x1, blocking collectives, on_device(): gains = lax.psum(gains, 'z')  17.6 us
    all_to_all x1, waiting for transfers between devices, on_device(): moved = lax.all_to_all(wire.reshape(8, 80, WIDTH), ('x', 'y_hi'), 0, 0)  10.3 us
    all_gather x1, blocking collectives, on_device(): whole = lax.all_gather(total_call(moved), SPACE_AXES, axis=0, tiled=False)  9.94 us
    all_to_all x1, starting transfers between devices, on_device(): moved = lax.all_to_all(half, 'z', 0, 0)  8.19 us
    pallas_call x1, Pallas kernels, input_call(): pl.pallas_call(input_kernel, out_shape=(jax.ShapeDtypeStruct((BAND, C), b...  7.15 us
    all_to_all x1, starting transfers between devices, on_device(): moved = lax.all_to_all(wire.reshape(8, 80, WIDTH), ('x', 'y_hi'), 0, 0)  6.95 us
    unnamed x20, local copies, waits for them, and re-layouts  5.98 us
  transfers between devices with their start and end apart: 8, of which 6 were waited for; matrix products, arithmetic and copies ran while one was open for 1% of the time, Pallas kernels for 6%

profile of v3, /device:TPU:1, one launch (start us, length us, event | category | flops | bytes accessed | tf_op | source)
XLA Modules:
  0.0 125.6 jit_solution(14285882281534291860)
XLA Ops:
  0.6 1.0 pad_maximum_fusion.own_xt_ref
  1.7 0.0 copy-start.6
  1.7 2.2 %collective-permute-start = (bf16[256,640]{1,0:T(8,128)(2,1)S(1)}, bf16[256,640]{1,0:T(8,128)(2,1)S(1)}, u32[]{:S(2)}, u32[]{:S(2)}) collective-permute-start(bf16[256,640]{1,0:T(8,128)(2,1)S(1)} %pad_maximum_fusion.own_xt_ref), channel_id=1, source_target_pairs={{0,2},{2,0},{1,3},{3,1},{4,6},{6,4},{5,7},{7,5},{8,10},{10,8},{9,1... | collective-permute-start | bytes 983048 | tf_op jit(solution)/shard_map/ppermute | solution.py:590
  3.9 1.2 collective-permute-start.1
  5.1 5.0 %collective-permute-done.y_xt_ref = bf16[256,640]{1,0:T(8,128)(2,1)S(1)} collective-permute-done((bf16[256,640]{1,0:T(8,128)(2,1)S(1)}, bf16[256,640]{1,0:T(8,128)(2,1)S(1)}, u32[]{:S(2)}, u32[]{:S(2)}) %collective-permute-start) | collective-permute-done | bytes 327712 | tf_op jit(solution)/shard_map/ppermute | solution.py:590
  10.1 0.0 copy-start.7
  10.1 2.5 %collective-permute-start.2 = (bf16[256,640]{1,0:T(8,128)(2,1)S(1)}, bf16[256,640]{1,0:T(8,128)(2,1)S(1)}, u32[]{:S(2)}, u32[]{:S(2)}) collective-permute-start(bf16[256,640]{1,0:T(8,128)(2,1)S(1)} %collective-permute-done.y_xt_ref), channel_id=1, source_target_pairs={{0,1},{1,0},{2,3},{3,2},{4,5},{5,4},{6,7},{7,6},{8,9},{9,8},{10,11... | collective-permute-start | bytes 983048 | tf_op jit(solution)/shard_map/ppermute | solution.py:592
  13.9 0.0 collective-permute-done.1.core_xt_ref
  13.9 0.0 copy-start.8
  13.9 0.0 collective-permute-done.2.far_xt_ref
  13.9 0.0 copy-start.9
  13.9 0.0 copy-done.6
  13.9 0.0 copy-done.7
  13.9 0.7 copy-done.8
  14.6 0.1 copy-done.9
  14.7 30.2 %pair.1 = (bf16[640,2176]{1,0:T(8,128)(2,1)}, bf16[512,640]{1,0:T(8,128)(2,1)}, bf16[512,640]{1,0:T(8,128)(2,1)}, f32[128,640]{1,0:T(8,128)}, f32[8,640]{1,0:T(8,128)}, /*index=5*/f32[8,128]{1,0:T(8,128)}) custom-call(s32[1]{0:T(128)} %bitcast.part_ref, s32[1]{0:T(128)S(6)} %copy.21.step_ref, s32[1]{0:T(128)S(6)} %copy.22.label_ref, f32[1,2]{1,0:T(1,128)} %error_ref.1, ...), custom_call_target="tpu_custom_call" | custom-call | tf_op jit(solution)/shard_map/pair/pallas_call | solution.py:357
  45.0 0.0 copy-start.1
  45.0 0.0 copy-start.2
  45.0 0.0 copy-start.5
  45.0 7.0 %all-to-all-start = ((bf16[8,80,2176]{2,1,0:T(8,128)(2,1)}), bf16[8,80,2176]{2,1,0:T(8,128)(2,1)S(1)}, u32[]{:S(2)}, u32[]{:S(2)}) async-start(bf16[8,80,2176]{2,1,0:T(8,128)(2,1)} %bitcast.21), calls=%async_computation | async-start | bytes 5570560 | tf_op jit(solution)/shard_map/all_to_all | solution.py:610
  51.9 0.0 copy-done.1
  51.9 0.0 copy-done.2
  52.0 0.0 copy-done.5
  52.0 0.0 copy-start
  52.0 3.1 %copy-done = bf16[3,3,640,640]{3,2,1,0:T(8,128)(2,1)S(1)} copy-done((bf16[3,3,640,640]{3,2,1,0:T(8,128)(2,1)S(1)}, bf16[3,3,640,640]{3,2,1,0:T(8,128)(2,1)}, u32[]{:S(2)}) %copy-start) | copy-done | bytes 7372824
  55.1 0.0 copy-start.3
  55.1 1.1 copy-done.3
  56.2 0.0 copy-start.4
  56.2 1.0 copy-done.4
  57.1 7.1 %input.1 = (bf16[128,640]{1,0:T(8,128)(2,1)}, f32[2,640]{1,0:T(2,128)S(1)}) custom-call(s32[1]{0:T(128)} %bitcast.part_ref, bf16[512,640]{1,0:T(8,128)(2,1)S(1)} %copy-done.2, bf16[512,640]{1,0:T(8,128)(2,1)S(1)} %copy-done.3, f32[128,640]{1,0:T(8,128)S(1)} %copy-done.4, f32[8,640]{1,0:T(8,128)S(1)} %copy-done.5, f32[640]{0:T(1024)S(1)} %copy-done.1, ...), custom_call_target="tpu_custom_call" | custom-call | flops 3774873600 | bytes 7372800 | tf_op jit(solution)/shard_map/input/pallas_call | solution.py:467
  64.3 17.6 %psum.7 = f32[2,640]{1,0:T(2,128)S(1)} all-reduce(f32[2,640]{1,0:T(2,128)S(1)} %get-tuple-element.30), channel_id=1, replica_groups=mesh['x'=4,'z'=8,'y_hi'=2,'y_lo'=2,'core'=2] {'z'}, use_global_device_ids=true, to_apply=%region_0.0 | all-reduce | flops 1280 | bytes 10240 | tf_op jit(solution)/shard_map/psum | solution.py:612
  81.9 10.3 %all-to-all-done.a_ref = bf16[8,80,2176]{2,1,0:T(8,128)(2,1)S(1)} async-done(((bf16[8,80,2176]{2,1,0:T(8,128)(2,1)}), bf16[8,80,2176]{2,1,0:T(8,128)(2,1)S(1)}, u32[]{:S(2)}, u32[]{:S(2)}) %all-to-all-start) | async-done | bytes 2785312 | tf_op jit(solution)/shard_map/all_to_all | solution.py:610
  92.2 1.4 %half.1 = bf16[8,176,128]{2,1,0:T(8,128)(2,1)} custom-call(bf16[8,80,2176]{2,1,0:T(8,128)(2,1)S(1)} %all-to-all-done.a_ref), custom_call_target="tpu_custom_call" | custom-call | tf_op jit(solution)/shard_map/half/pallas_call | solution.py:503
  93.6 8.2 %all-to-all-start.1 = ((bf16[8,176,128]{2,1,0:T(8,128)(2,1)}), bf16[8,176,128]{2,1,0:T(8,128)(2,1)S(1)}, u32[]{:S(2)}, u32[]{:S(2)}) async-start(bf16[8,176,128]{2,1,0:T(8,128)(2,1)} %half.1), calls=%async_computation.1 | async-start | bytes 720896 | tf_op jit(solution)/shard_map/all_to_all | solution.py:615
  101.8 2.2 %collective-permute-start.3 = (f32[2,640]{1,0:T(2,128)S(1)}, f32[2,640]{1,0:T(2,128)S(1)}, u32[]{:S(2)}, u32[]{:S(2)}) collective-permute-start(f32[2,640]{1,0:T(2,128)S(1)} %psum.7), channel_id=1, source_target_pairs={{0,4},{4,0},{1,5},{5,1},{2,6},{6,2},{3,7},{7,3},{8,12},{12,8},{9,1... | collective-permute-start | bytes 15368 | tf_op jit(solution)/shard_map/ppermute | solution.py:616
  104.0 1.8 %collective-permute-done.3 = f32[2,640]{1,0:T(2,128)S(1)} collective-permute-done((f32[2,640]{1,0:T(2,128)S(1)}, f32[2,640]{1,0:T(2,128)S(1)}, u32[]{:S(2)}, u32[]{:S(2)}) %collective-permute-start.3) | collective-permute-done | bytes 5152 | tf_op jit(solution)/shard_map/ppermute | solution.py:616
  105.8 0.0 collective-permute-start.4
  105.8 2.8 %collective-permute-done.4 = f32[2,640]{1,0:T(2,128)S(1)} collective-permute-done((f32[2,640]{1,0:T(2,128)S(1)}, f32[2,640]{1,0:T(2,128)S(1)}, u32[]{:S(2)}, u32[]{:S(2)}) %collective-permute-start.4) | collective-permute-done | bytes 5152 | tf_op jit(solution)/shard_map/ppermute | solution.py:617
  108.6 0.6 collective-permute-start.5
  109.2 1.2 slice.11
  111.1 1.4 %collective-permute-done.5 = f32[2,640]{1,0:T(2,128)S(1)} collective-permute-done((f32[2,640]{1,0:T(2,128)S(1)}, f32[2,640]{1,0:T(2,128)S(1)}, u32[]{:S(2)}, u32[]{:S(2)}) %collective-permute-start.5) | collective-permute-done | bytes 5152 | tf_op jit(solution)/shard_map/ppermute | solution.py:618
  112.5 0.1 dynamic-slice_add_fusion
  112.6 0.5 slice_bitcast_fusion
  113.1 0.4 all-to-all-done.1.a_ref
  113.6 9.9 %all-gather = f32[704,128]{1,0:T(8,128)S(1)} all-gather(f32[176,128]{1,0:T(8,128)S(1)} %total.1), channel_id=2, replica_groups=mesh['x'=4,'z'=8,'y_hi'=2,'y_lo'=2,'core'=2] {'y_lo','core'}, dimensions={0}, use_global_device_ids=true | all-gather | bytes 450560 | tf_op jit(solution)/shard_map/all_gather | solution.py:620
  123.6 0.9 unpack.1
  (3 shorter events, 0.1 us)
Async XLA Ops:
  1.7 12.2 %copy-start.6 = (bf16[256,640]{1,0:T(8,128)(2,1)}, bf16[256,640]{1,0:T(8,128)(2,1)S(1)}, u32[]{:S(2)}) copy-start(bf16[256,640]{1,0:T(8,128)(2,1)S(1)} %pad_maximum_fusion.own_xt_ref) | copy-start | bytes 983044
  1.7 8.4 %collective-permute-start = (bf16[256,640]{1,0:T(8,128)(2,1)S(1)}, bf16[256,640]{1,0:T(8,128)(2,1)S(1)}, u32[]{:S(2)}, u32[]{:S(2)}) collective-permute-start(bf16[256,640]{1,0:T(8,128)(2,1)S(1)} %pad_maximum_fusion.own_xt_ref), channel_id=1, source_target_pairs={{0,2},{2,0},{1,3},{3,1},{4,6},{6,4},{5,7},{7,5},{8,10},{10,8},{9,1... | collective-permute-start | bytes 983048 | tf_op jit(solution)/shard_map/ppermute | solution.py:590
  3.9 10.0 %collective-permute-start.1 = (bf16[256,640]{1,0:T(8,128)(2,1)S(1)}, bf16[256,640]{1,0:T(8,128)(2,1)S(1)}, u32[]{:S(2)}, u32[]{:S(2)}) collective-permute-start(bf16[256,640]{1,0:T(8,128)(2,1)S(1)} %pad_maximum_fusion.own_xt_ref), channel_id=1, source_target_pairs={{0,1},{1,0},{2,3},{3,2},{4,5},{5,4},{6,7},{7,6},{8,9},{9,8},{10,11... | collective-permute-start | bytes 983048 | tf_op jit(solution)/shard_map/ppermute | solution.py:591
  10.1 3.8 %copy-start.7 = (bf16[256,640]{1,0:T(8,128)(2,1)}, bf16[256,640]{1,0:T(8,128)(2,1)S(1)}, u32[]{:S(2)}) copy-start(bf16[256,640]{1,0:T(8,128)(2,1)S(1)} %collective-permute-done.y_xt_ref) | copy-start | bytes 983044
  10.1 3.8 %collective-permute-start.2 = (bf16[256,640]{1,0:T(8,128)(2,1)S(1)}, bf16[256,640]{1,0:T(8,128)(2,1)S(1)}, u32[]{:S(2)}, u32[]{:S(2)}) collective-permute-start(bf16[256,640]{1,0:T(8,128)(2,1)S(1)} %collective-permute-done.y_xt_ref), channel_id=1, source_target_pairs={{0,1},{1,0},{2,3},{3,2},{4,5},{5,4},{6,7},{7,6},{8,9},{9,8},{10,11... | collective-permute-start | bytes 983048 | tf_op jit(solution)/shard_map/ppermute | solution.py:592
  13.9 0.7 copy-start.8
  13.9 0.8 copy-start.9
  45.0 7.0 %copy-start.1 = (f32[640]{0:T(1024)S(1)}, f32[640]{0:T(1024)}, u32[]{:S(2)}) copy-start(f32[640]{0:T(1024)} %gain_ref.3) | copy-start | bytes 7684
  45.0 7.0 %copy-start.2 = (bf16[512,640]{1,0:T(8,128)(2,1)S(1)}, bf16[512,640]{1,0:T(8,128)(2,1)}, u32[]{:S(2)}) copy-start(bf16[512,640]{1,0:T(8,128)(2,1)} %get-tuple-element.24.x_ref) | copy-start | bytes 1966084
  45.0 7.0 %copy-start.5 = (f32[8,640]{1,0:T(8,128)S(1)}, f32[8,640]{1,0:T(8,128)}, u32[]{:S(2)}) copy-start(f32[8,640]{1,0:T(8,128)} %get-tuple-element.27.stat_ref) | copy-start | bytes 61444
  45.0 47.2 %all-to-all-start = ((bf16[8,80,2176]{2,1,0:T(8,128)(2,1)}), bf16[8,80,2176]{2,1,0:T(8,128)(2,1)S(1)}, u32[]{:S(2)}, u32[]{:S(2)}) async-start(bf16[8,80,2176]{2,1,0:T(8,128)(2,1)} %bitcast.21), calls=%async_computation | async-start | bytes 5570560 | tf_op jit(solution)/shard_map/all_to_all | solution.py:610
  52.0 3.1 %copy-start = (bf16[3,3,640,640]{3,2,1,0:T(8,128)(2,1)S(1)}, bf16[3,3,640,640]{3,2,1,0:T(8,128)(2,1)}, u32[]{:S(2)}) copy-start(bf16[3,3,640,640]{3,2,1,0:T(8,128)(2,1)} %param.14) | copy-start | bytes 22118404
  55.1 1.1 copy-start.3
  56.2 1.0 copy-start.4
  93.6 19.9 %all-to-all-start.1 = ((bf16[8,176,128]{2,1,0:T(8,128)(2,1)}), bf16[8,176,128]{2,1,0:T(8,128)(2,1)S(1)}, u32[]{:S(2)}, u32[]{:S(2)}) async-start(bf16[8,176,128]{2,1,0:T(8,128)(2,1)} %half.1), calls=%async_computation.1 | async-start | bytes 720896 | tf_op jit(solution)/shard_map/all_to_all | solution.py:615
  101.8 4.0 %collective-permute-start.3 = (f32[2,640]{1,0:T(2,128)S(1)}, f32[2,640]{1,0:T(2,128)S(1)}, u32[]{:S(2)}, u32[]{:S(2)}) collective-permute-start(f32[2,640]{1,0:T(2,128)S(1)} %psum.7), channel_id=1, source_target_pairs={{0,4},{4,0},{1,5},{5,1},{2,6},{6,2},{3,7},{7,3},{8,12},{12,8},{9,1... | collective-permute-start | bytes 15368 | tf_op jit(solution)/shard_map/ppermute | solution.py:616
  105.8 2.8 %collective-permute-start.4 = (f32[2,640]{1,0:T(2,128)S(1)}, f32[2,640]{1,0:T(2,128)S(1)}, u32[]{:S(2)}, u32[]{:S(2)}) collective-permute-start(f32[2,640]{1,0:T(2,128)S(1)} %add.28), channel_id=1, source_target_pairs={{0,64},{64,0},{128,192},{192,128},{1,65},{65,1},{129,193},{193,129... | collective-permute-start | bytes 15368 | tf_op jit(solution)/shard_map/ppermute | solution.py:617
  108.6 4.0 %collective-permute-start.5 = (f32[2,640]{1,0:T(2,128)S(1)}, f32[2,640]{1,0:T(2,128)S(1)}, u32[]{:S(2)}, u32[]{:S(2)}) collective-permute-start(f32[2,640]{1,0:T(2,128)S(1)} %add.29), channel_id=1, source_target_pairs={{0,192},{192,0},{64,128},{128,64},{1,193},{193,1},{65,129},{129,65... | collective-permute-start | bytes 15368 | tf_op jit(solution)/shard_map/ppermute | solution.py:618

commit v4 on v3

--- a/solution.py
+++ b/solution.py
@@ -30,9 +30,10 @@
 MESH_SHAPE = (4, 8, 2, 2, 2)
 OWN = C // 64
 TAP_BLOCKS = 12
-BLOCKS = 5 + TAP_BLOCKS
-WIDTH = BLOCKS * 128
+WIDTH = TAP_BLOCKS * 128
+TAP_ROWS = OWN * TAP_BLOCKS
 CHUNK = 176
+SIDE = C + 128
 MIB = 1024 * 1024
 LIMIT = 56
 
@@ -124,6 +125,8 @@
     freq_ref,
     wire_ref,
     x_ref,
+    gall_ref,
+    side_ref,
     cg_ref,
     own_ref,
     stat_ref,
@@ -145,6 +148,7 @@
     own_s,
     x_s,
     t_s,
+    side_s,
     conv_s,
     qkvw_s,
     outw_s,
@@ -156,24 +160,13 @@
     load_time = pltpu.make_async_copy(timew_ref, timew_s, sems.at[3])
     load_qkv = pltpu.make_async_copy(qkvw_ref, qkvw_s, sems.at[4])
     load_out = pltpu.make_async_copy(outw_ref, outw_s, sems.at[5])
-    load_x, load_t = [], []
-    for i, (ref, way) in enumerate(
-        ((own_xt_ref, 0), (core_xt_ref, 1), (y_xt_ref, 2), (far_xt_ref, 3))
-    ):
-        rows = pl.ds(pl.multiple_of((part ^ way) * BAND, BAND), BAND)
-        load_x.append(
-            pltpu.make_async_copy(ref.at[pl.ds(0, BAND)], x_s.at[rows], sems.at[12 + i])
-        )
-        load_t.append(
-            pltpu.make_async_copy(ref.at[pl.ds(BAND, BAND)], t_s.at[rows], sems.at[16 + i])
-        )
-    for load in load_x:
-        load.start()
     taps[0].start()
     load_time.start()
     taps[1].start()
-    for load in load_x:
-        load.wait()
+    for ref, way in ((own_xt_ref, 0), (core_xt_ref, 1), (y_xt_ref, 2), (far_xt_ref, 3)):
+        rows = pl.ds(pl.multiple_of((part ^ way) * BAND, BAND), BAND)
+        x_s[rows, :] = ref[0:BAND, :]
+        t_s[rows, :] = ref[BAND : 2 * BAND, :]
     stores = [pltpu.make_async_copy(x_s, x_ref, sems.at[6])]
     sums, squares = [], []
     for m in range(2):
@@ -220,8 +213,6 @@
     resid[...] = (x_s[...].astype(f32) + acc[...] + offset).astype(bf16)
     load_qkv.wait()
     load_out.start()
-    for load in load_t:
-        load.start()
     for third in range(3):
         cols = pl.ds(third * C, C)
         proj = dot(resid[...], qkvw_s[:, cols]).astype(bf16)
@@ -242,11 +233,12 @@
                     r * COLS : (r + 1) * COLS
                 ]
     load_out.wait()
-    for load in load_t:
-        load.wait()
     dev[...] = (
         resid[...].astype(f32) + dot(attended[...], outw_s[...]) - t_s[...].astype(f32)
     )
+    side_s[...] = jnp.where(part == 3, attended[...], resid[...])
+    stores.append(pltpu.make_async_copy(side_s, side_ref, sems.at[12]))
+    stores[1].start()
     margin = jnp.zeros((1, 1), f32)
     signs = []
     for m in range(2):
@@ -286,12 +278,14 @@
                 gall[here, pl.ds(h * 128, 128)] = dq[rows]
                 gall[here, pl.ds(C + h * 128, 128)] = dk[rows]
                 gall[here, pl.ds(2 * C + h * 128, 128)] = dv[rows]
+    stores.append(pltpu.make_async_copy(gall, gall_ref, sems.at[13]))
+    stores[2].start()
     acc[...] = out_grad.astype(f32) + dot(gall[:, 0 : 3 * C], qkvw_s[...], NT)
     cg_s[...] = acc[...].astype(bf16)
     own_s[...] = acc[pl.ds(pl.multiple_of(part * BAND, BAND), BAND), :]
     stores.append(pltpu.make_async_copy(cg_s, cg_ref, sems.at[7]))
     stores.append(pltpu.make_async_copy(own_s, own_ref, sems.at[8]))
-    for store in stores[1:]:
+    for store in stores[3:]:
         store.start()
     lane = lax.broadcasted_iota(jnp.int32, (160, 2 * IMG), 1)
     own_cols = wire_columns(OWN, 2 * IMG)[:, 0:IMG]
@@ -318,36 +312,14 @@
                 f = feats_s[0:1, (k - 9) * 128 : (k - 8) * 128]
                 asel[:, cols] = jnp.broadcast_to(f, (TOK, 128)).astype(bf16)
 
-    for i, low in enumerate((C, C + 768)):
+    for i, low in enumerate((0, 768)):
         cols = slice(low, low + 768)
-        wire_s[:, cols] = dot(turned[...], asel[:, low - C : low - C + 768]).astype(bf16)
+        wire_s[:, cols] = dot(turned[...], asel[:, cols]).astype(bf16)
         store = pltpu.make_async_copy(wire_s.at[:, cols], wire_ref.at[:, cols], sems.at[9 + i])
         store.start()
         stores.append(store)
-
-    @pl.when(part < 3)
-    def _():
-        at = lax.broadcasted_iota(jnp.int32, (160, C), 1)
-        cols = wire_columns(3 * OWN, C) + OWN * part
-        for x, low in enumerate((0, 384, 896, 1280)):
-            pick = jnp.where(at == cols + (480 * x - low), 1.0, 0.0).astype(bf16)
-            turned[160 * x : 160 * (x + 1), :] = dot(pick, gall[:, low : low + C], NT).astype(bf16)
-        wire_s[:, 0:C] = dot(turned[...], resid[...]).astype(bf16)
-
-    @pl.when(part == 3)
-    def _():
-        for x in range(4):
-            low = 3 * C + 128 * x
-            pick = jnp.where(lane[:, 0:IMG] == own_cols + 32 * x, 1.0, 0.0).astype(bf16)
-            turned[160 * x : 160 * (x + 1), :] = dot(pick, gall[:, low : low + IMG], NT).astype(
-                bf16
-            )
-        wire_s[:, 0:C] = dot(turned[...], attended[...]).astype(bf16)
-
-    store = pltpu.make_async_copy(wire_s.at[:, 0:C], wire_ref.at[:, 0:C], sems.at[11])
-    store.start()
-    for each in stores + [store]:
-        each.wait()
+    for store in stores:
+        store.wait()
 
 
 def pair_call(part, steps, labels, errors, own, near, core, far, conv, bias, gain, qkvw, outw, timew):
@@ -359,13 +331,15 @@
         out_shape=(
             jax.ShapeDtypeStruct((C, WIDTH), bf16),
             jax.ShapeDtypeStruct((TOK, C), bf16),
+            jax.ShapeDtypeStruct((TOK, 4 * C), bf16),
+            jax.ShapeDtypeStruct((TOK, C), bf16),
             jax.ShapeDtypeStruct((TOK, C), bf16),
             jax.ShapeDtypeStruct((BAND, C), f32),
             jax.ShapeDtypeStruct((8, C), f32),
             jax.ShapeDtypeStruct((8, 128), f32),
         ),
         in_specs=[smem] * 4 + [vmem] * 4 + [hbm] + [vmem] * 2 + [hbm] * 3 + [vmem],
-        out_specs=[hbm] * 4 + [vmem] * 2,
+        out_specs=[hbm] * 6 + [vmem] * 2,
         scratch_shapes=[
             pltpu.VMEM((TOK + 2 * BAND, 3 * C), bf16),
             pltpu.VMEM((TOK, C), f32),
@@ -384,11 +358,12 @@
             pltpu.VMEM((BAND, C), f32),
             pltpu.VMEM((TOK, C), bf16),
             pltpu.VMEM((TOK, C), bf16),
+            pltpu.VMEM((TOK, C), bf16),
             pltpu.VMEM((3, 3 * C, C), bf16),
             pltpu.VMEM((C, 3 * C), bf16),
             pltpu.VMEM((C, C), bf16),
             pltpu.VMEM((TDIM, C), bf16),
-            pltpu.SemaphoreType.DMA((20,)),
+            pltpu.SemaphoreType.DMA((14,)),
         ],
         compiler_params=pltpu.CompilerParams(vmem_limit_bytes=LIMIT * MIB),
         name="pair",
@@ -484,66 +459,190 @@
     )(part, x, cg, own, stat, gain, conv)
 
 
-def half_kernel(a_ref, out_ref, acc, mid):
+def share_kernel(part_ref, z_ref, gall_ref, side_ref, *refs):
+    outs, turned, share = refs[:8], refs[8], refs[9]
+    part = part_ref[0]
+
+    def place(x, v):
+        for y in range(2):
+            for z in range(8):
+                to, of = 80 * z + 20 * x + OWN * y, 80 * y + OWN * z
+                turned[to : to + OWN, :] = v[of : of + OWN]
+
+    @pl.when(part < 3)
+    def _():
+        at = lax.broadcasted_iota(jnp.int32, (160, C), 1)
+        cols = wire_columns(3 * OWN, C) + OWN * part
+        for x, low in enumerate((0, 384, 896, 1280)):
+            pick = jnp.where(at == cols + (480 * x - low), 1.0, 0.0).astype(bf16)
+            place(x, dot(pick, gall_ref[:, low : low + C], NT))
+
+    @pl.when(part == 3)
+    def _():
+        at = lax.broadcasted_iota(jnp.int32, (160, IMG), 1)
+        cols = wire_columns(OWN, IMG)
+        for x in range(4):
+            low = 3 * C + 128 * x
+            pick = jnp.where(at == cols + 32 * x, 1.0, 0.0).astype(bf16)
+            place(x, dot(pick, gall_ref[:, low : low + IMG], NT))
+
+    product = dot(turned[...].astype(bf16), side_ref[...])
+    for i in range(8):
+        share[i] = product[80 * i : 80 * (i + 1)].astype(bf16)
+    for k in range(8):
+        outs[k][...] = share[(z_ref[0] + k) & 7]
+
+
+def share_call(part, z, gall, side):
+    smem = pl.BlockSpec(memory_space=pltpu.SMEM)
+    vmem = pl.BlockSpec(memory_space=pltpu.VMEM)
+    return pl.pallas_call(
+        share_kernel,
+        out_shape=[jax.ShapeDtypeStruct((80, C), bf16)] * 8,
+        in_specs=[smem] * 2 + [vmem] * 2,
+        out_specs=[vmem] * 8,
+        scratch_shapes=[pltpu.VMEM((C, TOK), f32), pltpu.VMEM((8, 80, C), bf16)],
+        compiler_params=pltpu.CompilerParams(vmem_limit_bytes=24 * MIB),
+        cost_estimate=pl.CostEstimate(
+            flops=4 * TOK * C * C, bytes_accessed=TOK * 5 * C * 2, transcendentals=0
+        ),
+        name="share",
+    )(part, z, gall, side)
+
+
+def half_kernel(
+    z_ref, y_ref, a_ref, shares, gains_ref, out_ref, keep_ref, send_ref, acc, mid, ext, both
+):
     total = a_ref[0].astype(f32)
     for i in range(1, 8):
         total = total + a_ref[i].astype(f32)
     acc[...] = total
-    mid[:, OWN * BLOCKS :, :] = jnp.zeros((8, CHUNK - OWN * BLOCKS, 128), f32)
     for i in range(8):
-        for k in range(BLOCKS):
+        for k in range(TAP_BLOCKS):
             mid[i, OWN * k : OWN * (k + 1), :] = acc[
                 OWN * i : OWN * (i + 1), 128 * k : 128 * (k + 1)
             ]
     out_ref[...] = mid[...].astype(bf16)
-
-
-def half_call(a):
+    total = shares[0][...].astype(f32)
+    for i in range(1, 8):
+        total = total + shares[i][...].astype(f32)
+    ext[:, 0:C] = total
+    gains = gains_ref[...]
+    high = gains.astype(bf16).astype(f32)
+    rest = gains - high
+    middle = rest.astype(bf16).astype(f32)
+    stack = jnp.concatenate([high, middle, rest - middle, jnp.zeros((10, C), f32)], axis=0)
+    n = lax.broadcasted_iota(jnp.int32, (80, C), 0)
+    x = (n * 3277) >> 16
+    cols = 160 * x + 20 * z_ref[0] + n - 20 * x
+    pick = jnp.where(lax.broadcasted_iota(jnp.int32, (80, C), 1) == cols, 1.0, 0.0)
+    sums = dot(pick.astype(bf16), stack.astype(bf16), NT)
+    lane = lax.broadcasted_iota(jnp.int32, (80, 128), 1)
+    gain = sums[:, 0:1] + sums[:, 2:3] + sums[:, 4:5]
+    bias = sums[:, 1:2] + sums[:, 3:4] + sums[:, 5:6]
+    ext[:, C:] = jnp.where(lane == 0, gain, jnp.where(lane == 1, bias, 0.0))
+    both[...] = jnp.zeros(both.shape, f32)
+    for i in range(4):
+        for y in range(2):
+            of = 20 * i + OWN * y
+            both[y, i, 0:OWN, :] = ext[of : of + OWN, :]
+    keep_ref[...] = both[y_ref[0]]
+    send_ref[...] = both[1 - y_ref[0]].astype(bf16)
+
+
+def half_call(z, y, a, shares, gains):
+    smem = pl.BlockSpec(memory_space=pltpu.SMEM)
     vmem = pl.BlockSpec(memory_space=pltpu.VMEM)
     return pl.pallas_call(
-        half_kernel,
-        out_shape=jax.ShapeDtypeStruct((8, CHUNK, 128), bf16),
-        in_specs=[vmem],
-        out_specs=vmem,
+        lambda z, y, a, *refs: half_kernel(z, y, a, refs[:8], *refs[8:]),
+        out_shape=(
+            jax.ShapeDtypeStruct((8, TAP_ROWS, 128), bf16),
+            jax.ShapeDtypeStruct((4, 16, SIDE), f32),
+            jax.ShapeDtypeStruct((4, 16, SIDE), bf16),
+        ),
+        in_specs=[smem] * 2 + [vmem] * 10,
+        out_specs=[vmem] * 3,
         scratch_shapes=[
             pltpu.VMEM((80, WIDTH), f32),
-            pltpu.VMEM((8, CHUNK, 128), f32),
+            pltpu.VMEM((8, TAP_ROWS, 128), f32),
+            pltpu.VMEM((80, SIDE), f32),
+            pltpu.VMEM((2, 4, 16, SIDE), f32),
         ],
         compiler_params=pltpu.CompilerParams(vmem_limit_bytes=32 * MIB),
         name="half",
-    )(a)
-
-
-def total_kernel(a_ref, out_ref):
+    )(z, y, a, *shares, gains)
+
+
+def side_kernel(x_ref, keep_ref, got_ref, own_ref, one_ref, two_ref, three_ref, both):
+    both[...] = keep_ref[...] + got_ref[...].astype(f32)
+    x = x_ref[0]
+    own_ref[...] = both[x]
+    for k, ref in enumerate((one_ref, two_ref, three_ref)):
+        ref[...] = both[(x + k + 1) & 3].astype(bf16)
+
+
+def side_call(x, keep, got):
+    smem = pl.BlockSpec(memory_space=pltpu.SMEM)
+    vmem = pl.BlockSpec(memory_space=pltpu.VMEM)
+    return pl.pallas_call(
+        side_kernel,
+        out_shape=[jax.ShapeDtypeStruct((16, SIDE), f32)]
+        + [jax.ShapeDtypeStruct((16, SIDE), bf16)] * 3,
+        in_specs=[smem] + [vmem] * 2,
+        out_specs=[vmem] * 4,
+        scratch_shapes=[pltpu.VMEM((4, 16, SIDE), f32)],
+        compiler_params=pltpu.CompilerParams(vmem_limit_bytes=16 * MIB),
+        name="side",
+    )(x, keep, got)
+
+
+def total_kernel(a_ref, own_ref, one_ref, two_ref, three_ref, out_ref, gain_ref, mid):
     total = a_ref[0].astype(f32)
     for i in range(1, 8):
         total = total + a_ref[i].astype(f32)
-    out_ref[...] = total
-
-
-def total_call(a):
+    out_ref[0:TAP_ROWS, :] = total
+    mid[...] = (
+        own_ref[...]
+        + one_ref[...].astype(f32)
+        + two_ref[...].astype(f32)
+        + three_ref[...].astype(f32)
+    )
+    for k in range(5):
+        at = TAP_ROWS + OWN * k
+        out_ref[at : at + OWN, :] = mid[0:OWN, 128 * k : 128 * (k + 1)]
+    out_ref[TAP_ROWS + 5 * OWN :, :] = jnp.zeros((CHUNK - TAP_ROWS - 5 * OWN, 128), f32)
+    tail = jnp.concatenate([mid[:, C:], jnp.zeros((112, 128), f32)], axis=0)
+    gain_ref[...] = jnp.transpose(tail)[0:8]
+
+
+def total_call(a, own, one, two, three):
     vmem = pl.BlockSpec(memory_space=pltpu.VMEM)
     return pl.pallas_call(
         total_kernel,
-        out_shape=jax.ShapeDtypeStruct((CHUNK, 128), f32),
-        in_specs=[vmem],
-        out_specs=vmem,
+        out_shape=(
+            jax.ShapeDtypeStruct((CHUNK, 128), f32),
+            jax.ShapeDtypeStruct((8, 128), f32),
+        ),
+        in_specs=[vmem] * 5,
+        out_specs=[vmem] * 2,
+        scratch_shapes=[pltpu.VMEM((16, SIDE), f32)],
         compiler_params=pltpu.CompilerParams(vmem_limit_bytes=16 * MIB),
         name="total",
-    )(a)
+    )(a, own, one, two, three)
 
 
 def unpack_kernel(all_ref, conv_ref, qkv_ref, out_ref, time_ref):
     for part in range(4):
         for k in range(5):
-            rows = all_ref[part, OWN * k : OWN * (k + 1), :]
+            at = TAP_ROWS + OWN * k
+            rows = all_ref[part, at : at + OWN, :]
             cols = slice(128 * k, 128 * (k + 1))
             if part < 3:
                 qkv_ref[OWN * part : OWN * (part + 1), cols] = rows
             else:
                 out_ref[:, cols] = rows
         for k in range(TAP_BLOCKS):
-            rows = all_ref[part, OWN * (5 + k) : OWN * (6 + k), :]
+            rows = all_ref[part, OWN * k : OWN * (k + 1), :]
             place = part * TAP_BLOCKS + k
             tap, block = place // 5, place % 5
             if place < 45:
@@ -585,13 +684,14 @@
     ref_error,
 ):
     part = lax.axis_index(SPACE_AXES).astype(jnp.int32).reshape(1)
+    at_x, at_z, at_y = (lax.axis_index(a).astype(jnp.int32).reshape(1) for a in PAIR_AXES)
     swap = [(0, 1), (1, 0)]
     own_xt = jnp.concatenate([section_input.reshape(BAND, C), target.reshape(BAND, C)], axis=0)
     near = lax.ppermute(own_xt, "y_lo", swap)
     core = lax.ppermute(own_xt, "core", swap)
     far = lax.ppermute(near, "core", swap)
     conv = conv_weight.reshape(3, 3 * C, C)
-    wire, x, cg, own, stat, margin = pair_call(
+    wire, x, gall, side, cg, own, stat, margin = pair_call(
         part,
         timesteps,
         labels,
@@ -608,16 +708,23 @@
         time_weight,
     )
     moved = lax.all_to_all(wire.reshape(8, 80, WIDTH), ("x", "y_hi"), 0, 0)
+    shares = share_call(part, at_z, gall, side)
+    cg, shares = lax.optimization_barrier((cg, shares))
+    shares = list(shares[:1]) + [
+        lax.ppermute(shares[k], "z", [(i, (i + k) % 8) for i in range(8)]) for k in range(1, 8)
+    ]
     input_grad, gains = input_call(part, x, cg, own, stat, norm_gain, conv)
     gains = lax.psum(gains, "z")
-    moved, gains = lax.optimization_barrier((moved, gains))
-    half, gains = lax.optimization_barrier((half_call(moved), gains))
+    moved, gains, shares = lax.optimization_barrier((moved, gains, shares))
+    half, keep, send = half_call(at_z, at_y, moved, shares, gains)
+    got = lax.ppermute(send, "y_hi", swap)
     moved = lax.all_to_all(half, "z", 0, 0)
-    gains = gains + lax.ppermute(gains, "y_hi", swap)
-    gains = gains + lax.ppermute(gains, "x", [(0, 1), (1, 0), (2, 3), (3, 2)])
-    gains = gains + lax.ppermute(gains, "x", [(0, 3), (3, 0), (1, 2), (2, 1)])
-    gains = lax.dynamic_slice_in_dim(gains, lax.axis_index(PAIR_AXES) * OWN, OWN, 1)
-    whole = lax.all_gather(total_call(moved), SPACE_AXES, axis=0, tiled=False)
+    mine, *sides = side_call(at_x, keep, got)
+    sides = [
+        lax.ppermute(sides[k - 1], "x", [(i, (i + k) % 4) for i in range(4)]) for k in range(1, 4)
+    ]
+    total, gains = total_call(moved, mine, *sides)
+    whole = lax.all_gather(total, SPACE_AXES, axis=0, tiled=False)
     conv_out, qkv_out, out_out, time_out = unpack_call(whole)
     pair_loss = jax.nn.softplus(BETA * margin[0, 0:1])
     return (
@@ -626,8 +733,8 @@
         qkv_out.T,
         out_out.T,
         time_out.T,
-        gains[0],
-        gains[1],
+        gains[0, :OWN],
+        gains[1, :OWN],
         pair_loss,
     )
 

time: 126 us -> 132 us (1.048)
  starting transfers between devices: 23.9 us -> 40.8 us
  waiting for transfers between devices: 21.6 us -> 7.03 us
  local copies, waits for them, and re-layouts: 7.7 us -> 9.59 us
  blocking collectives: 27.6 us -> 29.2 us
    ppermute x3 -> x11, starting transfers between devices: 2.81 us -> 24.6 us  [the longest x7 16.4 us: on_device(): lax.ppermute(shares[k], 'z', [(i, (i + k) % 8) for i in range(8)])]
    all_to_all x1, waiting for transfers between devices: 10.3 us -> 0.01 us  [on_device(): moved = lax.all_to_all(wire.reshape(8, 80, WIDTH), ('x', 'y_hi'), 0, 0)]
    all_gather x1, blocking collectives: 9.94 us -> 17.6 us  [on_device(): whole = lax.all_gather(total, SPACE_AXES, axis=0, tiled=False)]
    psum x1, blocking collectives: 17.6 us -> 11.6 us  [on_device(): gains = lax.psum(gains, 'z')]
    all_to_all x1, starting transfers between devices: 8.19 us -> 3.41 us  [on_device(): moved = lax.all_to_all(half, 'z', 0, 0)]
    ppermute x3 -> x11, waiting for transfers between devices: 5.95 us -> 2.05 us  [the longest x1 2.02 us: on_device(): got = lax.ppermute(send, 'y_hi', swap)]
    pallas_call x1, Pallas kernels: 30.2 us -> 27 us  [pair_call(): pl.pallas_call(pair_kernel, out_shape=(jax.ShapeDtypeStruct((C, WIDTH), b...]
    pallas_call x2 -> x4, Pallas kernels: 1.47 us -> 4.22 us  [the longest x1 2.53 us: share_call(): pl.pallas_call(share_kernel, out_shape=[jax.ShapeDtypeStruct((80, C), bf1...]
  transfers between devices with their start and end apart: 8 -> 16, of which waited for: 6 -> 2; matrix products, arithmetic and copies ran while one was open for 1% -> 1% of each run, Pallas kernels for 6% -> 7%
where the time goes in v4:
time: 132 us; the launch traced here: 131 us
  starting transfers between devices  40.8 us (31%)
  Pallas kernels  39.4 us (30%)
  blocking collectives  29.2 us (22%)
  local copies, waits for them, and re-layouts  9.59 us (7%)
  waiting for transfers between devices  7.03 us (5%)
  between operations  4.05 us (3%)
    pallas_call x1, Pallas kernels, pair_call(): pl.pallas_call(pair_kernel, out_shape=(jax.ShapeDtypeStruct((C, WIDTH), b...  27 us
    all_gather x1, blocking collectives, on_device(): whole = lax.all_gather(total, SPACE_AXES, axis=0, tiled=False)  17.6 us
    ppermute x7, starting transfers between devices, on_device(): lax.ppermute(shares[k], 'z', [(i, (i + k) % 8) for i in range(8)])  16.4 us
    psum x1, blocking collectives, on_device(): gains = lax.psum(gains, 'z')  11.6 us
    unnamed x24, local copies, waits for them, and re-layouts  7.87 us
    pallas_call x1, Pallas kernels, input_call(): pl.pallas_call(input_kernel, out_shape=(jax.ShapeDtypeStruct((BAND, C), b...  7.23 us
    all_to_all x1, starting transfers between devices, on_device(): moved = lax.all_to_all(wire.reshape(8, 80, WIDTH), ('x', 'y_hi'), 0, 0)  6.96 us
    ppermute x3, starting transfers between devices, on_device(): lax.ppermute(sides[k - 1], 'x', [(i, (i + k) % 4) for i in range(4)])  5.1 us
  transfers between devices with their start and end apart: 16, of which 2 were waited for; matrix products, arithmetic and copies ran while one was open for 1% of the time, Pallas kernels for 7%

profile of v4, /device:TPU:1, one launch (start us, length us, event | category | flops | bytes accessed | tf_op | source)
XLA Modules:
  0.0 131.1 jit_solution(15338073896936679540)
XLA Ops:
  0.6 1.0 pad_maximum_fusion.own_xt_ref
  1.7 2.2 %collective-permute-start = (bf16[256,640]{1,0:T(8,128)(2,1)S(1)}, bf16[256,640]{1,0:T(8,128)(2,1)S(1)}, u32[]{:S(2)}, u32[]{:S(2)}) collective-permute-start(bf16[256,640]{1,0:T(8,128)(2,1)S(1)} %pad_maximum_fusion.own_xt_ref), channel_id=1, source_target_pairs={{0,2},{2,0},{1,3},{3,1},{4,6},{6,4},{5,7},{7,5},{8,10},{10,8},{9,1... | collective-permute-start | bytes 983048 | tf_op jit(solution)/shard_map/ppermute | solution.py:690
  3.9 1.2 collective-permute-start.1
  5.1 5.0 %collective-permute-done.y_xt_ref = bf16[256,640]{1,0:T(8,128)(2,1)S(1)} collective-permute-done((bf16[256,640]{1,0:T(8,128)(2,1)S(1)}, bf16[256,640]{1,0:T(8,128)(2,1)S(1)}, u32[]{:S(2)}, u32[]{:S(2)}) %collective-permute-start) | collective-permute-done | bytes 327712 | tf_op jit(solution)/shard_map/ppermute | solution.py:690
  10.1 2.5 %collective-permute-start.2 = (bf16[256,640]{1,0:T(8,128)(2,1)S(1)}, bf16[256,640]{1,0:T(8,128)(2,1)S(1)}, u32[]{:S(2)}, u32[]{:S(2)}) collective-permute-start(bf16[256,640]{1,0:T(8,128)(2,1)S(1)} %collective-permute-done.y_xt_ref), channel_id=1, source_target_pairs={{0,1},{1,0},{2,3},{3,2},{4,5},{5,4},{6,7},{7,6},{8,9},{9,8},{10,11... | collective-permute-start | bytes 983048 | tf_op jit(solution)/shard_map/ppermute | solution.py:692
  13.9 0.0 collective-permute-done.1.core_xt_ref
  13.9 0.0 collective-permute-done.2.far_xt_ref
  13.9 0.7 copy-done.10
  14.6 0.1 copy-done.11
  14.8 27.0 %pair.1 = (bf16[640,1536]{1,0:T(8,128)(2,1)}, bf16[512,640]{1,0:T(8,128)(2,1)}, bf16[512,2560]{1,0:T(8,128)(2,1)}, bf16[512,640]{1,0:T(8,128)(2,1)}, bf16[512,64...) custom-call(s32[1]{0:T(128)} %bitcast.part_ref, s32[1]{0:T(128)S(6)} %copy.21.step_ref, ...), custom_call_target="tpu_custom_call" | custom-call | tf_op jit(solution)/shard_map/pair/pallas_call | solution.py:329
  41.8 0.0 copy-start.7
  41.8 7.0 %all-to-all-start = ((bf16[8,80,1536]{2,1,0:T(8,128)(2,1)}), bf16[8,80,1536]{2,1,0:T(8,128)(2,1)S(1)}, u32[]{:S(2)}, u32[]{:S(2)}) async-start(bf16[8,80,1536]{2,1,0:T(8,128)(2,1)} %bitcast.24), calls=%async_computation | async-start | bytes 3932160 | tf_op jit(solution)/shard_map/all_to_all | solution.py:710
  48.8 1.7 %copy-done.1 = bf16[512,2560]{1,0:T(8,128)(2,1)S(1)} copy-done((bf16[512,2560]{1,0:T(8,128)(2,1)S(1)}, bf16[512,2560]{1,0:T(8,128)(2,1)}, u32[]{:S(2)}) %copy-start.1) | copy-done | bytes 2621464
  50.6 2.5 %share.1 = (bf16[80,640]{1,0:T(8,128)(2,1)S(1)}, bf16[80,640]{1,0:T(8,128)(2,1)S(1)}, bf16[80,640]{1,0:T(8,128)(2,1)S(1)}, bf16[80,640]{1,0:T(8,128)(2,1)}, bf16...) custom-call(s32[1]{0:T(128)} %bitcast.part_ref, ...), custom_call_target="tpu_custom_call" | custom-call | flops 838860800 | bytes 3276800 | tf_op jit(solution)/shard_map/share/pallas_call | solution.py:499
  53.1 1.6 %collective-permute-start.3 = (bf16[80,640]{1,0:T(8,128)(2,1)S(1)}, bf16[80,640]{1,0:T(8,128)(2,1)S(1)}, u32[]{:S(2)}, u32[]{:S(2)}) collective-permute-start(bf16[80,640]{1,0:T(8,128)(2,1)S(1)} %get-tuple-element.77), channel_id=1, source_target_pairs={{0,8},{8,16},{16,24},{24,32},{32,40},{40,48},{48,56},{56,0},{1,9},... | collective-permute-start | bytes 307208 | tf_op jit(solution)/shard_map/ppermute | solution.py:714
  54.7 3.0 %collective-permute-start.4 = (bf16[80,640]{1,0:T(8,128)(2,1)S(1)}, bf16[80,640]{1,0:T(8,128)(2,1)S(1)}, u32[]{:S(2)}, u32[]{:S(2)}) collective-permute-start(bf16[80,640]{1,0:T(8,128)(2,1)S(1)} %get-tuple-element.78), channel_id=1, source_target_pairs={{0,16},{8,24},{16,32},{24,40},{32,48},{40,56},{48,0},{56,8},{1,17}... | collective-permute-start | bytes 307208 | tf_op jit(solution)/shard_map/ppermute | solution.py:714
  57.7 3.8 %collective-permute-start.5 = (bf16[80,640]{1,0:T(8,128)(2,1)}, bf16[80,640]{1,0:T(8,128)(2,1)S(1)}, u32[]{:S(2)}, u32[]{:S(2)}) collective-permute-start(bf16[80,640]{1,0:T(8,128)(2,1)} %get-tuple-element.79), channel_id=1, source_target_pairs={{0,24},{8,32},{16,40},{24,48},{32,56},{40,0},{48,8},{56,16},{1,25}... | collective-permute-start | bytes 307208 | tf_op jit(solution)/shard_map/ppermute | solution.py:714
  61.5 0.5 collective-permute-start.6
  61.9 4.5 %collective-permute-start.7 = (bf16[80,640]{1,0:T(8,128)(2,1)}, bf16[80,640]{1,0:T(8,128)(2,1)S(1)}, u32[]{:S(2)}, u32[]{:S(2)}) collective-permute-start(bf16[80,640]{1,0:T(8,128)(2,1)} %get-tuple-element.81), channel_id=1, source_target_pairs={{0,40},{8,48},{16,56},{24,0},{32,8},{40,16},{48,24},{56,32},{1,41}... | collective-permute-start | bytes 307208 | tf_op jit(solution)/shard_map/ppermute | solution.py:714
  66.4 0.0 collective-permute-done.3.refs_1_
  66.4 2.4 %collective-permute-start.8 = (bf16[80,640]{1,0:T(8,128)(2,1)}, bf16[80,640]{1,0:T(8,128)(2,1)S(1)}, u32[]{:S(2)}, u32[]{:S(2)}) collective-permute-start(bf16[80,640]{1,0:T(8,128)(2,1)} %get-tuple-element.82), channel_id=1, source_target_pairs={{0,48},{8,56},{16,0},{24,8},{32,16},{40,24},{48,32},{56,40},{1,49}... | collective-permute-start | bytes 307208 | tf_op jit(solution)/shard_map/ppermute | solution.py:714
  68.8 0.0 collective-permute-done.4.refs_2_
  68.8 0.7 collective-permute-start.9
  69.5 3.1 %copy-done = bf16[3,3,640,640]{3,2,1,0:T(8,128)(2,1)S(1)} copy-done((bf16[3,3,640,640]{3,2,1,0:T(8,128)(2,1)S(1)}, bf16[3,3,640,640]{3,2,1,0:T(8,128)(2,1)}, u32[]{:S(2)}) %copy-start) | copy-done | bytes 7372824
  72.6 1.1 copy-done.4
  73.7 1.1 copy-done.5
  74.8 7.2 %input.1 = (bf16[128,640]{1,0:T(8,128)(2,1)}, f32[2,640]{1,0:T(2,128)S(1)}) custom-call(s32[1]{0:T(128)} %bitcast.part_ref, bf16[512,640]{1,0:T(8,128)(2,1)S(1)} %copy-done.4, bf16[512,640]{1,0:T(8,128)(2,1)S(1)} %copy-done.5, f32[128,640]{1,0:T(8,128)S(1)} %copy-done.6, f32[8,640]{1,0:T(8,128)S(1)} %copy-done.7, f32[640]{0:T(1024)S(1)} %copy-done.3, ...), custom_call_target="tpu_custom_call" | custom-call | flops 3774873600 | bytes 7372800 | tf_op jit(solution)/shard_map/input/pallas_call | solution.py:442
  82.0 11.6 %psum.7.refs_8_ = f32[2,640]{1,0:T(2,128)S(1)} all-reduce(f32[2,640]{1,0:T(2,128)S(1)} %get-tuple-element.75), channel_id=1, replica_groups=mesh['x'=4,'z'=8,'y_hi'=2,'y_lo'=2,'core'=2] {'z'}, use_global_device_ids=true, to_apply=%region_0.0 | all-reduce | flops 1280 | bytes 10240 | tf_op jit(solution)/shard_map/psum | solution.py:717
  93.6 0.0 collective-permute-done.5.refs_3_
  93.6 0.0 collective-permute-done.6.refs_4_
  93.7 0.0 collective-permute-done.7.refs_5_
  93.7 0.0 collective-permute-done.8.refs_6_
  93.7 0.0 collective-permute-done.9.refs_7_
  93.7 0.0 all-to-all-done.a
  93.7 1.6 %half.1 = (bf16[8,120,128]{2,1,0:T(8,128)(2,1)}, f32[4,16,768]{2,1,0:T(8,128)S(1)}, bf16[4,16,768]{2,1,0:T(8,128)(2,1)S(1)}) custom-call(s32[1]{0:T(128)} %bitcast.4.z_ref.z, s32[1]{0:T(128)} %bitcast.7.y, bf16[8,80,1536]{2,1,0:T(8,128)(2,1)S(1)} %all-to-all-done.a, bf16[80,640]{1,0:T(8,128)(2,1)S(1)} %get-tuple-element.85.refs_0_, ...), custom_call_target="tpu_custom_call" | custom-call | tf_op jit(solution)/shard_map/half/pallas_call | solution.py:556
  95.3 3.4 %all-to-all-start.1 = ((bf16[8,120,128]{2,1,0:T(8,128)(2,1)}), bf16[8,120,128]{2,1,0:T(8,128)(2,1)S(1)}, u32[]{:S(2)}, u32[]{:S(2)}) async-start(bf16[8,120,128]{2,1,0:T(8,128)(2,1)} %get-tuple-element.94), calls=%async_computation.1 | async-start | bytes 491520 | tf_op jit(solution)/shard_map/all_to_all | solution.py:721
  98.7 3.0 %collective-permute-start.10 = (bf16[4,16,768]{2,1,0:T(8,128)(2,1)S(1)}, bf16[4,16,768]{2,1,0:T(8,128)(2,1)S(1)}, u32[]{:S(2)}, u32[]{:S(2)}) collective-permute-start(bf16[4,16,768]{2,1,0:T(8,128)(2,1)S(1)} %get-tuple-element.96), channel_id=1, source_target_pairs={{0,4},{4,0},{1,5},{5,1},{2,6},{6,2},{3,7},{7,3},{8,12},{12,8},{9,1... | collective-permute-start | bytes 294920 | tf_op jit(solution)/shard_map/ppermute | solution.py:720
  101.7 2.0 %collective-permute-done.10.got_ref = bf16[4,16,768]{2,1,0:T(8,128)(2,1)S(1)} collective-permute-done((bf16[4,16,768]{2,1,0:T(8,128)(2,1)S(1)}, bf16[4,16,768]{2,1,0:T(8,128)(2,1)S(1)}, u32[]{:S(2)}, u32[]{:S(2)}) %collective-permute-start.10) | collective-permute-done | bytes 98336 | tf_op jit(solution)/shard_map/ppermute | solution.py:720
  103.8 1.5 %collective-permute-start.11 = (bf16[16,768]{1,0:T(8,128)(2,1)S(1)}, bf16[16,768]{1,0:T(8,128)(2,1)S(1)}, u32[]{:S(2)}, u32[]{:S(2)}) collective-permute-start(bf16[16,768]{1,0:T(8,128)(2,1)S(1)} %get-tuple-element.98), channel_id=1, source_target_pairs={{0,64},{64,128},{128,192},{192,0},{1,65},{65,129},{129,193},{193,1... | collective-permute-start | bytes 73736 | tf_op jit(solution)/shard_map/ppermute | solution.py:724
  105.3 2.4 %collective-permute-start.12 = (bf16[16,768]{1,0:T(8,128)(2,1)S(1)}, bf16[16,768]{1,0:T(8,128)(2,1)S(1)}, u32[]{:S(2)}, u32[]{:S(2)}) collective-permute-start(bf16[16,768]{1,0:T(8,128)(2,1)S(1)} %get-tuple-element.99), channel_id=1, source_target_pairs={{0,128},{64,192},{128,0},{192,64},{1,129},{65,193},{129,1},{193,65... | collective-permute-start | bytes 73736 | tf_op jit(solution)/shard_map/ppermute | solution.py:724
  107.7 1.2 collective-permute-start.13
  108.9 1.2 slice.11
  110.8 0.0 collective-permute-done.12.two_ref
  110.9 0.0 collective-permute-done.13.three_ref
  110.9 0.1 total.1
  111.0 17.6 %all-gather = f32[704,128]{1,0:T(8,128)S(1)} all-gather(f32[176,128]{1,0:T(8,128)S(1)} %get-tuple-element.101), channel_id=2, replica_groups=mesh['x'=4,'z'=8,'y_hi'=2,'y_lo'=2,'core'=2] {'y_lo','core'}, dimensions={0}, use_global_device_ids=true | all-gather | bytes 450560 | tf_op jit(solution)/shard_map/all_gather | solution.py:727
  128.5 0.9 unpack.1
  129.4 0.5 slice_bitcast_fusion
  (20 shorter events, 0.1 us)
Async XLA Ops:
  1.7 12.2 %copy-start.8 = (bf16[256,640]{1,0:T(8,128)(2,1)}, bf16[256,640]{1,0:T(8,128)(2,1)S(1)}, u32[]{:S(2)}) copy-start(bf16[256,640]{1,0:T(8,128)(2,1)S(1)} %pad_maximum_fusion.own_xt_ref) | copy-start | bytes 983044
  1.7 8.4 %collective-permute-start = (bf16[256,640]{1,0:T(8,128)(2,1)S(1)}, bf16[256,640]{1,0:T(8,128)(2,1)S(1)}, u32[]{:S(2)}, u32[]{:S(2)}) collective-permute-start(bf16[256,640]{1,0:T(8,128)(2,1)S(1)} %pad_maximum_fusion.own_xt_ref), channel_id=1, source_target_pairs={{0,2},{2,0},{1,3},{3,1},{4,6},{6,4},{5,7},{7,5},{8,10},{10,8},{9,1... | collective-permute-start | bytes 983048 | tf_op jit(solution)/shard_map/ppermute | solution.py:690
  3.9 10.0 %collective-permute-start.1 = (bf16[256,640]{1,0:T(8,128)(2,1)S(1)}, bf16[256,640]{1,0:T(8,128)(2,1)S(1)}, u32[]{:S(2)}, u32[]{:S(2)}) collective-permute-start(bf16[256,640]{1,0:T(8,128)(2,1)S(1)} %pad_maximum_fusion.own_xt_ref), channel_id=1, source_target_pairs={{0,1},{1,0},{2,3},{3,2},{4,5},{5,4},{6,7},{7,6},{8,9},{9,8},{10,11... | collective-permute-start | bytes 983048 | tf_op jit(solution)/shard_map/ppermute | solution.py:691
  10.1 3.8 %copy-start.9 = (bf16[256,640]{1,0:T(8,128)(2,1)}, bf16[256,640]{1,0:T(8,128)(2,1)S(1)}, u32[]{:S(2)}) copy-start(bf16[256,640]{1,0:T(8,128)(2,1)S(1)} %collective-permute-done.y_xt_ref) | copy-start | bytes 983044
  10.1 3.8 %collective-permute-start.2 = (bf16[256,640]{1,0:T(8,128)(2,1)S(1)}, bf16[256,640]{1,0:T(8,128)(2,1)S(1)}, u32[]{:S(2)}, u32[]{:S(2)}) collective-permute-start(bf16[256,640]{1,0:T(8,128)(2,1)S(1)} %collective-permute-done.y_xt_ref), channel_id=1, source_target_pairs={{0,1},{1,0},{2,3},{3,2},{4,5},{5,4},{6,7},{7,6},{8,9},{9,8},{10,11... | collective-permute-start | bytes 983048 | tf_op jit(solution)/shard_map/ppermute | solution.py:692
  13.9 0.8 copy-start.10
  13.9 0.9 copy-start.11
  41.8 7.0 %copy-start.2 = (bf16[512,640]{1,0:T(8,128)(2,1)S(1)}, bf16[512,640]{1,0:T(8,128)(2,1)}, u32[]{:S(2)}) copy-start(bf16[512,640]{1,0:T(8,128)(2,1)} %get-tuple-element.61.side_ref) | copy-start | bytes 1966084
  41.8 27.7 %copy-start.6 = (f32[128,640]{1,0:T(8,128)S(1)}, f32[128,640]{1,0:T(8,128)}, u32[]{:S(2)}) copy-start(f32[128,640]{1,0:T(8,128)} %get-tuple-element.71.own_ref) | copy-start | bytes 983044
  41.8 27.7 %copy-start.7 = (f32[8,640]{1,0:T(8,128)S(1)}, f32[8,640]{1,0:T(8,128)}, u32[]{:S(2)}) copy-start(f32[8,640]{1,0:T(8,128)} %get-tuple-element.72.stat_ref) | copy-start | bytes 61444
  41.8 51.9 %all-to-all-start = ((bf16[8,80,1536]{2,1,0:T(8,128)(2,1)}), bf16[8,80,1536]{2,1,0:T(8,128)(2,1)S(1)}, u32[]{:S(2)}, u32[]{:S(2)}) async-start(bf16[8,80,1536]{2,1,0:T(8,128)(2,1)} %bitcast.24), calls=%async_computation | async-start | bytes 3932160 | tf_op jit(solution)/shard_map/all_to_all | solution.py:710
  48.8 20.7 %copy-start.3 = (f32[640]{0:T(1024)S(1)}, f32[640]{0:T(1024)}, u32[]{:S(2)}) copy-start(f32[640]{0:T(1024)} %gain_ref.3) | copy-start | bytes 7684
  48.8 1.7 %copy-start.1 = (bf16[512,2560]{1,0:T(8,128)(2,1)S(1)}, bf16[512,2560]{1,0:T(8,128)(2,1)}, u32[]{:S(2)}) copy-start(bf16[512,2560]{1,0:T(8,128)(2,1)} %get-tuple-element.60.gall_ref) | copy-start | bytes 7864324
  53.1 13.3 %collective-permute-start.3 = (bf16[80,640]{1,0:T(8,128)(2,1)S(1)}, bf16[80,640]{1,0:T(8,128)(2,1)S(1)}, u32[]{:S(2)}, u32[]{:S(2)}) collective-permute-start(bf16[80,640]{1,0:T(8,128)(2,1)S(1)} %get-tuple-element.77), channel_id=1, source_target_pairs={{0,8},{8,16},{16,24},{24,32},{32,40},{40,48},{48,56},{56,0},{1,9},... | collective-permute-start | bytes 307208 | tf_op jit(solution)/shard_map/ppermute | solution.py:714
  54.7 14.1 %collective-permute-start.4 = (bf16[80,640]{1,0:T(8,128)(2,1)S(1)}, bf16[80,640]{1,0:T(8,128)(2,1)S(1)}, u32[]{:S(2)}, u32[]{:S(2)}) collective-permute-start(bf16[80,640]{1,0:T(8,128)(2,1)S(1)} %get-tuple-element.78), channel_id=1, source_target_pairs={{0,16},{8,24},{16,32},{24,40},{32,48},{40,56},{48,0},{56,8},{1,17}... | collective-permute-start | bytes 307208 | tf_op jit(solution)/shard_map/ppermute | solution.py:714
  57.7 35.9 %collective-permute-start.5 = (bf16[80,640]{1,0:T(8,128)(2,1)}, bf16[80,640]{1,0:T(8,128)(2,1)S(1)}, u32[]{:S(2)}, u32[]{:S(2)}) collective-permute-start(bf16[80,640]{1,0:T(8,128)(2,1)} %get-tuple-element.79), channel_id=1, source_target_pairs={{0,24},{8,32},{16,40},{24,48},{32,56},{40,0},{48,8},{56,16},{1,25}... | collective-permute-start | bytes 307208 | tf_op jit(solution)/shard_map/ppermute | solution.py:714
  61.5 32.2 %collective-permute-start.6 = (bf16[80,640]{1,0:T(8,128)(2,1)}, bf16[80,640]{1,0:T(8,128)(2,1)S(1)}, u32[]{:S(2)}, u32[]{:S(2)}) collective-permute-start(bf16[80,640]{1,0:T(8,128)(2,1)} %get-tuple-element.80), channel_id=1, source_target_pairs={{0,32},{8,40},{16,48},{24,56},{32,0},{40,8},{48,16},{56,24},{1,33}... | collective-permute-start | bytes 307208 | tf_op jit(solution)/shard_map/ppermute | solution.py:714
  61.9 31.7 %collective-permute-start.7 = (bf16[80,640]{1,0:T(8,128)(2,1)}, bf16[80,640]{1,0:T(8,128)(2,1)S(1)}, u32[]{:S(2)}, u32[]{:S(2)}) collective-permute-start(bf16[80,640]{1,0:T(8,128)(2,1)} %get-tuple-element.81), channel_id=1, source_target_pairs={{0,40},{8,48},{16,56},{24,0},{32,8},{40,16},{48,24},{56,32},{1,41}... | collective-permute-start | bytes 307208 | tf_op jit(solution)/shard_map/ppermute | solution.py:714
  66.4 27.3 %collective-permute-start.8 = (bf16[80,640]{1,0:T(8,128)(2,1)}, bf16[80,640]{1,0:T(8,128)(2,1)S(1)}, u32[]{:S(2)}, u32[]{:S(2)}) collective-permute-start(bf16[80,640]{1,0:T(8,128)(2,1)} %get-tuple-element.82), channel_id=1, source_target_pairs={{0,48},{8,56},{16,0},{24,8},{32,16},{40,24},{48,32},{56,40},{1,49}... | collective-permute-start | bytes 307208 | tf_op jit(solution)/shard_map/ppermute | solution.py:714
  68.8 24.9 %collective-permute-start.9 = (bf16[80,640]{1,0:T(8,128)(2,1)S(1)}, bf16[80,640]{1,0:T(8,128)(2,1)S(1)}, u32[]{:S(2)}, u32[]{:S(2)}) collective-permute-start(bf16[80,640]{1,0:T(8,128)(2,1)S(1)} %get-tuple-element.83), channel_id=1, source_target_pairs={{0,56},{8,0},{16,8},{24,16},{32,24},{40,32},{48,40},{56,48},{1,57}... | collective-permute-start | bytes 307208 | tf_op jit(solution)/shard_map/ppermute | solution.py:714
  69.5 3.1 %copy-start = (bf16[3,3,640,640]{3,2,1,0:T(8,128)(2,1)S(1)}, bf16[3,3,640,640]{3,2,1,0:T(8,128)(2,1)}, u32[]{:S(2)}) copy-start(bf16[3,3,640,640]{3,2,1,0:T(8,128)(2,1)} %param.14) | copy-start | bytes 22118404
  72.6 1.1 copy-start.4
  73.7 1.1 copy-start.5
  95.3 15.6 %all-to-all-start.1 = ((bf16[8,120,128]{2,1,0:T(8,128)(2,1)}), bf16[8,120,128]{2,1,0:T(8,128)(2,1)S(1)}, u32[]{:S(2)}, u32[]{:S(2)}) async-start(bf16[8,120,128]{2,1,0:T(8,128)(2,1)} %get-tuple-element.94), calls=%async_computation.1 | async-start | bytes 491520 | tf_op jit(solution)/shard_map/all_to_all | solution.py:721
  98.7 5.1 %collective-permute-start.10 = (bf16[4,16,768]{2,1,0:T(8,128)(2,1)S(1)}, bf16[4,16,768]{2,1,0:T(8,128)(2,1)S(1)}, u32[]{:S(2)}, u32[]{:S(2)}) collective-permute-start(bf16[4,16,768]{2,1,0:T(8,128)(2,1)S(1)} %get-tuple-element.96), channel_id=1, source_target_pairs={{0,4},{4,0},{1,5},{5,1},{2,6},{6,2},{3,7},{7,3},{8,12},{12,8},{9,1... | collective-permute-start | bytes 294920 | tf_op jit(solution)/shard_map/ppermute | solution.py:720
  103.8 7.0 %collective-permute-start.11 = (bf16[16,768]{1,0:T(8,128)(2,1)S(1)}, bf16[16,768]{1,0:T(8,128)(2,1)S(1)}, u32[]{:S(2)}, u32[]{:S(2)}) collective-permute-start(bf16[16,768]{1,0:T(8,128)(2,1)S(1)} %get-tuple-element.98), channel_id=1, source_target_pairs={{0,64},{64,128},{128,192},{192,0},{1,65},{65,129},{129,193},{193,1... | collective-permute-start | bytes 73736 | tf_op jit(solution)/shard_map/ppermute | solution.py:724
  105.3 5.5 %collective-permute-start.12 = (bf16[16,768]{1,0:T(8,128)(2,1)S(1)}, bf16[16,768]{1,0:T(8,128)(2,1)S(1)}, u32[]{:S(2)}, u32[]{:S(2)}) collective-permute-start(bf16[16,768]{1,0:T(8,128)(2,1)S(1)} %get-tuple-element.99), channel_id=1, source_target_pairs={{0,128},{64,192},{128,0},{192,64},{1,129},{65,193},{129,1},{193,65... | collective-permute-start | bytes 73736 | tf_op jit(solution)/shard_map/ppermute | solution.py:724
  107.7 3.1 %collective-permute-start.13 = (bf16[16,768]{1,0:T(8,128)(2,1)S(1)}, bf16[16,768]{1,0:T(8,128)(2,1)S(1)}, u32[]{:S(2)}, u32[]{:S(2)}) collective-permute-start(bf16[16,768]{1,0:T(8,128)(2,1)S(1)} %get-tuple-element.100), channel_id=1, source_target_pairs={{0,192},{64,0},{128,64},{192,128},{1,193},{65,1},{129,65},{193,129... | collective-permute-start | bytes 73736 | tf_op jit(solution)/shard_map/ppermute | solution.py:724

commit v5 on v4

--- a/solution.py
+++ b/solution.py
@@ -130,7 +130,7 @@
     cg_ref,
     own_ref,
     stat_ref,
-    margin_ref,
+    loss_ref,
     acat,
     acc,
     resid,
@@ -250,7 +250,9 @@
         sign = jnp.where(label_ref[0] == m, 1.0, -1.0)
         signs.append(sign)
         margin = margin + sign * (error - error_ref[0, m])
-    margin_ref[...] = jnp.broadcast_to(margin, (8, 128))
+    twice = BETA * margin
+    loss = jnp.maximum(twice, 0.0) + jnp.log1p(jnp.exp(-jnp.abs(twice)))
+    loss_ref[0] = loss[0, 0]
     slope = BETA * sigmoid(BETA * margin)
     for r, m, at in blocks():
         here = pl.ds(at, COLS)
@@ -336,10 +338,10 @@
             jax.ShapeDtypeStruct((TOK, C), bf16),
             jax.ShapeDtypeStruct((BAND, C), f32),
             jax.ShapeDtypeStruct((8, C), f32),
-            jax.ShapeDtypeStruct((8, 128), f32),
+            jax.ShapeDtypeStruct((1,), f32),
         ),
         in_specs=[smem] * 4 + [vmem] * 4 + [hbm] + [vmem] * 2 + [hbm] * 3 + [vmem],
-        out_specs=[hbm] * 6 + [vmem] * 2,
+        out_specs=[hbm] * 6 + [vmem, smem],
         scratch_shapes=[
             pltpu.VMEM((TOK + 2 * BAND, 3 * C), bf16),
             pltpu.VMEM((TOK, C), f32),
@@ -387,35 +389,72 @@
 
 
 def input_kernel(
-    part_ref, x_ref, cg_ref, own_ref, stat_ref, gain_ref, conv_ref, in_ref, gg_ref, gcat, acc
+    part_ref,
+    z_ref,
+    stat_ref,
+    gain_ref,
+    cg_ref,
+    x_ref,
+    own_ref,
+    gall_ref,
+    side_ref,
+    conv_ref,
+    in_ref,
+    *refs,
 ):
+    outs = refs[:8]
+    gcat, acc, cg_s, x_s, own_s, gall_s, side_s, conv_s, turned, columns, share, sems = refs[8:]
     part = part_ref[0]
+    load_cg = pltpu.make_async_copy(cg_ref, cg_s, sems.at[0])
+    taps = [pltpu.make_async_copy(conv_ref.at[i], conv_s.at[i], sems.at[1 + i]) for i in range(3)]
+    rest = [
+        pltpu.make_async_copy(ref, to, sems.at[4 + i])
+        for i, (ref, to) in enumerate(
+            ((x_ref, x_s), (own_ref, own_s), (gall_ref, gall_s), (side_ref, side_s))
+        )
+    ]
+    load_cg.start()
+    taps[0].start()
     gcat[0:BAND, :] = jnp.zeros((BAND, 3 * C), bf16)
     gcat[pl.ds(BAND + TOK, BAND), :] = jnp.zeros((BAND, 3 * C), bf16)
+    load_cg.wait()
+    taps[1].start()
+    bias_sum = jnp.zeros((1, C), f32)
     for r, m, at in blocks():
-        g = cg_ref[pl.ds(at, COLS), :]
+        g = cg_s[pl.ds(at, COLS), :]
+        wide = g.astype(f32)
+        bias_sum = bias_sum + jnp.sum(wide, axis=0, keepdims=True)
         here = pl.ds(BAND + at, COLS)
-        gcat[here, 0:C] = shifted(g.astype(f32), -1).astype(bf16)
+        gcat[here, 0:C] = shifted(wide, -1).astype(bf16)
         gcat[here, C : 2 * C] = g
-        gcat[here, 2 * C : 3 * C] = shifted(g.astype(f32), 1).astype(bf16)
+        gcat[here, 2 * C : 3 * C] = shifted(wide, 1).astype(bf16)
     for i in range(3):
+        taps[i].wait()
+        if i == 0:
+            taps[2].start()
+            rest[0].start()
+        if i == 1:
+            for load in rest[1:]:
+                load.start()
         for j in range(3):
             term = dot(
                 gcat[pl.ds((2 - i) * BAND, TOK), j * C : (j + 1) * C],
-                conv_ref[i, j * C : (j + 1) * C, :],
+                conv_s[i, j * C : (j + 1) * C, :],
                 NT,
             )
             if i == 0 and j == 0:
                 acc[...] = term
             else:
                 acc[...] += term
+    for load in rest:
+        load.wait()
     gain = gain_ref[...].reshape(1, C)
     gain_sum = jnp.zeros((1, C), f32)
     ones = [jnp.zeros((1, C), f32) for _ in range(2)]
     twos = [jnp.zeros((1, C), f32) for _ in range(2)]
     for r, m, at in blocks():
         here = pl.ds(at, COLS)
-        normed = (x_ref[here, :].astype(f32) - stat_ref[row(m), :]) * stat_ref[row(2 + m), :]
+        normed = (x_s[here, :].astype(f32) - stat_ref[row(m), :]) * stat_ref[row(2 + m), :]
         a = normed * gain
         s = sigmoid(a)
         pre = acc[here, :] * (s * (1.0 + a * (1.0 - s)))
@@ -424,50 +463,24 @@
         acc[here, :] = scaled
         ones[m] = ones[m] + jnp.sum(scaled, axis=0, keepdims=True)
         twos[m] = twos[m] + jnp.sum(scaled * normed, axis=0, keepdims=True)
-    bias_sum = jnp.sum(cg_ref[...].astype(f32), axis=0, keepdims=True)
-    gg_ref[...] = jnp.concatenate([gain_sum, bias_sum], axis=0)
-    means = group_sums(jnp.concatenate(ones + twos, axis=0)) / GROUP_COUNT
-    for m in range(2):
-        here = pl.ds(pl.multiple_of(part * BAND + m * COLS, COLS), COLS)
-        inv = stat_ref[row(2 + m), :]
-        normed = (x_ref[here, :].astype(f32) - stat_ref[row(m), :]) * inv
-        inner = inv * (acc[here, :] - means[m : m + 1] - normed * means[2 + m : 3 + m])
-        mine = slice(m * COLS, (m + 1) * COLS)
-        in_ref[mine, :] = (own_ref[mine, :] + inner).astype(bf16)
-
-
-def input_call(part, x, cg, own, stat, gain, conv):
-    smem = pl.BlockSpec(memory_space=pltpu.SMEM)
-    vmem = pl.BlockSpec(memory_space=pltpu.VMEM)
-    return pl.pallas_call(
-        input_kernel,
-        out_shape=(
-            jax.ShapeDtypeStruct((BAND, C), bf16),
-            jax.ShapeDtypeStruct((2, C), f32),
-        ),
-        in_specs=[smem] + [vmem] * 6,
-        out_specs=[vmem] * 2,
-        scratch_shapes=[
-            pltpu.VMEM((TOK + 2 * BAND, 3 * C), bf16),
-            pltpu.VMEM((TOK, C), f32),
-        ],
-        compiler_params=pltpu.CompilerParams(vmem_limit_bytes=40 * MIB),
-        cost_estimate=pl.CostEstimate(
-            flops=2 * TOK * 9 * C * C, bytes_accessed=9 * C * C * 2, transcendentals=TOK * C
-        ),
-        name="input",
-    )(part, x, cg, own, stat, gain, conv)
-
-
-def share_kernel(part_ref, z_ref, gall_ref, side_ref, *refs):
-    outs, turned, share = refs[:8], refs[8], refs[9]
-    part = part_ref[0]
-
-    def place(x, v):
+    lane = lax.broadcasted_iota(jnp.int32, (160, IMG), 1)
+    own_cols = wire_columns(OWN, IMG)
+
+    def place(to_ref, x, v):
         for y in range(2):
             for z in range(8):
                 to, of = 80 * z + 20 * x + OWN * y, 80 * y + OWN * z
-                turned[to : to + OWN, :] = v[of : of + OWN]
+                to_ref[to : to + OWN, :] = v[of : of + OWN]
+
+    rows = jnp.concatenate([gain_sum, bias_sum], axis=0)
+    high = rows.astype(bf16).astype(f32)
+    left = rows - high
+    middle = left.astype(bf16).astype(f32)
+    stack = jnp.concatenate([high, middle, left - middle, jnp.zeros((122, C), f32)], axis=0)
+    stack = stack.astype(bf16)
+    for x in range(4):
+        pick = jnp.where(lane == own_cols + 32 * x, 1.0, 0.0).astype(bf16)
+        place(columns, x, dot(pick, stack[:, 128 * x : 128 * x + IMG], NT))
 
     @pl.when(part < 3)
     def _():
@@ -475,44 +488,104 @@
         cols = wire_columns(3 * OWN, C) + OWN * part
         for x, low in enumerate((0, 384, 896, 1280)):
             pick = jnp.where(at == cols + (480 * x - low), 1.0, 0.0).astype(bf16)
-            place(x, dot(pick, gall_ref[:, low : low + C], NT))
+            place(turned, x, dot(pick, gall_s[:, low : low + C], NT))
 
     @pl.when(part == 3)
     def _():
-        at = lax.broadcasted_iota(jnp.int32, (160, IMG), 1)
-        cols = wire_columns(OWN, IMG)
         for x in range(4):
             low = 3 * C + 128 * x
-            pick = jnp.where(at == cols + 32 * x, 1.0, 0.0).astype(bf16)
-            place(x, dot(pick, gall_ref[:, low : low + IMG], NT))
-
-    product = dot(turned[...].astype(bf16), side_ref[...])
+            pick = jnp.where(lane == own_cols + 32 * x, 1.0, 0.0).astype(bf16)
+            place(turned, x, dot(pick, gall_s[:, low : low + IMG], NT))
+
+    product = dot(turned[...].astype(bf16), side_s[...])
+    at = lax.broadcasted_iota(jnp.int32, (80, 128), 1)
     for i in range(8):
-        share[i] = product[80 * i : 80 * (i + 1)].astype(bf16)
+        here = slice(80 * i, 80 * (i + 1))
+        share[i, :, 0:C] = product[here].astype(bf16)
+        sums = columns[here, :]
+        gains = sums[:, 0:1] + sums[:, 2:3] + sums[:, 4:5]
+        biases = sums[:, 1:2] + sums[:, 3:4] + sums[:, 5:6]
+        share[i, :, C:] = jnp.where(at == 0, gains, jnp.where(at == 1, biases, 0.0)).astype(bf16)
     for k in range(8):
         outs[k][...] = share[(z_ref[0] + k) & 7]
-
-
-def share_call(part, z, gall, side):
+    means = group_sums(jnp.concatenate(ones + twos, axis=0)) / GROUP_COUNT
+    for m in range(2):
+        here = pl.ds(pl.multiple_of(part * BAND + m * COLS, COLS), COLS)
+        inv = stat_ref[row(2 + m), :]
+        normed = (x_s[here, :].astype(f32) - stat_ref[row(m), :]) * inv
+        inner = inv * (acc[here, :] - means[m : m + 1] - normed * means[2 + m : 3 + m])
+        mine = slice(m * COLS, (m + 1) * COLS)
+        in_ref[mine, :] = (own_s[mine, :] + inner).astype(bf16)
+
+
+def input_call(part, z, stat, gain, cg, x, own, gall, side, conv):
+    smem = pl.BlockSpec(memory_space=pltpu.SMEM)
+    vmem = pl.BlockSpec(memory_space=pltpu.VMEM)
+    hbm = pl.BlockSpec(memory_space=pltpu.HBM)
+    return pl.pallas_call(
+        input_kernel,
+        out_shape=[jax.ShapeDtypeStruct((BAND, C), bf16)]
+        + [jax.ShapeDtypeStruct((80, SIDE), bf16)] * 8,
+        in_specs=[smem] * 2 + [vmem] * 2 + [hbm] * 6,
+        out_specs=[vmem] * 9,
+        scratch_shapes=[
+            pltpu.VMEM((TOK + 2 * BAND, 3 * C), bf16),
+            pltpu.VMEM((TOK, C), f32),
+            pltpu.VMEM((TOK, C), bf16),
+            pltpu.VMEM((TOK, C), bf16),
+            pltpu.VMEM((BAND, C), f32),
+            pltpu.VMEM((TOK, 4 * C), bf16),
+            pltpu.VMEM((TOK, C), bf16),
+            pltpu.VMEM((3, 3 * C, C), bf16),
+            pltpu.VMEM((C, TOK), f32),
+            pltpu.VMEM((C, 128), f32),
+            pltpu.VMEM((8, 80, SIDE), bf16),
+            pltpu.SemaphoreType.DMA((8,)),
+        ],
+        compiler_params=pltpu.CompilerParams(vmem_limit_bytes=LIMIT * MIB),
+        cost_estimate=pl.CostEstimate(
+            flops=2 * TOK * 10 * C * C, bytes_accessed=9 * C * C * 2, transcendentals=TOK * C
+        ),
+        name="input",
+    )(part, z, stat, gain, cg, x, own, gall, side, conv)
+
+
+def chunk_kernel(y_ref, *refs):
+    shares, keep_ref, send_ref, ext, both = refs[:8], *refs[8:]
+    total = shares[0][...].astype(f32)
+    for i in range(1, 8):
+        total = total + shares[i][...].astype(f32)
+    ext[...] = total
+    both[...] = jnp.zeros(both.shape, f32)
+    for i in range(4):
+        for y in range(2):
+            of = 20 * i + OWN * y
+            both[y, i, 0:OWN, :] = ext[of : of + OWN, :]
+    keep_ref[...] = both[y_ref[0]]
+    send_ref[...] = both[1 - y_ref[0]].astype(bf16)
+
+
+def chunk_call(y, shares):
     smem = pl.BlockSpec(memory_space=pltpu.SMEM)
     vmem = pl.BlockSpec(memory_space=pltpu.VMEM)
     return pl.pallas_call(
-        share_kernel,
-        out_shape=[jax.ShapeDtypeStruct((80, C), bf16)] * 8,
-        in_specs=[smem] * 2 + [vmem] * 2,
-        out_specs=[vmem] * 8,
-        scratch_shapes=[pltpu.VMEM((C, TOK), f32), pltpu.VMEM((8, 80, C), bf16)],
-        compiler_params=pltpu.CompilerParams(vmem_limit_bytes=24 * MIB),
-        cost_estimate=pl.CostEstimate(
-            flops=4 * TOK * C * C, bytes_accessed=TOK * 5 * C * 2, transcendentals=0
+        chunk_kernel,
+        out_shape=(
+            jax.ShapeDtypeStruct((4, 16, SIDE), f32),
+            jax.ShapeDtypeStruct((4, 16, SIDE), bf16),
         ),
-        name="share",
-    )(part, z, gall, side)
-
-
-def half_kernel(
-    z_ref, y_ref, a_ref, shares, gains_ref, out_ref, keep_ref, send_ref, acc, mid, ext, both
-):
+        in_specs=[smem] + [vmem] * 8,
+        out_specs=[vmem] * 2,
+        scratch_shapes=[
+            pltpu.VMEM((80, SIDE), f32),
+            pltpu.VMEM((2, 4, 16, SIDE), f32),
+        ],
+        compiler_params=pltpu.CompilerParams(vmem_limit_bytes=16 * MIB),
+        name="chunk",
+    )(y, *shares)
+
+
+def half_kernel(a_ref, out_ref, acc, mid):
     total = a_ref[0].astype(f32)
     for i in range(1, 8):
         total = total + a_ref[i].astype(f32)
@@ -523,54 +596,22 @@
                 OWN * i : OWN * (i + 1), 128 * k : 128 * (k + 1)
             ]
     out_ref[...] = mid[...].astype(bf16)
-    total = shares[0][...].astype(f32)
-    for i in range(1, 8):
-        total = total + shares[i][...].astype(f32)
-    ext[:, 0:C] = total
-    gains = gains_ref[...]
-    high = gains.astype(bf16).astype(f32)
-    rest = gains - high
-    middle = rest.astype(bf16).astype(f32)
-    stack = jnp.concatenate([high, middle, rest - middle, jnp.zeros((10, C), f32)], axis=0)
-    n = lax.broadcasted_iota(jnp.int32, (80, C), 0)
-    x = (n * 3277) >> 16
-    cols = 160 * x + 20 * z_ref[0] + n - 20 * x
-    pick = jnp.where(lax.broadcasted_iota(jnp.int32, (80, C), 1) == cols, 1.0, 0.0)
-    sums = dot(pick.astype(bf16), stack.astype(bf16), NT)
-    lane = lax.broadcasted_iota(jnp.int32, (80, 128), 1)
-    gain = sums[:, 0:1] + sums[:, 2:3] + sums[:, 4:5]
-    bias = sums[:, 1:2] + sums[:, 3:4] + sums[:, 5:6]
-    ext[:, C:] = jnp.where(lane == 0, gain, jnp.where(lane == 1, bias, 0.0))
-    both[...] = jnp.zeros(both.shape, f32)
-    for i in range(4):
-        for y in range(2):
-            of = 20 * i + OWN * y
-            both[y, i, 0:OWN, :] = ext[of : of + OWN, :]
-    keep_ref[...] = both[y_ref[0]]
-    send_ref[...] = both[1 - y_ref[0]].astype(bf16)
-
-
-def half_call(z, y, a, shares, gains):
-    smem = pl.BlockSpec(memory_space=pltpu.SMEM)
+
+
+def half_call(a):
     vmem = pl.BlockSpec(memory_space=pltpu.VMEM)
     return pl.pallas_call(
-        lambda z, y, a, *refs: half_kernel(z, y, a, refs[:8], *refs[8:]),
-        out_shape=(
-            jax.ShapeDtypeStruct((8, TAP_ROWS, 128), bf16),
-            jax.ShapeDtypeStruct((4, 16, SIDE), f32),
-            jax.ShapeDtypeStruct((4, 16, SIDE), bf16),
-        ),
-        in_specs=[smem] * 2 + [vmem] * 10,
-        out_specs=[vmem] * 3,
+        half_kernel,
+        out_shape=jax.ShapeDtypeStruct((8, TAP_ROWS, 128), bf16),
+        in_specs=[vmem],
+        out_specs=vmem,
         scratch_shapes=[
             pltpu.VMEM((80, WIDTH), f32),
             pltpu.VMEM((8, TAP_ROWS, 128), f32),
-            pltpu.VMEM((80, SIDE), f32),
-            pltpu.VMEM((2, 4, 16, SIDE), f32),
         ],
         compiler_params=pltpu.CompilerParams(vmem_limit_bytes=32 * MIB),
         name="half",
-    )(z, y, a, *shares, gains)
+    )(a)
 
 
 def side_kernel(x_ref, keep_ref, got_ref, own_ref, one_ref, two_ref, three_ref, both):
@@ -691,7 +732,7 @@
     core = lax.ppermute(own_xt, "core", swap)
     far = lax.ppermute(near, "core", swap)
     conv = conv_weight.reshape(3, 3 * C, C)
-    wire, x, gall, side, cg, own, stat, margin = pair_call(
+    wire, x, gall, side, cg, own, stat, pair_loss = pair_call(
         part,
         timesteps,
         labels,
@@ -708,17 +749,16 @@
         time_weight,
     )
     moved = lax.all_to_all(wire.reshape(8, 80, WIDTH), ("x", "y_hi"), 0, 0)
-    shares = share_call(part, at_z, gall, side)
-    cg, shares = lax.optimization_barrier((cg, shares))
-    shares = list(shares[:1]) + [
+    input_grad, *shares = input_call(
+        part, at_z, stat, norm_gain, cg, x, own, gall, side, conv
+    )
+    shares = shares[:1] + [
         lax.ppermute(shares[k], "z", [(i, (i + k) % 8) for i in range(8)]) for k in range(1, 8)
     ]
-    input_grad, gains = input_call(part, x, cg, own, stat, norm_gain, conv)
-    gains = lax.psum(gains, "z")
-    moved, gains, shares = lax.optimization_barrier((moved, gains, shares))
-    half, keep, send = half_call(at_z, at_y, moved, shares, gains)
+    keep, send = chunk_call(at_y, shares)
     got = lax.ppermute(send, "y_hi", swap)
-    moved = lax.all_to_all(half, "z", 0, 0)
+    moved, keep = lax.optimization_barrier((moved, keep))
+    moved = lax.all_to_all(half_call(moved), "z", 0, 0)
     mine, *sides = side_call(at_x, keep, got)
     sides = [
         lax.ppermute(sides[k - 1], "x", [(i, (i + k) % 4) for i in range(4)]) for k in range(1, 4)
@@ -726,7 +766,6 @@
     total, gains = total_call(moved, mine, *sides)
     whole = lax.all_gather(total, SPACE_AXES, axis=0, tiled=False)
     conv_out, qkv_out, out_out, time_out = unpack_call(whole)
-    pair_loss = jax.nn.softplus(BETA * margin[0, 0:1])
     return (
         input_grad.reshape(section_input.shape),
         conv_out.transpose(0, 2, 3, 1),

time: 132 us -> 125 us (0.947)
  blocking collectives: 29.2 us -> 9.26 us
  waiting for transfers between devices: 7.03 us -> 25.4 us
  local copies, waits for them, and re-layouts: 9.59 us -> 2.29 us
  Pallas kernels: 39.4 us -> 42.6 us
  between operations: 4.05 us -> 2.04 us
  starting transfers between devices: 40.8 us -> 42.2 us
    ppermute x7, waiting for transfers between devices: 0.02 us -> 16.6 us  [on_device(): lax.ppermute(shares[k], 'z', [(i, (i + k) % 8) for i in range(8)])]
    psum x1 -> x0, blocking collectives: 11.6 us -> none  [on_device(): gains = lax.psum(gains, 'z')]
    all_gather x1, blocking collectives: 17.6 us -> 9.26 us  [on_device(): whole = lax.all_gather(total, SPACE_AXES, axis=0, tiled=False)]
    unnamed x24 -> x10, local copies, waits for them, and re-layouts: 7.87 us -> 1.77 us
    pallas_call x3, Pallas kernels: 11.3 us -> 14.5 us  [the longest x1 13.1 us: input_call(): pl.pallas_call(input_kernel, out_shape=[jax.ShapeDtypeStruct((BAND, C), b...]
    ppermute x3, waiting for transfers between devices: 0.01 us -> 1.79 us  [on_device(): lax.ppermute(sides[k - 1], 'x', [(i, (i + k) % 4) for i in range(4)])]
    all_to_all x1, starting transfers between devices: 3.41 us -> 4.77 us  [on_device(): moved = lax.all_to_all(half_call(moved), 'z', 0, 0)]
  transfers between devices with their start and end apart: 16 -> 16, of which waited for: 2 -> 7; matrix products, arithmetic and copies ran while one was open for 1% -> 0% of each run, Pallas kernels for 7% -> 11%
where the time goes in v5:
time: 125 us
  Pallas kernels  42.6 us (34%)
  starting transfers between devices  42.2 us (34%)
  waiting for transfers between devices  25.4 us (20%)
  blocking collectives  9.26 us (7%)
  local copies, waits for them, and re-layouts  2.29 us (2%)
  between operations  2.04 us (2%)
    pallas_call x1, Pallas kernels, pair_call(): pl.pallas_call(pair_kernel, out_shape=(jax.ShapeDtypeStruct((C, WIDTH), b...  27 us
    ppermute x7, starting transfers between devices, on_device(): lax.ppermute(shares[k], 'z', [(i, (i + k) % 8) for i in range(8)])  16.6 us
    ppermute x7, waiting for transfers between devices, on_device(): lax.ppermute(shares[k], 'z', [(i, (i + k) % 8) for i in range(8)])  16.6 us
    pallas_call x1, Pallas kernels, input_call(): pl.pallas_call(input_kernel, out_shape=[jax.ShapeDtypeStruct((BAND, C), b...  13.1 us
    all_gather x1, blocking collectives, on_device(): whole = lax.all_gather(total, SPACE_AXES, axis=0, tiled=False)  9.26 us
    all_to_all x1, starting transfers between devices, on_device(): moved = lax.all_to_all(wire.reshape(8, 80, WIDTH), ('x', 'y_hi'), 0, 0)  6.82 us
    ppermute x3, starting transfers between devices, on_device(): lax.ppermute(sides[k - 1], 'x', [(i, (i + k) % 4) for i in range(4)])  5.12 us
    ppermute x1, waiting for transfers between devices, on_device(): near = lax.ppermute(own_xt, 'y_lo', swap)  4.97 us
  transfers between devices with their start and end apart: 16, of which 7 were waited for; matrix products, arithmetic and copies ran while one was open for 0% of the time, Pallas kernels for 11%

profile of v5, /device:TPU:1, one launch (start us, length us, event | category | flops | bytes accessed | tf_op | source)
XLA Modules:
  0.0 124.8 jit_solution(7026643043768574295)
XLA Ops:
  0.6 1.0 pad_maximum_fusion.own_xt_ref
  1.7 0.0 copy-start.1
  1.7 2.2 %collective-permute-start = (bf16[256,640]{1,0:T(8,128)(2,1)S(1)}, bf16[256,640]{1,0:T(8,128)(2,1)S(1)}, u32[]{:S(2)}, u32[]{:S(2)}) collective-permute-start(bf16[256,640]{1,0:T(8,128)(2,1)S(1)} %pad_maximum_fusion.own_xt_ref), channel_id=1, source_target_pairs={{0,2},{2,0},{1,3},{3,1},{4,6},{6,4},{5,7},{7,5},{8,10},{10,8},{9,1... | collective-permute-start | bytes 983048 | tf_op jit(solution)/shard_map/ppermute | solution.py:731
  3.9 1.2 collective-permute-start.1
  5.1 5.0 %collective-permute-done.y_xt_ref = bf16[256,640]{1,0:T(8,128)(2,1)S(1)} collective-permute-done((bf16[256,640]{1,0:T(8,128)(2,1)S(1)}, bf16[256,640]{1,0:T(8,128)(2,1)S(1)}, u32[]{:S(2)}, u32[]{:S(2)}) %collective-permute-start) | collective-permute-done | bytes 327712 | tf_op jit(solution)/shard_map/ppermute | solution.py:731
  10.1 2.5 %collective-permute-start.2 = (bf16[256,640]{1,0:T(8,128)(2,1)S(1)}, bf16[256,640]{1,0:T(8,128)(2,1)S(1)}, u32[]{:S(2)}, u32[]{:S(2)}) collective-permute-start(bf16[256,640]{1,0:T(8,128)(2,1)S(1)} %collective-permute-done.y_xt_ref), channel_id=1, source_target_pairs={{0,1},{1,0},{2,3},{3,2},{4,5},{5,4},{6,7},{7,6},{8,9},{9,8},{10,11... | collective-permute-start | bytes 983048 | tf_op jit(solution)/shard_map/ppermute | solution.py:733
  13.9 0.0 collective-permute-done.1.core_xt_ref
  13.9 0.0 copy-start.3
  13.9 0.0 collective-permute-done.2.far_xt_ref
  13.9 0.0 copy-start.4
  13.9 0.0 copy-done.1
  13.9 0.7 copy-done.3
  14.6 0.2 copy-done.4
  14.8 27.0 %pair.1 = (bf16[640,1536]{1,0:T(8,128)(2,1)}, bf16[512,640]{1,0:T(8,128)(2,1)}, bf16[512,2560]{1,0:T(8,128)(2,1)}, bf16[512,640]{1,0:T(8,128)(2,1)}, bf16[512,64...) custom-call(s32[1]{0:T(128)} %bitcast.part_ref, s32[1]{0:T(128)S(6)} %copy.21.step_ref, ...), custom_call_target="tpu_custom_call" | custom-call | tf_op jit(solution)/shard_map/pair/pallas_call | solution.py:331
  41.8 6.8 %all-to-all-start = ((bf16[8,80,1536]{2,1,0:T(8,128)(2,1)}), bf16[8,80,1536]{2,1,0:T(8,128)(2,1)S(1)}, u32[]{:S(2)}, u32[]{:S(2)}) async-start(bf16[8,80,1536]{2,1,0:T(8,128)(2,1)} %bitcast.23), calls=%async_computation | async-start | bytes 3932160 | tf_op jit(solution)/shard_map/all_to_all | solution.py:751
  48.6 13.1 %input.1 = (bf16[128,640]{1,0:T(8,128)(2,1)}, bf16[80,768]{1,0:T(8,128)(2,1)}, bf16[80,768]{1,0:T(8,128)(2,1)}, bf16[80,768]{1,0:T(8,128)(2,1)}, bf16[80,768]{1,...) custom-call(s32[1]{0:T(128)} %bitcast.part_ref, ...), custom_call_target="tpu_custom_call" | custom-call | flops 4194304000 | bytes 7372800 | tf_op jit(solution)/shard_map/input/pallas_call | solution.py:525
  61.8 1.7 %collective-permute-start.3 = (bf16[80,768]{1,0:T(8,128)(2,1)}, bf16[80,768]{1,0:T(8,128)(2,1)S(1)}, u32[]{:S(2)}, u32[]{:S(2)}) collective-permute-start(bf16[80,768]{1,0:T(8,128)(2,1)} %get-tuple-element.48), channel_id=1, source_target_pairs={{0,8},{8,16},{16,24},{24,32},{32,40},{40,48},{48,56},{56,0},{1,9},... | collective-permute-start | bytes 368648 | tf_op jit(solution)/shard_map/ppermute | solution.py:756
  63.5 3.0 %collective-permute-start.4 = (bf16[80,768]{1,0:T(8,128)(2,1)}, bf16[80,768]{1,0:T(8,128)(2,1)S(1)}, u32[]{:S(2)}, u32[]{:S(2)}) collective-permute-start(bf16[80,768]{1,0:T(8,128)(2,1)} %get-tuple-element.49), channel_id=1, source_target_pairs={{0,16},{8,24},{16,32},{24,40},{32,48},{40,56},{48,0},{56,8},{1,17}... | collective-permute-start | bytes 368648 | tf_op jit(solution)/shard_map/ppermute | solution.py:756
  66.5 3.8 %collective-permute-start.5 = (bf16[80,768]{1,0:T(8,128)(2,1)}, bf16[80,768]{1,0:T(8,128)(2,1)S(1)}, u32[]{:S(2)}, u32[]{:S(2)}) collective-permute-start(bf16[80,768]{1,0:T(8,128)(2,1)} %get-tuple-element.50), channel_id=1, source_target_pairs={{0,24},{8,32},{16,40},{24,48},{32,56},{40,0},{48,8},{56,16},{1,25}... | collective-permute-start | bytes 368648 | tf_op jit(solution)/shard_map/ppermute | solution.py:756
  70.3 0.5 collective-permute-start.6
  70.7 4.5 %collective-permute-start.7 = (bf16[80,768]{1,0:T(8,128)(2,1)}, bf16[80,768]{1,0:T(8,128)(2,1)S(1)}, u32[]{:S(2)}, u32[]{:S(2)}) collective-permute-start(bf16[80,768]{1,0:T(8,128)(2,1)} %get-tuple-element.52), channel_id=1, source_target_pairs={{0,40},{8,48},{16,56},{24,0},{32,8},{40,16},{48,24},{56,32},{1,41}... | collective-permute-start | bytes 368648 | tf_op jit(solution)/shard_map/ppermute | solution.py:756
  75.2 0.0 collective-permute-done.3.refs_1_
  75.2 2.4 %collective-permute-start.8 = (bf16[80,768]{1,0:T(8,128)(2,1)}, bf16[80,768]{1,0:T(8,128)(2,1)S(1)}, u32[]{:S(2)}, u32[]{:S(2)}) collective-permute-start(bf16[80,768]{1,0:T(8,128)(2,1)} %get-tuple-element.53), channel_id=1, source_target_pairs={{0,48},{8,56},{16,0},{24,8},{32,16},{40,24},{48,32},{56,40},{1,49}... | collective-permute-start | bytes 368648 | tf_op jit(solution)/shard_map/ppermute | solution.py:756
  77.6 0.0 collective-permute-done.4.refs_2_
  77.6 0.9 collective-permute-start.9
  78.4 7.8 %collective-permute-done.5.refs_3_ = bf16[80,768]{1,0:T(8,128)(2,1)S(1)} collective-permute-done((bf16[80,768]{1,0:T(8,128)(2,1)}, bf16[80,768]{1,0:T(8,128)(2,1)S(1)}, u32[]{:S(2)}, u32[]{:S(2)}) %collective-permute-start.5) | collective-permute-done | bytes 122912 | tf_op jit(solution)/shard_map/ppermute | solution.py:756
  86.3 0.0 collective-permute-done.6.refs_4_
  86.3 0.0 collective-permute-done.7.refs_5_
  86.3 7.9 %collective-permute-done.8.refs_6_ = bf16[80,768]{1,0:T(8,128)(2,1)S(1)} collective-permute-done((bf16[80,768]{1,0:T(8,128)(2,1)}, bf16[80,768]{1,0:T(8,128)(2,1)S(1)}, u32[]{:S(2)}, u32[]{:S(2)}) %collective-permute-start.8) | collective-permute-done | bytes 122912 | tf_op jit(solution)/shard_map/ppermute | solution.py:756
  94.1 0.9 collective-permute-done.9.refs_7_
  95.0 0.9 copy-done
  95.9 0.2 chunk.1
  96.1 0.0 all-to-all-done.a_ref
  96.2 1.1 half.1
  97.3 4.8 %all-to-all-start.1 = ((bf16[8,120,128]{2,1,0:T(8,128)(2,1)}), bf16[8,120,128]{2,1,0:T(8,128)(2,1)S(1)}, u32[]{:S(2)}, u32[]{:S(2)}) async-start(bf16[8,120,128]{2,1,0:T(8,128)(2,1)} %half.1), calls=%async_computation.1 | async-start | bytes 491520 | tf_op jit(solution)/shard_map/all_to_all | solution.py:761
  102.1 3.0 %collective-permute-start.10 = (bf16[4,16,768]{2,1,0:T(8,128)(2,1)S(1)}, bf16[4,16,768]{2,1,0:T(8,128)(2,1)S(1)}, u32[]{:S(2)}, u32[]{:S(2)}) collective-permute-start(bf16[4,16,768]{2,1,0:T(8,128)(2,1)S(1)} %get-tuple-element.58), channel_id=1, source_target_pairs={{0,4},{4,0},{1,5},{5,1},{2,6},{6,2},{3,7},{7,3},{8,12},{12,8},{9,1... | collective-permute-start | bytes 294920 | tf_op jit(solution)/shard_map/ppermute | solution.py:759
  105.1 2.0 %collective-permute-done.10.got_ref = bf16[4,16,768]{2,1,0:T(8,128)(2,1)S(1)} collective-permute-done((bf16[4,16,768]{2,1,0:T(8,128)(2,1)S(1)}, bf16[4,16,768]{2,1,0:T(8,128)(2,1)S(1)}, u32[]{:S(2)}, u32[]{:S(2)}) %collective-permute-start.10) | collective-permute-done | bytes 98336 | tf_op jit(solution)/shard_map/ppermute | solution.py:759
  107.1 1.5 %collective-permute-start.11 = (bf16[16,768]{1,0:T(8,128)(2,1)S(1)}, bf16[16,768]{1,0:T(8,128)(2,1)S(1)}, u32[]{:S(2)}, u32[]{:S(2)}) collective-permute-start(bf16[16,768]{1,0:T(8,128)(2,1)S(1)} %get-tuple-element.60), channel_id=1, source_target_pairs={{0,64},{64,128},{128,192},{192,0},{1,65},{65,129},{129,193},{193,1... | collective-permute-start | bytes 73736 | tf_op jit(solution)/shard_map/ppermute | solution.py:764
  108.6 2.4 %collective-permute-start.12 = (bf16[16,768]{1,0:T(8,128)(2,1)S(1)}, bf16[16,768]{1,0:T(8,128)(2,1)S(1)}, u32[]{:S(2)}, u32[]{:S(2)}) collective-permute-start(bf16[16,768]{1,0:T(8,128)(2,1)S(1)} %get-tuple-element.61), channel_id=1, source_target_pairs={{0,128},{64,192},{128,0},{192,64},{1,129},{65,193},{129,1},{193,65... | collective-permute-start | bytes 73736 | tf_op jit(solution)/shard_map/ppermute | solution.py:764
  111.0 1.2 collective-permute-start.13
  112.2 0.0 collective-permute-done.11.one_ref
  112.2 0.6 collective-permute-done.12.two_ref
  112.8 1.2 collective-permute-done.13.three_ref
  114.0 0.0 all-to-all-done.1.a_ref
  114.0 0.1 total.1
  114.1 9.3 %all-gather = f32[704,128]{1,0:T(8,128)S(1)} all-gather(f32[176,128]{1,0:T(8,128)S(1)} %get-tuple-element.63), channel_id=2, replica_groups=mesh['x'=4,'z'=8,'y_hi'=2,'y_lo'=2,'core'=2] {'y_lo','core'}, dimensions={0}, use_global_device_ids=true | all-gather | bytes 450560 | tf_op jit(solution)/shard_map/all_gather | solution.py:767
  123.3 0.9 unpack.1
  124.2 0.5 slice_bitcast_fusion
  (4 shorter events, 0.0 us)
Async XLA Ops:
  1.7 12.2 %copy-start.1 = (bf16[256,640]{1,0:T(8,128)(2,1)}, bf16[256,640]{1,0:T(8,128)(2,1)S(1)}, u32[]{:S(2)}) copy-start(bf16[256,640]{1,0:T(8,128)(2,1)S(1)} %pad_maximum_fusion.own_xt_ref) | copy-start | bytes 983044
  1.7 8.4 %collective-permute-start = (bf16[256,640]{1,0:T(8,128)(2,1)S(1)}, bf16[256,640]{1,0:T(8,128)(2,1)S(1)}, u32[]{:S(2)}, u32[]{:S(2)}) collective-permute-start(bf16[256,640]{1,0:T(8,128)(2,1)S(1)} %pad_maximum_fusion.own_xt_ref), channel_id=1, source_target_pairs={{0,2},{2,0},{1,3},{3,1},{4,6},{6,4},{5,7},{7,5},{8,10},{10,8},{9,1... | collective-permute-start | bytes 983048 | tf_op jit(solution)/shard_map/ppermute | solution.py:731
  3.9 10.0 %collective-permute-start.1 = (bf16[256,640]{1,0:T(8,128)(2,1)S(1)}, bf16[256,640]{1,0:T(8,128)(2,1)S(1)}, u32[]{:S(2)}, u32[]{:S(2)}) collective-permute-start(bf16[256,640]{1,0:T(8,128)(2,1)S(1)} %pad_maximum_fusion.own_xt_ref), channel_id=1, source_target_pairs={{0,1},{1,0},{2,3},{3,2},{4,5},{5,4},{6,7},{7,6},{8,9},{9,8},{10,11... | collective-permute-start | bytes 983048 | tf_op jit(solution)/shard_map/ppermute | solution.py:732
  10.1 3.8 %copy-start.2 = (bf16[256,640]{1,0:T(8,128)(2,1)}, bf16[256,640]{1,0:T(8,128)(2,1)S(1)}, u32[]{:S(2)}) copy-start(bf16[256,640]{1,0:T(8,128)(2,1)S(1)} %collective-permute-done.y_xt_ref) | copy-start | bytes 983044
  10.1 3.8 %collective-permute-start.2 = (bf16[256,640]{1,0:T(8,128)(2,1)S(1)}, bf16[256,640]{1,0:T(8,128)(2,1)S(1)}, u32[]{:S(2)}, u32[]{:S(2)}) collective-permute-start(bf16[256,640]{1,0:T(8,128)(2,1)S(1)} %collective-permute-done.y_xt_ref), channel_id=1, source_target_pairs={{0,1},{1,0},{2,3},{3,2},{4,5},{5,4},{6,7},{7,6},{8,9},{9,8},{10,11... | collective-permute-start | bytes 983048 | tf_op jit(solution)/shard_map/ppermute | solution.py:733
  13.9 0.7 copy-start.3
  13.9 0.9 copy-start.4
  41.8 54.3 %all-to-all-start = ((bf16[8,80,1536]{2,1,0:T(8,128)(2,1)}), bf16[8,80,1536]{2,1,0:T(8,128)(2,1)S(1)}, u32[]{:S(2)}, u32[]{:S(2)}) async-start(bf16[8,80,1536]{2,1,0:T(8,128)(2,1)} %bitcast.23), calls=%async_computation | async-start | bytes 3932160 | tf_op jit(solution)/shard_map/all_to_all | solution.py:751
  61.8 13.4 %collective-permute-start.3 = (bf16[80,768]{1,0:T(8,128)(2,1)}, bf16[80,768]{1,0:T(8,128)(2,1)S(1)}, u32[]{:S(2)}, u32[]{:S(2)}) collective-permute-start(bf16[80,768]{1,0:T(8,128)(2,1)} %get-tuple-element.48), channel_id=1, source_target_pairs={{0,8},{8,16},{16,24},{24,32},{32,40},{40,48},{48,56},{56,0},{1,9},... | collective-permute-start | bytes 368648 | tf_op jit(solution)/shard_map/ppermute | solution.py:756
  63.5 14.1 %collective-permute-start.4 = (bf16[80,768]{1,0:T(8,128)(2,1)}, bf16[80,768]{1,0:T(8,128)(2,1)S(1)}, u32[]{:S(2)}, u32[]{:S(2)}) collective-permute-start(bf16[80,768]{1,0:T(8,128)(2,1)} %get-tuple-element.49), channel_id=1, source_target_pairs={{0,16},{8,24},{16,32},{24,40},{32,48},{40,56},{48,0},{56,8},{1,17}... | collective-permute-start | bytes 368648 | tf_op jit(solution)/shard_map/ppermute | solution.py:756
  66.5 19.8 %collective-permute-start.5 = (bf16[80,768]{1,0:T(8,128)(2,1)}, bf16[80,768]{1,0:T(8,128)(2,1)S(1)}, u32[]{:S(2)}, u32[]{:S(2)}) collective-permute-start(bf16[80,768]{1,0:T(8,128)(2,1)} %get-tuple-element.50), channel_id=1, source_target_pairs={{0,24},{8,32},{16,40},{24,48},{32,56},{40,0},{48,8},{56,16},{1,25}... | collective-permute-start | bytes 368648 | tf_op jit(solution)/shard_map/ppermute | solution.py:756
  70.3 16.0 %collective-permute-start.6 = (bf16[80,768]{1,0:T(8,128)(2,1)}, bf16[80,768]{1,0:T(8,128)(2,1)S(1)}, u32[]{:S(2)}, u32[]{:S(2)}) collective-permute-start(bf16[80,768]{1,0:T(8,128)(2,1)} %get-tuple-element.51), channel_id=1, source_target_pairs={{0,32},{8,40},{16,48},{24,56},{32,0},{40,8},{48,16},{56,24},{1,33}... | collective-permute-start | bytes 368648 | tf_op jit(solution)/shard_map/ppermute | solution.py:756
  70.7 15.5 %collective-permute-start.7 = (bf16[80,768]{1,0:T(8,128)(2,1)}, bf16[80,768]{1,0:T(8,128)(2,1)S(1)}, u32[]{:S(2)}, u32[]{:S(2)}) collective-permute-start(bf16[80,768]{1,0:T(8,128)(2,1)} %get-tuple-element.52), channel_id=1, source_target_pairs={{0,40},{8,48},{16,56},{24,0},{32,8},{40,16},{48,24},{56,32},{1,41}... | collective-permute-start | bytes 368648 | tf_op jit(solution)/shard_map/ppermute | solution.py:756
  75.2 18.9 %collective-permute-start.8 = (bf16[80,768]{1,0:T(8,128)(2,1)}, bf16[80,768]{1,0:T(8,128)(2,1)S(1)}, u32[]{:S(2)}, u32[]{:S(2)}) collective-permute-start(bf16[80,768]{1,0:T(8,128)(2,1)} %get-tuple-element.53), channel_id=1, source_target_pairs={{0,48},{8,56},{16,0},{24,8},{32,16},{40,24},{48,32},{56,40},{1,49}... | collective-permute-start | bytes 368648 | tf_op jit(solution)/shard_map/ppermute | solution.py:756
  77.6 17.4 %collective-permute-start.9 = (bf16[80,768]{1,0:T(8,128)(2,1)}, bf16[80,768]{1,0:T(8,128)(2,1)S(1)}, u32[]{:S(2)}, u32[]{:S(2)}) collective-permute-start(bf16[80,768]{1,0:T(8,128)(2,1)} %get-tuple-element.54), channel_id=1, source_target_pairs={{0,56},{8,0},{16,8},{24,16},{32,24},{40,32},{48,40},{56,48},{1,57}... | collective-permute-start | bytes 368648 | tf_op jit(solution)/shard_map/ppermute | solution.py:756
  95.0 0.9 copy-start
  97.3 16.7 %all-to-all-start.1 = ((bf16[8,120,128]{2,1,0:T(8,128)(2,1)}), bf16[8,120,128]{2,1,0:T(8,128)(2,1)S(1)}, u32[]{:S(2)}, u32[]{:S(2)}) async-start(bf16[8,120,128]{2,1,0:T(8,128)(2,1)} %half.1), calls=%async_computation.1 | async-start | bytes 491520 | tf_op jit(solution)/shard_map/all_to_all | solution.py:761
  102.1 5.0 %collective-permute-start.10 = (bf16[4,16,768]{2,1,0:T(8,128)(2,1)S(1)}, bf16[4,16,768]{2,1,0:T(8,128)(2,1)S(1)}, u32[]{:S(2)}, u32[]{:S(2)}) collective-permute-start(bf16[4,16,768]{2,1,0:T(8,128)(2,1)S(1)} %get-tuple-element.58), channel_id=1, source_target_pairs={{0,4},{4,0},{1,5},{5,1},{2,6},{6,2},{3,7},{7,3},{8,12},{12,8},{9,1... | collective-permute-start | bytes 294920 | tf_op jit(solution)/shard_map/ppermute | solution.py:759
  107.1 5.1 %collective-permute-start.11 = (bf16[16,768]{1,0:T(8,128)(2,1)S(1)}, bf16[16,768]{1,0:T(8,128)(2,1)S(1)}, u32[]{:S(2)}, u32[]{:S(2)}) collective-permute-start(bf16[16,768]{1,0:T(8,128)(2,1)S(1)} %get-tuple-element.60), channel_id=1, source_target_pairs={{0,64},{64,128},{128,192},{192,0},{1,65},{65,129},{129,193},{193,1... | collective-permute-start | bytes 73736 | tf_op jit(solution)/shard_map/ppermute | solution.py:764
  108.6 4.2 %collective-permute-start.12 = (bf16[16,768]{1,0:T(8,128)(2,1)S(1)}, bf16[16,768]{1,0:T(8,128)(2,1)S(1)}, u32[]{:S(2)}, u32[]{:S(2)}) collective-permute-start(bf16[16,768]{1,0:T(8,128)(2,1)S(1)} %get-tuple-element.61), channel_id=1, source_target_pairs={{0,128},{64,192},{128,0},{192,64},{1,129},{65,193},{129,1},{193,65... | collective-permute-start | bytes 73736 | tf_op jit(solution)/shard_map/ppermute | solution.py:764
  111.0 3.0 %collective-permute-start.13 = (bf16[16,768]{1,0:T(8,128)(2,1)S(1)}, bf16[16,768]{1,0:T(8,128)(2,1)S(1)}, u32[]{:S(2)}, u32[]{:S(2)}) collective-permute-start(bf16[16,768]{1,0:T(8,128)(2,1)S(1)} %get-tuple-element.62), channel_id=1, source_target_pairs={{0,192},{64,0},{128,64},{192,128},{1,193},{65,1},{129,65},{193,129... | collective-permute-start | bytes 73736 | tf_op jit(solution)/shard_map/ppermute | solution.py:764

commit v6 on v3

--- a/solution.py
+++ b/solution.py
@@ -127,7 +127,7 @@
     cg_ref,
     own_ref,
     stat_ref,
-    margin_ref,
+    loss_ref,
     acat,
     acc,
     resid,
@@ -156,24 +156,13 @@
     load_time = pltpu.make_async_copy(timew_ref, timew_s, sems.at[3])
     load_qkv = pltpu.make_async_copy(qkvw_ref, qkvw_s, sems.at[4])
     load_out = pltpu.make_async_copy(outw_ref, outw_s, sems.at[5])
-    load_x, load_t = [], []
-    for i, (ref, way) in enumerate(
-        ((own_xt_ref, 0), (core_xt_ref, 1), (y_xt_ref, 2), (far_xt_ref, 3))
-    ):
-        rows = pl.ds(pl.multiple_of((part ^ way) * BAND, BAND), BAND)
-        load_x.append(
-            pltpu.make_async_copy(ref.at[pl.ds(0, BAND)], x_s.at[rows], sems.at[12 + i])
-        )
-        load_t.append(
-            pltpu.make_async_copy(ref.at[pl.ds(BAND, BAND)], t_s.at[rows], sems.at[16 + i])
-        )
-    for load in load_x:
-        load.start()
     taps[0].start()
     load_time.start()
     taps[1].start()
-    for load in load_x:
-        load.wait()
+    for ref, way in ((own_xt_ref, 0), (core_xt_ref, 1), (y_xt_ref, 2), (far_xt_ref, 3)):
+        rows = pl.ds(pl.multiple_of((part ^ way) * BAND, BAND), BAND)
+        x_s[rows, :] = ref[0:BAND, :]
+        t_s[rows, :] = ref[BAND : 2 * BAND, :]
     stores = [pltpu.make_async_copy(x_s, x_ref, sems.at[6])]
     sums, squares = [], []
     for m in range(2):
@@ -220,8 +209,6 @@
     resid[...] = (x_s[...].astype(f32) + acc[...] + offset).astype(bf16)
     load_qkv.wait()
     load_out.start()
-    for load in load_t:
-        load.start()
     for third in range(3):
         cols = pl.ds(third * C, C)
         proj = dot(resid[...], qkvw_s[:, cols]).astype(bf16)
@@ -242,8 +229,6 @@
                     r * COLS : (r + 1) * COLS
                 ]
     load_out.wait()
-    for load in load_t:
-        load.wait()
     dev[...] = (
         resid[...].astype(f32) + dot(attended[...], outw_s[...]) - t_s[...].astype(f32)
     )
@@ -258,7 +243,9 @@
         sign = jnp.where(label_ref[0] == m, 1.0, -1.0)
         signs.append(sign)
         margin = margin + sign * (error - error_ref[0, m])
-    margin_ref[...] = jnp.broadcast_to(margin, (8, 128))
+    twice = BETA * margin
+    loss = jnp.maximum(twice, 0.0) + jnp.log1p(jnp.exp(-jnp.abs(twice)))
+    loss_ref[0] = loss[0, 0]
     slope = BETA * sigmoid(BETA * margin)
     for r, m, at in blocks():
         here = pl.ds(at, COLS)
@@ -362,10 +349,10 @@
             jax.ShapeDtypeStruct((TOK, C), bf16),
             jax.ShapeDtypeStruct((BAND, C), f32),
             jax.ShapeDtypeStruct((8, C), f32),
-            jax.ShapeDtypeStruct((8, 128), f32),
+            jax.ShapeDtypeStruct((1,), f32),
         ),
         in_specs=[smem] * 4 + [vmem] * 4 + [hbm] + [vmem] * 2 + [hbm] * 3 + [vmem],
-        out_specs=[hbm] * 4 + [vmem] * 2,
+        out_specs=[hbm] * 4 + [vmem, smem],
         scratch_shapes=[
             pltpu.VMEM((TOK + 2 * BAND, 3 * C), bf16),
             pltpu.VMEM((TOK, C), f32),
@@ -388,7 +375,7 @@
             pltpu.VMEM((C, 3 * C), bf16),
             pltpu.VMEM((C, C), bf16),
             pltpu.VMEM((TDIM, C), bf16),
-            pltpu.SemaphoreType.DMA((20,)),
+            pltpu.SemaphoreType.DMA((12,)),
         ],
         compiler_params=pltpu.CompilerParams(vmem_limit_bytes=LIMIT * MIB),
         name="pair",
@@ -412,35 +399,71 @@
 
 
 def input_kernel(
-    part_ref, x_ref, cg_ref, own_ref, stat_ref, gain_ref, conv_ref, in_ref, gg_ref, gcat, acc
+    part_ref,
+    stat_ref,
+    gain_ref,
+    cg_ref,
+    x_ref,
+    own_ref,
+    conv_ref,
+    in_ref,
+    sum_ref,
+    gcat,
+    acc,
+    cg_s,
+    x_s,
+    own_s,
+    conv_s,
+    sems,
 ):
     part = part_ref[0]
+    load_cg = pltpu.make_async_copy(cg_ref, cg_s, sems.at[0])
+    taps = [pltpu.make_async_copy(conv_ref.at[i], conv_s.at[i], sems.at[1 + i]) for i in range(3)]
+    rest = [
+        pltpu.make_async_copy(ref, to, sems.at[4 + i])
+        for i, (ref, to) in enumerate(((x_ref, x_s), (own_ref, own_s)))
+    ]
+    load_cg.start()
+    taps[0].start()
     gcat[0:BAND, :] = jnp.zeros((BAND, 3 * C), bf16)
     gcat[pl.ds(BAND + TOK, BAND), :] = jnp.zeros((BAND, 3 * C), bf16)
+    load_cg.wait()
+    taps[1].start()
+    bias_sum = jnp.zeros((1, C), f32)
     for r, m, at in blocks():
-        g = cg_ref[pl.ds(at, COLS), :]
+        g = cg_s[pl.ds(at, COLS), :]
+        wide = g.astype(f32)
+        bias_sum = bias_sum + jnp.sum(wide, axis=0, keepdims=True)
         here = pl.ds(BAND + at, COLS)
-        gcat[here, 0:C] = shifted(g.astype(f32), -1).astype(bf16)
+        gcat[here, 0:C] = shifted(wide, -1).astype(bf16)
         gcat[here, C : 2 * C] = g
-        gcat[here, 2 * C : 3 * C] = shifted(g.astype(f32), 1).astype(bf16)
+        gcat[here, 2 * C : 3 * C] = shifted(wide, 1).astype(bf16)
     for i in range(3):
+        taps[i].wait()
+        if i == 0:
+            taps[2].start()
+            rest[0].start()
+        if i == 1:
+            rest[1].start()
         for j in range(3):
             term = dot(
                 gcat[pl.ds((2 - i) * BAND, TOK), j * C : (j + 1) * C],
-                conv_ref[i, j * C : (j + 1) * C, :],
+                conv_s[i, j * C : (j + 1) * C, :],
                 NT,
             )
             if i == 0 and j == 0:
                 acc[...] = term
             else:
                 acc[...] += term
+    for load in rest:
+        load.wait()
     gain = gain_ref[...].reshape(1, C)
     gain_sum = jnp.zeros((1, C), f32)
     ones = [jnp.zeros((1, C), f32) for _ in range(2)]
     twos = [jnp.zeros((1, C), f32) for _ in range(2)]
     for r, m, at in blocks():
         here = pl.ds(at, COLS)
-        normed = (x_ref[here, :].astype(f32) - stat_ref[row(m), :]) * stat_ref[row(2 + m), :]
+        normed = (x_s[here, :].astype(f32) - stat_ref[row(m), :]) * stat_ref[row(2 + m), :]
         a = normed * gain
         s = sigmoid(a)
         pre = acc[here, :] * (s * (1.0 + a * (1.0 - s)))
@@ -449,39 +472,44 @@
         acc[here, :] = scaled
         ones[m] = ones[m] + jnp.sum(scaled, axis=0, keepdims=True)
         twos[m] = twos[m] + jnp.sum(scaled * normed, axis=0, keepdims=True)
-    bias_sum = jnp.sum(cg_ref[...].astype(f32), axis=0, keepdims=True)
-    gg_ref[...] = jnp.concatenate([gain_sum, bias_sum], axis=0)
+    sum_ref[...] = jnp.concatenate([gain_sum, bias_sum], axis=0)
     means = group_sums(jnp.concatenate(ones + twos, axis=0)) / GROUP_COUNT
     for m in range(2):
         here = pl.ds(pl.multiple_of(part * BAND + m * COLS, COLS), COLS)
         inv = stat_ref[row(2 + m), :]
-        normed = (x_ref[here, :].astype(f32) - stat_ref[row(m), :]) * inv
+        normed = (x_s[here, :].astype(f32) - stat_ref[row(m), :]) * inv
         inner = inv * (acc[here, :] - means[m : m + 1] - normed * means[2 + m : 3 + m])
         mine = slice(m * COLS, (m + 1) * COLS)
-        in_ref[mine, :] = (own_ref[mine, :] + inner).astype(bf16)
-
-
-def input_call(part, x, cg, own, stat, gain, conv):
+        in_ref[mine, :] = (own_s[mine, :] + inner).astype(bf16)
+
+
+def input_call(part, stat, gain, cg, x, own, conv):
     smem = pl.BlockSpec(memory_space=pltpu.SMEM)
     vmem = pl.BlockSpec(memory_space=pltpu.VMEM)
+    hbm = pl.BlockSpec(memory_space=pltpu.HBM)
     return pl.pallas_call(
         input_kernel,
         out_shape=(
             jax.ShapeDtypeStruct((BAND, C), bf16),
             jax.ShapeDtypeStruct((2, C), f32),
         ),
-        in_specs=[smem] + [vmem] * 6,
+        in_specs=[smem] + [vmem] * 2 + [hbm] * 4,
         out_specs=[vmem] * 2,
         scratch_shapes=[
             pltpu.VMEM((TOK + 2 * BAND, 3 * C), bf16),
             pltpu.VMEM((TOK, C), f32),
+            pltpu.VMEM((TOK, C), bf16),
+            pltpu.VMEM((TOK, C), bf16),
+            pltpu.VMEM((BAND, C), f32),
+            pltpu.VMEM((3, 3 * C, C), bf16),
+            pltpu.SemaphoreType.DMA((6,)),
         ],
-        compiler_params=pltpu.CompilerParams(vmem_limit_bytes=40 * MIB),
+        compiler_params=pltpu.CompilerParams(vmem_limit_bytes=LIMIT * MIB),
         cost_estimate=pl.CostEstimate(
-            flops=2 * TOK * 9 * C * C, bytes_accessed=9 * C * C * 2, transcendentals=TOK * C
+            flops=2 * TOK * 10 * C * C, bytes_accessed=9 * C * C * 2, transcendentals=TOK * C
         ),
         name="input",
-    )(part, x, cg, own, stat, gain, conv)
+    )(part, stat, gain, cg, x, own, conv)
 
 
 def half_kernel(a_ref, out_ref, acc, mid):
@@ -591,7 +619,7 @@
     core = lax.ppermute(own_xt, "core", swap)
     far = lax.ppermute(near, "core", swap)
     conv = conv_weight.reshape(3, 3 * C, C)
-    wire, x, cg, own, stat, margin = pair_call(
+    wire, x, cg, own, stat, pair_loss = pair_call(
         part,
         timesteps,
         labels,
@@ -608,18 +636,18 @@
         time_weight,
     )
     moved = lax.all_to_all(wire.reshape(8, 80, WIDTH), ("x", "y_hi"), 0, 0)
-    input_grad, gains = input_call(part, x, cg, own, stat, norm_gain, conv)
+    input_grad, gains = input_call(part, stat, norm_gain, cg, x, own, conv)
     gains = lax.psum(gains, "z")
+    gains = gains + lax.ppermute(gains, "y_hi", swap)
     moved, gains = lax.optimization_barrier((moved, gains))
     half, gains = lax.optimization_barrier((half_call(moved), gains))
     moved = lax.all_to_all(half, "z", 0, 0)
-    gains = gains + lax.ppermute(gains, "y_hi", swap)
     gains = gains + lax.ppermute(gains, "x", [(0, 1), (1, 0), (2, 3), (3, 2)])
+    total, gains = lax.optimization_barrier((total_call(moved), gains))
     gains = gains + lax.ppermute(gains, "x", [(0, 3), (3, 0), (1, 2), (2, 1)])
     gains = lax.dynamic_slice_in_dim(gains, lax.axis_index(PAIR_AXES) * OWN, OWN, 1)
-    whole = lax.all_gather(total_call(moved), SPACE_AXES, axis=0, tiled=False)
+    whole = lax.all_gather(total, SPACE_AXES, axis=0, tiled=False)
     conv_out, qkv_out, out_out, time_out = unpack_call(whole)
-    pair_loss = jax.nn.softplus(BETA * margin[0, 0:1])
     return (
         input_grad.reshape(section_input.shape),
         conv_out.transpose(0, 2, 3, 1),

time: 126 us -> 124 us (0.984)
  local copies, waits for them, and re-layouts: 7.7 us -> 1.36 us
  waiting for transfers between devices: 21.6 us -> 25.7 us
  between operations: 3.96 us -> 2.04 us
  Pallas kernels: 39.7 us -> 41.4 us
    all_to_all x1, waiting for transfers between devices: 0.42 us -> 9.27 us  [on_device(): moved = lax.all_to_all(half, 'z', 0, 0)]
    unnamed x20 -> x8, local copies, waits for them, and re-layouts: 5.98 us -> 0.83 us
    pallas_call x1, Pallas kernels: 7.15 us -> 10.7 us  [input_call(): pl.pallas_call(input_kernel, out_shape=(jax.ShapeDtypeStruct((BAND, C), b...]
    all_to_all x1, waiting for transfers between devices: 10.3 us -> 6.91 us  [on_device(): moved = lax.all_to_all(wire.reshape(8, 80, WIDTH), ('x', 'y_hi'), 0, 0)]
    pallas_call x1, Pallas kernels: 30.2 us -> 28.3 us  [pair_call(): pl.pallas_call(pair_kernel, out_shape=(jax.ShapeDtypeStruct((C, WIDTH), b...]
    ppermute x1, waiting for transfers between devices: 1.44 us -> 0.01 us  [on_device(): gains = gains + lax.ppermute(gains, 'x', [(0, 3), (3, 0), (1, 2), (2, 1)])]
  transfers between devices with their start and end apart: 8 -> 8, of which waited for: 6 -> 5; matrix products, arithmetic and copies ran while one was open for 1% -> 0% of each run, Pallas kernels for 6% -> 9%
where the time goes in v6:
time: 124 us; the launch traced here: 123 us
  Pallas kernels  41.4 us (33%)
  blocking collectives  27.2 us (22%)
  waiting for transfers between devices  25.7 us (21%)
  starting transfers between devices  24.3 us (20%)
  between operations  2.04 us (2%)
  local copies, waits for them, and re-layouts  1.36 us (1%)
    pallas_call x1, Pallas kernels, pair_call(): pl.pallas_call(pair_kernel, out_shape=(jax.ShapeDtypeStruct((C, WIDTH), b...  28.3 us
    psum x1, blocking collectives, on_device(): gains = lax.psum(gains, 'z')  17.8 us
    pallas_call x1, Pallas kernels, input_call(): pl.pallas_call(input_kernel, out_shape=(jax.ShapeDtypeStruct((BAND, C), b...  10.7 us
    all_gather x1, blocking collectives, on_device(): whole = lax.all_gather(total, SPACE_AXES, axis=0, tiled=False)  9.36 us
    all_to_all x1, waiting for transfers between devices, on_device(): moved = lax.all_to_all(half, 'z', 0, 0)  9.27 us
    all_to_all x1, starting transfers between devices, on_device(): moved = lax.all_to_all(half, 'z', 0, 0)  8.18 us
    all_to_all x1, waiting for transfers between devices, on_device(): moved = lax.all_to_all(wire.reshape(8, 80, WIDTH), ('x', 'y_hi'), 0, 0)  6.91 us
    all_to_all x1, starting transfers between devices, on_device(): moved = lax.all_to_all(wire.reshape(8, 80, WIDTH), ('x', 'y_hi'), 0, 0)  6.83 us
  transfers between devices with their start and end apart: 8, of which 5 were waited for; matrix products, arithmetic and copies ran while one was open for 0% of the time, Pallas kernels for 9%

profile of v6, /device:TPU:1, one launch (start us, length us, event | category | flops | bytes accessed | tf_op | source)
XLA Modules:
  0.0 123.1 jit_solution(8637402319968315080)
XLA Ops:
  0.6 1.0 pad_maximum_fusion.own_xt_ref
  1.7 0.0 copy-start
  1.7 2.2 %collective-permute-start = (bf16[256,640]{1,0:T(8,128)(2,1)S(1)}, bf16[256,640]{1,0:T(8,128)(2,1)S(1)}, u32[]{:S(2)}, u32[]{:S(2)}) collective-permute-start(bf16[256,640]{1,0:T(8,128)(2,1)S(1)} %pad_maximum_fusion.own_xt_ref), channel_id=1, source_target_pairs={{0,2},{2,0},{1,3},{3,1},{4,6},{6,4},{5,7},{7,5},{8,10},{10,8},{9,1... | collective-permute-start | bytes 983048 | tf_op jit(solution)/shard_map/ppermute | solution.py:618
  3.9 1.2 collective-permute-start.1
  5.1 5.0 %collective-permute-done.y_xt_ref = bf16[256,640]{1,0:T(8,128)(2,1)S(1)} collective-permute-done((bf16[256,640]{1,0:T(8,128)(2,1)S(1)}, bf16[256,640]{1,0:T(8,128)(2,1)S(1)}, u32[]{:S(2)}, u32[]{:S(2)}) %collective-permute-start) | collective-permute-done | bytes 327712 | tf_op jit(solution)/shard_map/ppermute | solution.py:618
  10.1 0.0 copy-start.1
  10.1 2.5 %collective-permute-start.2 = (bf16[256,640]{1,0:T(8,128)(2,1)S(1)}, bf16[256,640]{1,0:T(8,128)(2,1)S(1)}, u32[]{:S(2)}, u32[]{:S(2)}) collective-permute-start(bf16[256,640]{1,0:T(8,128)(2,1)S(1)} %collective-permute-done.y_xt_ref), channel_id=1, source_target_pairs={{0,1},{1,0},{2,3},{3,2},{4,5},{5,4},{6,7},{7,6},{8,9},{9,8},{10,11... | collective-permute-start | bytes 983048 | tf_op jit(solution)/shard_map/ppermute | solution.py:620
  13.9 0.0 collective-permute-done.1.core_xt_ref
  13.9 0.0 copy-start.2
  13.9 0.0 collective-permute-done.2.far_xt_ref
  13.9 0.0 copy-start.3
  13.9 0.0 copy-done
  13.9 0.0 copy-done.1
  13.9 0.7 copy-done.2
  14.6 0.1 copy-done.3
  14.7 28.3 %pair.1 = (bf16[640,2176]{1,0:T(8,128)(2,1)}, bf16[512,640]{1,0:T(8,128)(2,1)}, bf16[512,640]{1,0:T(8,128)(2,1)}, f32[128,640]{1,0:T(8,128)}, f32[8,640]{1,0:T(8,128)}, /*index=5*/f32[1]{0:T(128)}) custom-call(s32[1]{0:T(128)} %bitcast.part_ref, s32[1]{0:T(128)S(6)} %copy.21.step_ref, s32[1]{0:T(128)S(6)} %copy.22.label_ref, f32[1,2]{1,0:T(1,128)} %error_ref.1, ...), custom_call_target="tpu_custom_call" | custom-call | tf_op jit(solution)/shard_map/pair/pallas_call | solution.py:344
  43.1 6.8 %all-to-all-start = ((bf16[8,80,2176]{2,1,0:T(8,128)(2,1)}), bf16[8,80,2176]{2,1,0:T(8,128)(2,1)S(1)}, u32[]{:S(2)}, u32[]{:S(2)}) async-start(bf16[8,80,2176]{2,1,0:T(8,128)(2,1)} %bitcast.20), calls=%async_computation | async-start | bytes 5570560 | tf_op jit(solution)/shard_map/all_to_all | solution.py:638
  49.9 10.7 %input.1 = (bf16[128,640]{1,0:T(8,128)(2,1)}, f32[2,640]{1,0:T(2,128)}) custom-call(s32[1]{0:T(128)} %bitcast.part_ref, f32[8,640]{1,0:T(8,128)} %get-tuple-element.26.stat_ref, f32[640]{0:T(1024)} %gain_ref.3, bf16[512,640]{1,0:T(8,128)(2,1)} %get-tuple-element.27.cg_ref, bf16[512,640]{1,0:T(8,128)(2,1)} %get-tuple-element.28.x_ref, ...), custom_call_target="tpu_custom_call" | custom-call | flops 4194304000 | bytes 7372800 | tf_op jit(solution)/shard_map/input/pallas_call | solution.py:490
  60.6 17.8 %psum.7 = f32[2,640]{1,0:T(2,128)S(1)} all-reduce(f32[2,640]{1,0:T(2,128)} %get-tuple-element.32), channel_id=1, replica_groups=mesh['x'=4,'z'=8,'y_hi'=2,'y_lo'=2,'core'=2] {'z'}, use_global_device_ids=true, to_apply=%region_0.0 | all-reduce | flops 1280 | bytes 10240 | tf_op jit(solution)/shard_map/psum | solution.py:640
  78.4 2.7 %collective-permute-start.3 = (f32[2,640]{1,0:T(2,128)S(1)}, f32[2,640]{1,0:T(2,128)S(1)}, u32[]{:S(2)}, u32[]{:S(2)}) collective-permute-start(f32[2,640]{1,0:T(2,128)S(1)} %psum.7), channel_id=1, source_target_pairs={{0,4},{4,0},{1,5},{5,1},{2,6},{6,2},{3,7},{7,3},{8,12},{12,8},{9,1... | collective-permute-start | bytes 15368 | tf_op jit(solution)/shard_map/ppermute | solution.py:641
  81.1 2.1 %collective-permute-done.3 = f32[2,640]{1,0:T(2,128)S(1)} collective-permute-done((f32[2,640]{1,0:T(2,128)S(1)}, f32[2,640]{1,0:T(2,128)S(1)}, u32[]{:S(2)}, u32[]{:S(2)}) %collective-permute-start.3) | collective-permute-done | bytes 5152 | tf_op jit(solution)/shard_map/ppermute | solution.py:641
  83.3 6.9 %all-to-all-done.a_ref = bf16[8,80,2176]{2,1,0:T(8,128)(2,1)S(1)} async-done(((bf16[8,80,2176]{2,1,0:T(8,128)(2,1)}), bf16[8,80,2176]{2,1,0:T(8,128)(2,1)S(1)}, u32[]{:S(2)}, u32[]{:S(2)}) %all-to-all-start) | async-done | bytes 2785312 | tf_op jit(solution)/shard_map/all_to_all | solution.py:638
  90.2 1.4 %half.1 = bf16[8,176,128]{2,1,0:T(8,128)(2,1)} custom-call(bf16[8,80,2176]{2,1,0:T(8,128)(2,1)S(1)} %all-to-all-done.a_ref), custom_call_target="tpu_custom_call" | custom-call | tf_op jit(solution)/shard_map/half/pallas_call | solution.py:531
  91.6 8.2 %all-to-all-start.1 = ((bf16[8,176,128]{2,1,0:T(8,128)(2,1)}), bf16[8,176,128]{2,1,0:T(8,128)(2,1)S(1)}, u32[]{:S(2)}, u32[]{:S(2)}) async-start(bf16[8,176,128]{2,1,0:T(8,128)(2,1)} %half.1), calls=%async_computation.1 | async-start | bytes 720896 | tf_op jit(solution)/shard_map/all_to_all | solution.py:644
  99.8 0.0 collective-permute-start.4
  99.8 2.5 %collective-permute-done.4 = f32[2,640]{1,0:T(2,128)S(1)} collective-permute-done((f32[2,640]{1,0:T(2,128)S(1)}, f32[2,640]{1,0:T(2,128)S(1)}, u32[]{:S(2)}, u32[]{:S(2)}) %collective-permute-start.4) | collective-permute-done | bytes 5152 | tf_op jit(solution)/shard_map/ppermute | solution.py:645
  102.2 9.3 %all-to-all-done.1.a_ref = bf16[8,176,128]{2,1,0:T(8,128)(2,1)S(1)} async-done(((bf16[8,176,128]{2,1,0:T(8,128)(2,1)}), bf16[8,176,128]{2,1,0:T(8,128)(2,1)S(1)}, u32[]{:S(2)}, u32[]{:S(2)}) %all-to-all-start.1) | async-done | bytes 360480 | tf_op jit(solution)/shard_map/all_to_all | solution.py:644
  111.6 0.7 collective-permute-start.5
  112.2 9.4 %all-gather = f32[704,128]{1,0:T(8,128)S(1)} all-gather(f32[176,128]{1,0:T(8,128)S(1)} %total.1), channel_id=2, replica_groups=mesh['x'=4,'z'=8,'y_hi'=2,'y_lo'=2,'core'=2] {'y_lo','core'}, dimensions={0}, use_global_device_ids=true | all-gather | bytes 450560 | tf_op jit(solution)/shard_map/all_gather | solution.py:649
  121.6 0.9 unpack.1
  122.5 0.0 collective-permute-done.5
  122.5 0.1 dynamic-slice_add_fusion
  122.6 0.5 slice_bitcast_fusion
  (3 shorter events, 0.1 us)
Async XLA Ops:
  1.7 12.2 %copy-start = (bf16[256,640]{1,0:T(8,128)(2,1)}, bf16[256,640]{1,0:T(8,128)(2,1)S(1)}, u32[]{:S(2)}) copy-start(bf16[256,640]{1,0:T(8,128)(2,1)S(1)} %pad_maximum_fusion.own_xt_ref) | copy-start | bytes 983044
  1.7 8.4 %collective-permute-start = (bf16[256,640]{1,0:T(8,128)(2,1)S(1)}, bf16[256,640]{1,0:T(8,128)(2,1)S(1)}, u32[]{:S(2)}, u32[]{:S(2)}) collective-permute-start(bf16[256,640]{1,0:T(8,128)(2,1)S(1)} %pad_maximum_fusion.own_xt_ref), channel_id=1, source_target_pairs={{0,2},{2,0},{1,3},{3,1},{4,6},{6,4},{5,7},{7,5},{8,10},{10,8},{9,1... | collective-permute-start | bytes 983048 | tf_op jit(solution)/shard_map/ppermute | solution.py:618
  3.9 10.0 %collective-permute-start.1 = (bf16[256,640]{1,0:T(8,128)(2,1)S(1)}, bf16[256,640]{1,0:T(8,128)(2,1)S(1)}, u32[]{:S(2)}, u32[]{:S(2)}) collective-permute-start(bf16[256,640]{1,0:T(8,128)(2,1)S(1)} %pad_maximum_fusion.own_xt_ref), channel_id=1, source_target_pairs={{0,1},{1,0},{2,3},{3,2},{4,5},{5,4},{6,7},{7,6},{8,9},{9,8},{10,11... | collective-permute-start | bytes 983048 | tf_op jit(solution)/shard_map/ppermute | solution.py:619
  10.1 3.8 %copy-start.1 = (bf16[256,640]{1,0:T(8,128)(2,1)}, bf16[256,640]{1,0:T(8,128)(2,1)S(1)}, u32[]{:S(2)}) copy-start(bf16[256,640]{1,0:T(8,128)(2,1)S(1)} %collective-permute-done.y_xt_ref) | copy-start | bytes 983044
  10.1 3.8 %collective-permute-start.2 = (bf16[256,640]{1,0:T(8,128)(2,1)S(1)}, bf16[256,640]{1,0:T(8,128)(2,1)S(1)}, u32[]{:S(2)}, u32[]{:S(2)}) collective-permute-start(bf16[256,640]{1,0:T(8,128)(2,1)S(1)} %collective-permute-done.y_xt_ref), channel_id=1, source_target_pairs={{0,1},{1,0},{2,3},{3,2},{4,5},{5,4},{6,7},{7,6},{8,9},{9,8},{10,11... | collective-permute-start | bytes 983048 | tf_op jit(solution)/shard_map/ppermute | solution.py:620
  13.9 0.7 copy-start.2
  13.9 0.8 copy-start.3
  43.1 47.1 %all-to-all-start = ((bf16[8,80,2176]{2,1,0:T(8,128)(2,1)}), bf16[8,80,2176]{2,1,0:T(8,128)(2,1)S(1)}, u32[]{:S(2)}, u32[]{:S(2)}) async-start(bf16[8,80,2176]{2,1,0:T(8,128)(2,1)} %bitcast.20), calls=%async_computation | async-start | bytes 5570560 | tf_op jit(solution)/shard_map/all_to_all | solution.py:638
  78.4 4.9 %collective-permute-start.3 = (f32[2,640]{1,0:T(2,128)S(1)}, f32[2,640]{1,0:T(2,128)S(1)}, u32[]{:S(2)}, u32[]{:S(2)}) collective-permute-start(f32[2,640]{1,0:T(2,128)S(1)} %psum.7), channel_id=1, source_target_pairs={{0,4},{4,0},{1,5},{5,1},{2,6},{6,2},{3,7},{7,3},{8,12},{12,8},{9,1... | collective-permute-start | bytes 15368 | tf_op jit(solution)/shard_map/ppermute | solution.py:641
  91.6 19.9 %all-to-all-start.1 = ((bf16[8,176,128]{2,1,0:T(8,128)(2,1)}), bf16[8,176,128]{2,1,0:T(8,128)(2,1)S(1)}, u32[]{:S(2)}, u32[]{:S(2)}) async-start(bf16[8,176,128]{2,1,0:T(8,128)(2,1)} %half.1), calls=%async_computation.1 | async-start | bytes 720896 | tf_op jit(solution)/shard_map/all_to_all | solution.py:644
  99.8 2.5 %collective-permute-start.4 = (f32[2,640]{1,0:T(2,128)S(1)}, f32[2,640]{1,0:T(2,128)S(1)}, u32[]{:S(2)}, u32[]{:S(2)}) collective-permute-start(f32[2,640]{1,0:T(2,128)S(1)} %add.24), channel_id=1, source_target_pairs={{0,64},{64,0},{128,192},{192,128},{1,65},{65,1},{129,193},{193,129... | collective-permute-start | bytes 15368 | tf_op jit(solution)/shard_map/ppermute | solution.py:645
  111.6 10.9 %collective-permute-start.5 = (f32[2,640]{1,0:T(2,128)S(1)}, f32[2,640]{1,0:T(2,128)S(1)}, u32[]{:S(2)}, u32[]{:S(2)}) collective-permute-start(f32[2,640]{1,0:T(2,128)S(1)} %add.25), channel_id=1, source_target_pairs={{0,192},{192,0},{64,128},{128,64},{1,193},{193,1},{65,129},{129,65... | collective-permute-start | bytes 15368 | tf_op jit(solution)/shard_map/ppermute | solution.py:647

commit v7 on v6

--- a/solution.py
+++ b/solution.py
@@ -111,10 +111,14 @@
     step_ref,
     label_ref,
     error_ref,
-    own_xt_ref,
-    y_xt_ref,
-    core_xt_ref,
-    far_xt_ref,
+    own_x_ref,
+    y_x_ref,
+    core_x_ref,
+    far_x_ref,
+    own_t_ref,
+    y_t_ref,
+    core_t_ref,
+    far_t_ref,
     conv_ref,
     bias_ref,
     gain_ref,
@@ -159,10 +163,12 @@
     taps[0].start()
     load_time.start()
     taps[1].start()
-    for ref, way in ((own_xt_ref, 0), (core_xt_ref, 1), (y_xt_ref, 2), (far_xt_ref, 3)):
+    x_refs = (own_x_ref, core_x_ref, y_x_ref, far_x_ref)
+    t_refs = (own_t_ref, core_t_ref, y_t_ref, far_t_ref)
+    for way in range(4):
         rows = pl.ds(pl.multiple_of((part ^ way) * BAND, BAND), BAND)
-        x_s[rows, :] = ref[0:BAND, :]
-        t_s[rows, :] = ref[BAND : 2 * BAND, :]
+        x_s[rows, :] = x_refs[way][...]
+        t_s[rows, :] = t_refs[way][...]
     stores = [pltpu.make_async_copy(x_s, x_ref, sems.at[6])]
     sums, squares = [], []
     for m in range(2):
@@ -337,7 +343,7 @@
         each.wait()
 
 
-def pair_call(part, steps, labels, errors, own, near, core, far, conv, bias, gain, qkvw, outw, timew):
+def pair_call(part, steps, labels, errors, rows, conv, bias, gain, qkvw, outw, timew):
     smem = pl.BlockSpec(memory_space=pltpu.SMEM)
     vmem = pl.BlockSpec(memory_space=pltpu.VMEM)
     hbm = pl.BlockSpec(memory_space=pl.ANY)
@@ -351,7 +357,7 @@
             jax.ShapeDtypeStruct((8, C), f32),
             jax.ShapeDtypeStruct((1,), f32),
         ),
-        in_specs=[smem] * 4 + [vmem] * 4 + [hbm] + [vmem] * 2 + [hbm] * 3 + [vmem],
+        in_specs=[smem] * 4 + [vmem] * 8 + [hbm] + [vmem] * 2 + [hbm] * 3 + [vmem],
         out_specs=[hbm] * 4 + [vmem, smem],
         scratch_shapes=[
             pltpu.VMEM((TOK + 2 * BAND, 3 * C), bf16),
@@ -384,10 +390,7 @@
         steps,
         labels,
         errors,
-        own,
-        near,
-        core,
-        far,
+        *rows,
         conv,
         bias,
         gain,
@@ -546,14 +549,14 @@
     total = a_ref[0].astype(f32)
     for i in range(1, 8):
         total = total + a_ref[i].astype(f32)
-    out_ref[...] = total
+    out_ref[...] = total.astype(bf16)
 
 
 def total_call(a):
     vmem = pl.BlockSpec(memory_space=pltpu.VMEM)
     return pl.pallas_call(
         total_kernel,
-        out_shape=jax.ShapeDtypeStruct((CHUNK, 128), f32),
+        out_shape=jax.ShapeDtypeStruct((CHUNK, 128), bf16),
         in_specs=[vmem],
         out_specs=vmem,
         compiler_params=pltpu.CompilerParams(vmem_limit_bytes=16 * MIB),
@@ -563,15 +566,16 @@
 
 def unpack_kernel(all_ref, conv_ref, qkv_ref, out_ref, time_ref):
     for part in range(4):
+        whole = all_ref[part].astype(f32)
         for k in range(5):
-            rows = all_ref[part, OWN * k : OWN * (k + 1), :]
+            rows = whole[OWN * k : OWN * (k + 1), :]
             cols = slice(128 * k, 128 * (k + 1))
             if part < 3:
                 qkv_ref[OWN * part : OWN * (part + 1), cols] = rows
             else:
                 out_ref[:, cols] = rows
         for k in range(TAP_BLOCKS):
-            rows = all_ref[part, OWN * (5 + k) : OWN * (6 + k), :]
+            rows = whole[OWN * (5 + k) : OWN * (6 + k), :]
             place = part * TAP_BLOCKS + k
             tap, block = place // 5, place % 5
             if place < 45:
@@ -614,20 +618,21 @@
 ):
     part = lax.axis_index(SPACE_AXES).astype(jnp.int32).reshape(1)
     swap = [(0, 1), (1, 0)]
-    own_xt = jnp.concatenate([section_input.reshape(BAND, C), target.reshape(BAND, C)], axis=0)
-    near = lax.ppermute(own_xt, "y_lo", swap)
-    core = lax.ppermute(own_xt, "core", swap)
-    far = lax.ppermute(near, "core", swap)
+    own_x, own_t = section_input.reshape(BAND, C), target.reshape(BAND, C)
+    near_x = lax.ppermute(own_x, "y_lo", swap)
+    near_t = lax.ppermute(own_t, "y_lo", swap)
+    core_x = lax.ppermute(own_x, "core", swap)
+    core_t = lax.ppermute(own_t, "core", swap)
+    far_x = lax.ppermute(near_x, "core", swap)
+    far_t = lax.ppermute(near_t, "core", swap)
+    rows = (own_x, near_x, core_x, far_x, own_t, near_t, core_t, far_t)
     conv = conv_weight.reshape(3, 3 * C, C)
     wire, x, cg, own, stat, pair_loss = pair_call(
         part,
         timesteps,
         labels,
         ref_error,
-        own_xt,
-        near,
-        core,
-        far,
+        rows,
         conv,
         conv_bias,
         norm_gain,
@@ -643,10 +648,10 @@
     half, gains = lax.optimization_barrier((half_call(moved), gains))
     moved = lax.all_to_all(half, "z", 0, 0)
     gains = gains + lax.ppermute(gains, "x", [(0, 1), (1, 0), (2, 3), (3, 2)])
-    total, gains = lax.optimization_barrier((total_call(moved), gains))
     gains = gains + lax.ppermute(gains, "x", [(0, 3), (3, 0), (1, 2), (2, 1)])
     gains = lax.dynamic_slice_in_dim(gains, lax.axis_index(PAIR_AXES) * OWN, OWN, 1)
-    whole = lax.all_gather(total, SPACE_AXES, axis=0, tiled=False)
+    moved, gains = lax.optimization_barrier((moved, gains))
+    whole = lax.all_gather(total_call(moved), SPACE_AXES, axis=0, tiled=False)
     conv_out, qkv_out, out_out, time_out = unpack_call(whole)
     return (
         input_grad.reshape(section_input.shape),

time: 124 us -> 121 us (0.976)
  starting transfers between devices: 24.3 us -> 29.6 us
  waiting for transfers between devices: 25.7 us -> 20.4 us
    ppermute x3 -> x6, starting transfers between devices: 5.91 us -> 11.1 us  [the longest x1 3.97 us: on_device(): far_x = lax.ppermute(near_x, 'core', swap)]
    ppermute x3 -> x6, waiting for transfers between devices: 4.98 us -> 0.02 us  [the longest x1 0.01 us: on_device(): near_x = lax.ppermute(own_x, 'y_lo', swap)]
    all_to_all x1, waiting for transfers between devices: 9.27 us -> 5.78 us  [on_device(): moved = lax.all_to_all(half, 'z', 0, 0)]
    ppermute x1, waiting for transfers between devices: 0.01 us -> 2.85 us  [on_device(): gains = gains + lax.ppermute(gains, 'x', [(0, 3), (3, 0), (1, 2), (2, 1)])]
  transfers between devices with their start and end apart: 8 -> 11, of which waited for: 5 -> 5; matrix products, arithmetic and copies ran while one was open for 0% -> 0% of each run, Pallas kernels for 9% -> 9%
where the time goes in v7:
time: 121 us
  Pallas kernels  41.4 us (34%)
  starting transfers between devices  29.6 us (24%)
  blocking collectives  26.1 us (22%)
  waiting for transfers between devices  20.4 us (17%)
  between operations  2.06 us (2%)
  local copies, waits for them, and re-layouts  1.27 us (1%)
    pallas_call x1, Pallas kernels, pair_call(): pl.pallas_call(pair_kernel, out_shape=(jax.ShapeDtypeStruct((C, WIDTH), b...  28.4 us
    psum x1, blocking collectives, on_device(): gains = lax.psum(gains, 'z')  17.8 us
    pallas_call x1, Pallas kernels, input_call(): pl.pallas_call(input_kernel, out_shape=(jax.ShapeDtypeStruct((BAND, C), b...  10.7 us
    all_gather x1, blocking collectives, on_device(): whole = lax.all_gather(total_call(moved), SPACE_AXES, axis=0, tiled=False)  8.31 us
    all_to_all x1, starting transfers between devices, on_device(): moved = lax.all_to_all(half, 'z', 0, 0)  8.17 us
    all_to_all x1, waiting for transfers between devices, on_device(): moved = lax.all_to_all(wire.reshape(8, 80, WIDTH), ('x', 'y_hi'), 0, 0)  7.14 us
    all_to_all x1, starting transfers between devices, on_device(): moved = lax.all_to_all(wire.reshape(8, 80, WIDTH), ('x', 'y_hi'), 0, 0)  6.83 us
    all_to_all x1, waiting for transfers between devices, on_device(): moved = lax.all_to_all(half, 'z', 0, 0)  5.78 us
  transfers between devices with their start and end apart: 11, of which 5 were waited for; matrix products, arithmetic and copies ran while one was open for 0% of the time, Pallas kernels for 9%

profile of v7, /device:TPU:1, one launch (start us, length us, event | category | flops | bytes accessed | tf_op | source)
XLA Modules:
  0.0 120.9 jit_solution(6859864952925262388)
XLA Ops:
  0.6 2.2 %collective-permute-start = (bf16[128,640]{1,0:T(8,128)(2,1)}, bf16[128,640]{1,0:T(8,128)(2,1)S(1)}, u32[]{:S(2)}, u32[]{:S(2)}) collective-permute-start(bf16[128,640]{1,0:T(8,128)(2,1)} %bitcast.21), channel_id=1, source_target_pairs={{0,2},{2,0},{1,3},{3,1},{4,6},{6,4},{5,7},{7,5},{8,10},{10,8},{9,1... | collective-permute-start | bytes 491528 | tf_op jit(solution)/shard_map/ppermute | solution.py:622
  2.8 0.1 collective-permute-start.3
  2.9 3.0 %collective-permute-start.1 = (bf16[128,640]{1,0:T(8,128)(2,1)}, bf16[128,640]{1,0:T(8,128)(2,1)S(1)}, u32[]{:S(2)}, u32[]{:S(2)}) collective-permute-start(bf16[128,640]{1,0:T(8,128)(2,1)} %bitcast.22), channel_id=1, source_target_pairs={{0,1},{1,0},{2,3},{3,2},{4,5},{5,4},{6,7},{7,6},{8,9},{9,8},{10,11... | collective-permute-start | bytes 491528 | tf_op jit(solution)/shard_map/ppermute | solution.py:624
  6.0 0.0 collective-permute-start.4
  6.0 0.0 collective-permute-done.y_x_ref
  6.0 0.0 copy-start
  6.0 4.0 %collective-permute-start.2 = (bf16[128,640]{1,0:T(8,128)(2,1)S(1)}, bf16[128,640]{1,0:T(8,128)(2,1)S(1)}, u32[]{:S(2)}, u32[]{:S(2)}) collective-permute-start(bf16[128,640]{1,0:T(8,128)(2,1)S(1)} %collective-permute-done.y_x_ref), channel_id=1, source_target_pairs={{0,1},{1,0},{2,3},{3,2},{4,5},{5,4},{6,7},{7,6},{8,9},{9,8},{10,11... | collective-permute-start | bytes 491528 | tf_op jit(solution)/shard_map/ppermute | solution.py:626
  10.0 0.0 collective-permute-done.3.y_t_ref
  10.0 0.0 copy-start.1
  10.0 1.8 %collective-permute-start.5 = (bf16[128,640]{1,0:T(8,128)(2,1)S(1)}, bf16[128,640]{1,0:T(8,128)(2,1)S(1)}, u32[]{:S(2)}, u32[]{:S(2)}) collective-permute-start(bf16[128,640]{1,0:T(8,128)(2,1)S(1)} %collective-permute-done.3.y_t_ref), channel_id=1, source_target_pairs={{0,1},{1,0},{2,3},{3,2},{4,5},{5,4},{6,7},{7,6},{8,9},{9,8},{10,11... | collective-permute-start | bytes 491528 | tf_op jit(solution)/shard_map/ppermute | solution.py:627
  13.0 0.0 collective-permute-done.1.core_x_ref
  13.0 0.0 copy-start.2
  13.0 0.0 collective-permute-done.4.core_t_ref
  13.1 0.0 copy-start.3
  13.1 0.0 collective-permute-done.2.far_x_ref
  13.1 0.0 copy-start.4
  13.1 0.0 collective-permute-done.5.far_t_ref
  13.1 0.0 copy-start.5
  13.1 0.0 copy-done
  13.1 0.0 copy-done.1
  13.1 0.6 copy-done.2
  13.7 0.1 copy-done.3
  13.8 0.0 copy-done.4
  13.8 0.1 copy-done.5
  13.9 28.4 %pair.1 = (bf16[640,2176]{1,0:T(8,128)(2,1)}, bf16[512,640]{1,0:T(8,128)(2,1)}, bf16[512,640]{1,0:T(8,128)(2,1)}, f32[128,640]{1,0:T(8,128)}, f32[8,640]{1,0:T(8,128)}, /*index=5*/f32[1]{0:T(128)}) custom-call(s32[1]{0:T(128)} %bitcast.part_ref, s32[1]{0:T(128)S(6)} %copy.21.step_ref, s32[1]{0:T(128)S(6)} %copy.22.label_ref, f32[1,2]{1,0:T(1,128)} %error_ref.1, ...), custom_call_target="tpu_custom_call" | custom-call | tf_op jit(solution)/shard_map/pair/pallas_call | solution.py:350
  42.3 6.8 %all-to-all-start = ((bf16[8,80,2176]{2,1,0:T(8,128)(2,1)}), bf16[8,80,2176]{2,1,0:T(8,128)(2,1)S(1)}, u32[]{:S(2)}, u32[]{:S(2)}) async-start(bf16[8,80,2176]{2,1,0:T(8,128)(2,1)} %bitcast.20), calls=%async_computation | async-start | bytes 5570560 | tf_op jit(solution)/shard_map/all_to_all | solution.py:643
  49.1 10.7 %input.1 = (bf16[128,640]{1,0:T(8,128)(2,1)}, f32[2,640]{1,0:T(2,128)}) custom-call(s32[1]{0:T(128)} %bitcast.part_ref, f32[8,640]{1,0:T(8,128)} %get-tuple-element.26.stat_ref, f32[640]{0:T(1024)} %gain_ref.3, bf16[512,640]{1,0:T(8,128)(2,1)} %get-tuple-element.27.cg_ref, bf16[512,640]{1,0:T(8,128)(2,1)} %get-tuple-element.28.x_ref, ...), custom_call_target="tpu_custom_call" | custom-call | flops 4194304000 | bytes 7372800 | tf_op jit(solution)/shard_map/input/pallas_call | solution.py:493
  59.8 17.8 %psum.7 = f32[2,640]{1,0:T(2,128)S(1)} all-reduce(f32[2,640]{1,0:T(2,128)} %get-tuple-element.32), channel_id=1, replica_groups=mesh['x'=4,'z'=8,'y_hi'=2,'y_lo'=2,'core'=2] {'z'}, use_global_device_ids=true, to_apply=%region_0.0 | all-reduce | flops 1280 | bytes 10240 | tf_op jit(solution)/shard_map/psum | solution.py:645
  77.6 2.7 %collective-permute-start.6 = (f32[2,640]{1,0:T(2,128)S(1)}, f32[2,640]{1,0:T(2,128)S(1)}, u32[]{:S(2)}, u32[]{:S(2)}) collective-permute-start(f32[2,640]{1,0:T(2,128)S(1)} %psum.7), channel_id=1, source_target_pairs={{0,4},{4,0},{1,5},{5,1},{2,6},{6,2},{3,7},{7,3},{8,12},{12,8},{9,1... | collective-permute-start | bytes 15368 | tf_op jit(solution)/shard_map/ppermute | solution.py:646
  80.3 2.1 %collective-permute-done.6 = f32[2,640]{1,0:T(2,128)S(1)} collective-permute-done((f32[2,640]{1,0:T(2,128)S(1)}, f32[2,640]{1,0:T(2,128)S(1)}, u32[]{:S(2)}, u32[]{:S(2)}) %collective-permute-start.6) | collective-permute-done | bytes 5152 | tf_op jit(solution)/shard_map/ppermute | solution.py:646
  82.4 7.1 %all-to-all-done.a_ref = bf16[8,80,2176]{2,1,0:T(8,128)(2,1)S(1)} async-done(((bf16[8,80,2176]{2,1,0:T(8,128)(2,1)}), bf16[8,80,2176]{2,1,0:T(8,128)(2,1)S(1)}, u32[]{:S(2)}, u32[]{:S(2)}) %all-to-all-start) | async-done | bytes 2785312 | tf_op jit(solution)/shard_map/all_to_all | solution.py:643
  89.6 1.4 %half.1 = bf16[8,176,128]{2,1,0:T(8,128)(2,1)} custom-call(bf16[8,80,2176]{2,1,0:T(8,128)(2,1)S(1)} %all-to-all-done.a_ref), custom_call_target="tpu_custom_call" | custom-call | tf_op jit(solution)/shard_map/half/pallas_call | solution.py:534
  91.0 8.2 %all-to-all-start.1 = ((bf16[8,176,128]{2,1,0:T(8,128)(2,1)}), bf16[8,176,128]{2,1,0:T(8,128)(2,1)S(1)}, u32[]{:S(2)}, u32[]{:S(2)}) async-start(bf16[8,176,128]{2,1,0:T(8,128)(2,1)} %half.1), calls=%async_computation.1 | async-start | bytes 720896 | tf_op jit(solution)/shard_map/all_to_all | solution.py:649
  99.2 0.0 collective-permute-start.7
  99.2 2.5 %collective-permute-done.7 = f32[2,640]{1,0:T(2,128)S(1)} collective-permute-done((f32[2,640]{1,0:T(2,128)S(1)}, f32[2,640]{1,0:T(2,128)S(1)}, u32[]{:S(2)}, u32[]{:S(2)}) %collective-permute-start.7) | collective-permute-done | bytes 5152 | tf_op jit(solution)/shard_map/ppermute | solution.py:650
  101.6 0.8 collective-permute-start.8
  102.5 2.9 %collective-permute-done.8 = f32[2,640]{1,0:T(2,128)S(1)} collective-permute-done((f32[2,640]{1,0:T(2,128)S(1)}, f32[2,640]{1,0:T(2,128)S(1)}, u32[]{:S(2)}, u32[]{:S(2)}) %collective-permute-start.8) | collective-permute-done | bytes 5152 | tf_op jit(solution)/shard_map/ppermute | solution.py:651
  105.3 0.1 dynamic-slice_add_fusion
  105.4 5.8 %all-to-all-done.1.a_ref = bf16[8,176,128]{2,1,0:T(8,128)(2,1)S(1)} async-done(((bf16[8,176,128]{2,1,0:T(8,128)(2,1)}), bf16[8,176,128]{2,1,0:T(8,128)(2,1)S(1)}, u32[]{:S(2)}, u32[]{:S(2)}) %all-to-all-start.1) | async-done | bytes 360480 | tf_op jit(solution)/shard_map/all_to_all | solution.py:649
  111.2 0.1 total.1
  111.2 0.5 slice_bitcast_fusion
  111.8 8.3 %all-gather = bf16[704,128]{1,0:T(8,128)(2,1)S(1)} all-gather(bf16[176,128]{1,0:T(8,128)(2,1)S(1)} %total.1), channel_id=2, replica_groups=mesh['x'=4,'z'=8,'y_hi'=2,'y_lo'=2,'core'=2] {'y_lo','core'}, dimensions={0}, use_global_device_ids=true | all-gather | bytes 225280 | tf_op jit(solution)/shard_map/all_gather | solution.py:654
  120.1 0.9 unpack.1
  (2 shorter events, 0.0 us)
Async XLA Ops:
  0.6 5.4 %collective-permute-start = (bf16[128,640]{1,0:T(8,128)(2,1)}, bf16[128,640]{1,0:T(8,128)(2,1)S(1)}, u32[]{:S(2)}, u32[]{:S(2)}) collective-permute-start(bf16[128,640]{1,0:T(8,128)(2,1)} %bitcast.21), channel_id=1, source_target_pairs={{0,2},{2,0},{1,3},{3,1},{4,6},{6,4},{5,7},{7,5},{8,10},{10,8},{9,1... | collective-permute-start | bytes 491528 | tf_op jit(solution)/shard_map/ppermute | solution.py:622
  2.8 7.1 %collective-permute-start.3 = (bf16[128,640]{1,0:T(8,128)(2,1)}, bf16[128,640]{1,0:T(8,128)(2,1)S(1)}, u32[]{:S(2)}, u32[]{:S(2)}) collective-permute-start(bf16[128,640]{1,0:T(8,128)(2,1)} %bitcast.24), channel_id=1, source_target_pairs={{0,2},{2,0},{1,3},{3,1},{4,6},{6,4},{5,7},{7,5},{8,10},{10,8},{9,1... | collective-permute-start | bytes 491528 | tf_op jit(solution)/shard_map/ppermute | solution.py:623
  2.9 10.1 %collective-permute-start.1 = (bf16[128,640]{1,0:T(8,128)(2,1)}, bf16[128,640]{1,0:T(8,128)(2,1)S(1)}, u32[]{:S(2)}, u32[]{:S(2)}) collective-permute-start(bf16[128,640]{1,0:T(8,128)(2,1)} %bitcast.22), channel_id=1, source_target_pairs={{0,1},{1,0},{2,3},{3,2},{4,5},{5,4},{6,7},{7,6},{8,9},{9,8},{10,11... | collective-permute-start | bytes 491528 | tf_op jit(solution)/shard_map/ppermute | solution.py:624
  6.0 7.1 %collective-permute-start.4 = (bf16[128,640]{1,0:T(8,128)(2,1)}, bf16[128,640]{1,0:T(8,128)(2,1)S(1)}, u32[]{:S(2)}, u32[]{:S(2)}) collective-permute-start(bf16[128,640]{1,0:T(8,128)(2,1)} %bitcast.25), channel_id=1, source_target_pairs={{0,1},{1,0},{2,3},{3,2},{4,5},{5,4},{6,7},{7,6},{8,9},{9,8},{10,11... | collective-permute-start | bytes 491528 | tf_op jit(solution)/shard_map/ppermute | solution.py:625
  6.0 7.1 %copy-start = (bf16[128,640]{1,0:T(8,128)(2,1)}, bf16[128,640]{1,0:T(8,128)(2,1)S(1)}, u32[]{:S(2)}) copy-start(bf16[128,640]{1,0:T(8,128)(2,1)S(1)} %collective-permute-done.y_x_ref) | copy-start | bytes 491524
  6.0 7.1 %collective-permute-start.2 = (bf16[128,640]{1,0:T(8,128)(2,1)S(1)}, bf16[128,640]{1,0:T(8,128)(2,1)S(1)}, u32[]{:S(2)}, u32[]{:S(2)}) collective-permute-start(bf16[128,640]{1,0:T(8,128)(2,1)S(1)} %collective-permute-done.y_x_ref), channel_id=1, source_target_pairs={{0,1},{1,0},{2,3},{3,2},{4,5},{5,4},{6,7},{7,6},{8,9},{9,8},{10,11... | collective-permute-start | bytes 491528 | tf_op jit(solution)/shard_map/ppermute | solution.py:626
  10.0 3.1 %copy-start.1 = (bf16[128,640]{1,0:T(8,128)(2,1)}, bf16[128,640]{1,0:T(8,128)(2,1)S(1)}, u32[]{:S(2)}) copy-start(bf16[128,640]{1,0:T(8,128)(2,1)S(1)} %collective-permute-done.3.y_t_ref) | copy-start | bytes 491524
  10.0 3.1 %collective-permute-start.5 = (bf16[128,640]{1,0:T(8,128)(2,1)S(1)}, bf16[128,640]{1,0:T(8,128)(2,1)S(1)}, u32[]{:S(2)}, u32[]{:S(2)}) collective-permute-start(bf16[128,640]{1,0:T(8,128)(2,1)S(1)} %collective-permute-done.3.y_t_ref), channel_id=1, source_target_pairs={{0,1},{1,0},{2,3},{3,2},{4,5},{5,4},{6,7},{7,6},{8,9},{9,8},{10,11... | collective-permute-start | bytes 491528 | tf_op jit(solution)/shard_map/ppermute | solution.py:627
  13.0 0.7 copy-start.2
  13.1 0.7 copy-start.3
  13.1 0.7 copy-start.4
  13.1 0.8 copy-start.5
  42.3 47.3 %all-to-all-start = ((bf16[8,80,2176]{2,1,0:T(8,128)(2,1)}), bf16[8,80,2176]{2,1,0:T(8,128)(2,1)S(1)}, u32[]{:S(2)}, u32[]{:S(2)}) async-start(bf16[8,80,2176]{2,1,0:T(8,128)(2,1)} %bitcast.20), calls=%async_computation | async-start | bytes 5570560 | tf_op jit(solution)/shard_map/all_to_all | solution.py:643
  77.6 4.9 %collective-permute-start.6 = (f32[2,640]{1,0:T(2,128)S(1)}, f32[2,640]{1,0:T(2,128)S(1)}, u32[]{:S(2)}, u32[]{:S(2)}) collective-permute-start(f32[2,640]{1,0:T(2,128)S(1)} %psum.7), channel_id=1, source_target_pairs={{0,4},{4,0},{1,5},{5,1},{2,6},{6,2},{3,7},{7,3},{8,12},{12,8},{9,1... | collective-permute-start | bytes 15368 | tf_op jit(solution)/shard_map/ppermute | solution.py:646
  91.0 20.2 %all-to-all-start.1 = ((bf16[8,176,128]{2,1,0:T(8,128)(2,1)}), bf16[8,176,128]{2,1,0:T(8,128)(2,1)S(1)}, u32[]{:S(2)}, u32[]{:S(2)}) async-start(bf16[8,176,128]{2,1,0:T(8,128)(2,1)} %half.1), calls=%async_computation.1 | async-start | bytes 720896 | tf_op jit(solution)/shard_map/all_to_all | solution.py:649
  99.2 2.5 %collective-permute-start.7 = (f32[2,640]{1,0:T(2,128)S(1)}, f32[2,640]{1,0:T(2,128)S(1)}, u32[]{:S(2)}, u32[]{:S(2)}) collective-permute-start(f32[2,640]{1,0:T(2,128)S(1)} %add.24), channel_id=1, source_target_pairs={{0,64},{64,0},{128,192},{192,128},{1,65},{65,1},{129,193},{193,129... | collective-permute-start | bytes 15368 | tf_op jit(solution)/shard_map/ppermute | solution.py:650
  101.6 3.7 %collective-permute-start.8 = (f32[2,640]{1,0:T(2,128)S(1)}, f32[2,640]{1,0:T(2,128)S(1)}, u32[]{:S(2)}, u32[]{:S(2)}) collective-permute-start(f32[2,640]{1,0:T(2,128)S(1)} %add.25), channel_id=1, source_target_pairs={{0,192},{192,0},{64,128},{128,64},{1,193},{193,1},{65,129},{129,65... | collective-permute-start | bytes 15368 | tf_op jit(solution)/shard_map/ppermute | solution.py:651

commit v8 on v7

--- a/solution.py
+++ b/solution.py
@@ -291,7 +291,9 @@
     for x in range(4):
         low = 128 * x
         pick = jnp.where(lane[:, 0:IMG] == own_cols + 32 * x, 1.0, 0.0).astype(bf16)
-        turned[160 * x : 160 * (x + 1), :] = dot(pick, cg_s[:, low : low + IMG], NT).astype(bf16)
+        rows = dot(pick, cg_s[:, low : low + IMG], NT).astype(bf16)
+        turned[80 * x : 80 * (x + 1), :] = rows[0:80]
+        turned[320 + 80 * x : 400 + 80 * x, :] = rows[80:160]
     for k in range(TAP_BLOCKS):
         place = part * TAP_BLOCKS + k
         cols = slice(k * 128, (k + 1) * 128)
@@ -324,7 +326,9 @@
         cols = wire_columns(3 * OWN, C) + OWN * part
         for x, low in enumerate((0, 384, 896, 1280)):
             pick = jnp.where(at == cols + (480 * x - low), 1.0, 0.0).astype(bf16)
-            turned[160 * x : 160 * (x + 1), :] = dot(pick, gall[:, low : low + C], NT).astype(bf16)
+            rows = dot(pick, gall[:, low : low + C], NT).astype(bf16)
+            turned[80 * x : 80 * (x + 1), :] = rows[0:80]
+            turned[320 + 80 * x : 400 + 80 * x, :] = rows[80:160]
         wire_s[:, 0:C] = dot(turned[...], resid[...]).astype(bf16)
 
     @pl.when(part == 3)
@@ -332,9 +336,11 @@
         for x in range(4):
             low = 3 * C + 128 * x
             pick = jnp.where(lane[:, 0:IMG] == own_cols + 32 * x, 1.0, 0.0).astype(bf16)
-            turned[160 * x : 160 * (x + 1), :] = dot(pick, gall[:, low : low + IMG], NT).astype(
+            rows = dot(pick, gall[:, low : low + IMG], NT).astype(
                 bf16
             )
+            turned[80 * x : 80 * (x + 1), :] = rows[0:80]
+            turned[320 + 80 * x : 400 + 80 * x, :] = rows[80:160]
         wire_s[:, 0:C] = dot(turned[...], attended[...]).astype(bf16)
 
     store = pltpu.make_async_copy(wire_s.at[:, 0:C], wire_ref.at[:, 0:C], sems.at[11])
@@ -640,7 +646,7 @@
         out_weight,
         time_weight,
     )
-    moved = lax.all_to_all(wire.reshape(8, 80, WIDTH), ("x", "y_hi"), 0, 0)
+    moved = lax.all_to_all(wire.reshape(8, 80, WIDTH), ("y_hi", "x"), 0, 0)
     input_grad, gains = input_call(part, stat, norm_gain, cg, x, own, conv)
     gains = lax.psum(gains, "z")
     gains = gains + lax.ppermute(gains, "y_hi", swap)

time: 121 us -> 121 us (level)
  the two profiles are of different devices: /device:TPU:1 before, /device:TPU:7 now
where the time goes in v8:
time: 121 us
  Pallas kernels  41.4 us (34%)
  blocking collectives  25.9 us (21%)
  starting transfers between devices  25.2 us (21%)
  waiting for transfers between devices  24.8 us (20%)
  between operations  2.07 us (2%)
  local copies, waits for them, and re-layouts  1.27 us (1%)
    pallas_call x1, Pallas kernels, pair_call(): pl.pallas_call(pair_kernel, out_shape=(jax.ShapeDtypeStruct((C, WIDTH), b...  28.4 us
    psum x1, blocking collectives, on_device(): gains = lax.psum(gains, 'z')  17.5 us
    pallas_call x1, Pallas kernels, input_call(): pl.pallas_call(input_kernel, out_shape=(jax.ShapeDtypeStruct((BAND, C), b...  10.7 us
    all_gather x1, blocking collectives, on_device(): whole = lax.all_gather(total_call(moved), SPACE_AXES, axis=0, tiled=False)  8.39 us
    all_to_all x1, starting transfers between devices, on_device(): moved = lax.all_to_all(half, 'z', 0, 0)  8.21 us
    all_to_all x1, waiting for transfers between devices, on_device(): moved = lax.all_to_all(wire.reshape(8, 80, WIDTH), ('y_hi', 'x'), 0, 0)  7.78 us
    all_to_all x1, starting transfers between devices, on_device(): moved = lax.all_to_all(wire.reshape(8, 80, WIDTH), ('y_hi', 'x'), 0, 0)  6.86 us
    all_to_all x1, waiting for transfers between devices, on_device(): moved = lax.all_to_all(half, 'z', 0, 0)  5.7 us
  transfers between devices with their start and end apart: 11, of which 7 were waited for; matrix products, arithmetic and copies ran while one was open for 0% of the time, Pallas kernels for 9%

profile of v8, /device:TPU:7, one launch (start us, length us, event | category | flops | bytes accessed | tf_op | source)
XLA Modules:
  0.0 120.7 jit_solution(756106060157104201)
XLA Ops:
  0.6 1.4 %collective-permute-start = (bf16[128,640]{1,0:T(8,128)(2,1)}, bf16[128,640]{1,0:T(8,128)(2,1)S(1)}, u32[]{:S(2)}, u32[]{:S(2)}) collective-permute-start(bf16[128,640]{1,0:T(8,128)(2,1)} %bitcast.21), channel_id=1, source_target_pairs={{0,2},{2,0},{1,3},{3,1},{4,6},{6,4},{5,7},{7,5},{8,10},{10,8},{9,1... | collective-permute-start | bytes 491528 | tf_op jit(solution)/shard_map/ppermute | solution.py:628
  2.0 0.2 collective-permute-start.3
  2.2 1.2 %collective-permute-start.1 = (bf16[128,640]{1,0:T(8,128)(2,1)}, bf16[128,640]{1,0:T(8,128)(2,1)S(1)}, u32[]{:S(2)}, u32[]{:S(2)}) collective-permute-start(bf16[128,640]{1,0:T(8,128)(2,1)} %bitcast.22), channel_id=1, source_target_pairs={{0,1},{1,0},{2,3},{3,2},{4,5},{5,4},{6,7},{7,6},{8,9},{9,8},{10,11... | collective-permute-start | bytes 491528 | tf_op jit(solution)/shard_map/ppermute | solution.py:630
  3.4 0.0 collective-permute-start.4
  3.4 2.6 %collective-permute-done.y_x_ref = bf16[128,640]{1,0:T(8,128)(2,1)S(1)} collective-permute-done((bf16[128,640]{1,0:T(8,128)(2,1)}, bf16[128,640]{1,0:T(8,128)(2,1)S(1)}, u32[]{:S(2)}, u32[]{:S(2)}) %collective-permute-start) | collective-permute-done | bytes 163872 | tf_op jit(solution)/shard_map/ppermute | solution.py:628
  6.0 0.0 copy-start
  6.0 2.7 %collective-permute-start.2 = (bf16[128,640]{1,0:T(8,128)(2,1)S(1)}, bf16[128,640]{1,0:T(8,128)(2,1)S(1)}, u32[]{:S(2)}, u32[]{:S(2)}) collective-permute-start(bf16[128,640]{1,0:T(8,128)(2,1)S(1)} %collective-permute-done.y_x_ref), channel_id=1, source_target_pairs={{0,1},{1,0},{2,3},{3,2},{4,5},{5,4},{6,7},{7,6},{8,9},{9,8},{10,11... | collective-permute-start | bytes 491528 | tf_op jit(solution)/shard_map/ppermute | solution.py:632
  8.7 0.8 collective-permute-done.3.y_t_ref
  9.5 0.0 copy-start.1
  9.5 1.5 %collective-permute-start.5 = (bf16[128,640]{1,0:T(8,128)(2,1)S(1)}, bf16[128,640]{1,0:T(8,128)(2,1)S(1)}, u32[]{:S(2)}, u32[]{:S(2)}) collective-permute-start(bf16[128,640]{1,0:T(8,128)(2,1)S(1)} %collective-permute-done.3.y_t_ref), channel_id=1, source_target_pairs={{0,1},{1,0},{2,3},{3,2},{4,5},{5,4},{6,7},{7,6},{8,9},{9,8},{10,11... | collective-permute-start | bytes 491528 | tf_op jit(solution)/shard_map/ppermute | solution.py:633
  12.4 0.0 collective-permute-done.1.core_x_ref
  12.4 0.0 copy-start.2
  12.4 0.0 collective-permute-done.4.core_t_ref
  12.4 0.0 copy-start.3
  12.4 0.0 collective-permute-done.2.far_x_ref
  12.4 0.0 copy-start.4
  12.4 0.0 collective-permute-done.5.far_t_ref
  12.4 0.0 copy-start.5
  12.4 0.0 copy-done
  12.5 0.0 copy-done.1
  12.5 0.6 copy-done.2
  13.0 0.1 copy-done.3
  13.1 0.0 copy-done.4
  13.1 0.1 copy-done.5
  13.2 28.4 %pair.1 = (bf16[640,2176]{1,0:T(8,128)(2,1)}, bf16[512,640]{1,0:T(8,128)(2,1)}, bf16[512,640]{1,0:T(8,128)(2,1)}, f32[128,640]{1,0:T(8,128)}, f32[8,640]{1,0:T(8,128)}, /*index=5*/f32[1]{0:T(128)}) custom-call(s32[1]{0:T(128)} %bitcast.part_ref, s32[1]{0:T(128)S(6)} %copy.21.step_ref, s32[1]{0:T(128)S(6)} %copy.22.label_ref, f32[1,2]{1,0:T(1,128)} %error_ref.1, ...), custom_call_target="tpu_custom_call" | custom-call | tf_op jit(solution)/shard_map/pair/pallas_call | solution.py:356
  41.6 6.9 %all-to-all-start = ((bf16[8,80,2176]{2,1,0:T(8,128)(2,1)}), bf16[8,80,2176]{2,1,0:T(8,128)(2,1)S(1)}, u32[]{:S(2)}, u32[]{:S(2)}) async-start(bf16[8,80,2176]{2,1,0:T(8,128)(2,1)} %bitcast.20), calls=%async_computation | async-start | bytes 5570560 | tf_op jit(solution)/shard_map/all_to_all | solution.py:649
  48.5 10.7 %input.1 = (bf16[128,640]{1,0:T(8,128)(2,1)}, f32[2,640]{1,0:T(2,128)}) custom-call(s32[1]{0:T(128)} %bitcast.part_ref, f32[8,640]{1,0:T(8,128)} %get-tuple-element.26.stat_ref, f32[640]{0:T(1024)} %gain_ref.3, bf16[512,640]{1,0:T(8,128)(2,1)} %get-tuple-element.27.cg_ref, bf16[512,640]{1,0:T(8,128)(2,1)} %get-tuple-element.28.x_ref, ...), custom_call_target="tpu_custom_call" | custom-call | flops 4194304000 | bytes 7372800 | tf_op jit(solution)/shard_map/input/pallas_call | solution.py:499
  59.1 17.5 %psum.7 = f32[2,640]{1,0:T(2,128)S(1)} all-reduce(f32[2,640]{1,0:T(2,128)} %get-tuple-element.32), channel_id=1, replica_groups=mesh['x'=4,'z'=8,'y_hi'=2,'y_lo'=2,'core'=2] {'z'}, use_global_device_ids=true, to_apply=%region_0.0 | all-reduce | flops 1280 | bytes 10240 | tf_op jit(solution)/shard_map/psum | solution.py:651
  76.7 3.1 %collective-permute-start.6 = (f32[2,640]{1,0:T(2,128)S(1)}, f32[2,640]{1,0:T(2,128)S(1)}, u32[]{:S(2)}, u32[]{:S(2)}) collective-permute-start(f32[2,640]{1,0:T(2,128)S(1)} %psum.7), channel_id=1, source_target_pairs={{0,4},{4,0},{1,5},{5,1},{2,6},{6,2},{3,7},{7,3},{8,12},{12,8},{9,1... | collective-permute-start | bytes 15368 | tf_op jit(solution)/shard_map/ppermute | solution.py:652
  79.7 1.8 %collective-permute-done.6 = f32[2,640]{1,0:T(2,128)S(1)} collective-permute-done((f32[2,640]{1,0:T(2,128)S(1)}, f32[2,640]{1,0:T(2,128)S(1)}, u32[]{:S(2)}, u32[]{:S(2)}) %collective-permute-start.6) | collective-permute-done | bytes 5152 | tf_op jit(solution)/shard_map/ppermute | solution.py:652
  81.5 7.8 %all-to-all-done.a_ref = bf16[8,80,2176]{2,1,0:T(8,128)(2,1)S(1)} async-done(((bf16[8,80,2176]{2,1,0:T(8,128)(2,1)}), bf16[8,80,2176]{2,1,0:T(8,128)(2,1)S(1)}, u32[]{:S(2)}, u32[]{:S(2)}) %all-to-all-start) | async-done | bytes 2785312 | tf_op jit(solution)/shard_map/all_to_all | solution.py:649
  89.3 1.4 %half.1 = bf16[8,176,128]{2,1,0:T(8,128)(2,1)} custom-call(bf16[8,80,2176]{2,1,0:T(8,128)(2,1)S(1)} %all-to-all-done.a_ref), custom_call_target="tpu_custom_call" | custom-call | tf_op jit(solution)/shard_map/half/pallas_call | solution.py:540
  90.7 8.2 %all-to-all-start.1 = ((bf16[8,176,128]{2,1,0:T(8,128)(2,1)}), bf16[8,176,128]{2,1,0:T(8,128)(2,1)S(1)}, u32[]{:S(2)}, u32[]{:S(2)}) async-start(bf16[8,176,128]{2,1,0:T(8,128)(2,1)} %half.1), calls=%async_computation.1 | async-start | bytes 720896 | tf_op jit(solution)/shard_map/all_to_all | solution.py:655
  99.0 0.0 collective-permute-start.7
  99.0 2.5 %collective-permute-done.7 = f32[2,640]{1,0:T(2,128)S(1)} collective-permute-done((f32[2,640]{1,0:T(2,128)S(1)}, f32[2,640]{1,0:T(2,128)S(1)}, u32[]{:S(2)}, u32[]{:S(2)}) %collective-permute-start.7) | collective-permute-done | bytes 5152 | tf_op jit(solution)/shard_map/ppermute | solution.py:656
  101.4 0.0 collective-permute-start.8
  101.4 3.7 %collective-permute-done.8 = f32[2,640]{1,0:T(2,128)S(1)} collective-permute-done((f32[2,640]{1,0:T(2,128)S(1)}, f32[2,640]{1,0:T(2,128)S(1)}, u32[]{:S(2)}, u32[]{:S(2)}) %collective-permute-start.8) | collective-permute-done | bytes 5152 | tf_op jit(solution)/shard_map/ppermute | solution.py:657
  105.1 0.1 dynamic-slice_add_fusion
  105.2 5.7 %all-to-all-done.1.a_ref = bf16[8,176,128]{2,1,0:T(8,128)(2,1)S(1)} async-done(((bf16[8,176,128]{2,1,0:T(8,128)(2,1)}), bf16[8,176,128]{2,1,0:T(8,128)(2,1)S(1)}, u32[]{:S(2)}, u32[]{:S(2)}) %all-to-all-start.1) | async-done | bytes 360480 | tf_op jit(solution)/shard_map/all_to_all | solution.py:655
  110.9 0.1 total.1
  110.9 0.5 slice_bitcast_fusion
  111.5 8.4 %all-gather = bf16[704,128]{1,0:T(8,128)(2,1)S(1)} all-gather(bf16[176,128]{1,0:T(8,128)(2,1)S(1)} %total.1), channel_id=2, replica_groups=mesh['x'=4,'z'=8,'y_hi'=2,'y_lo'=2,'core'=2] {'y_lo','core'}, dimensions={0}, use_global_device_ids=true | all-gather | bytes 225280 | tf_op jit(solution)/shard_map/all_gather | solution.py:660
  119.9 0.9 unpack.1
  (2 shorter events, 0.0 us)
Async XLA Ops:
  0.6 5.4 %collective-permute-start = (bf16[128,640]{1,0:T(8,128)(2,1)}, bf16[128,640]{1,0:T(8,128)(2,1)S(1)}, u32[]{:S(2)}, u32[]{:S(2)}) collective-permute-start(bf16[128,640]{1,0:T(8,128)(2,1)} %bitcast.21), channel_id=1, source_target_pairs={{0,2},{2,0},{1,3},{3,1},{4,6},{6,4},{5,7},{7,5},{8,10},{10,8},{9,1... | collective-permute-start | bytes 491528 | tf_op jit(solution)/shard_map/ppermute | solution.py:628
  2.0 7.5 %collective-permute-start.3 = (bf16[128,640]{1,0:T(8,128)(2,1)}, bf16[128,640]{1,0:T(8,128)(2,1)S(1)}, u32[]{:S(2)}, u32[]{:S(2)}) collective-permute-start(bf16[128,640]{1,0:T(8,128)(2,1)} %bitcast.24), channel_id=1, source_target_pairs={{0,2},{2,0},{1,3},{3,1},{4,6},{6,4},{5,7},{7,5},{8,10},{10,8},{9,1... | collective-permute-start | bytes 491528 | tf_op jit(solution)/shard_map/ppermute | solution.py:629
  2.2 10.2 %collective-permute-start.1 = (bf16[128,640]{1,0:T(8,128)(2,1)}, bf16[128,640]{1,0:T(8,128)(2,1)S(1)}, u32[]{:S(2)}, u32[]{:S(2)}) collective-permute-start(bf16[128,640]{1,0:T(8,128)(2,1)} %bitcast.22), channel_id=1, source_target_pairs={{0,1},{1,0},{2,3},{3,2},{4,5},{5,4},{6,7},{7,6},{8,9},{9,8},{10,11... | collective-permute-start | bytes 491528 | tf_op jit(solution)/shard_map/ppermute | solution.py:630
  3.4 9.0 %collective-permute-start.4 = (bf16[128,640]{1,0:T(8,128)(2,1)}, bf16[128,640]{1,0:T(8,128)(2,1)S(1)}, u32[]{:S(2)}, u32[]{:S(2)}) collective-permute-start(bf16[128,640]{1,0:T(8,128)(2,1)} %bitcast.25), channel_id=1, source_target_pairs={{0,1},{1,0},{2,3},{3,2},{4,5},{5,4},{6,7},{7,6},{8,9},{9,8},{10,11... | collective-permute-start | bytes 491528 | tf_op jit(solution)/shard_map/ppermute | solution.py:631
  6.0 6.4 %copy-start = (bf16[128,640]{1,0:T(8,128)(2,1)}, bf16[128,640]{1,0:T(8,128)(2,1)S(1)}, u32[]{:S(2)}) copy-start(bf16[128,640]{1,0:T(8,128)(2,1)S(1)} %collective-permute-done.y_x_ref) | copy-start | bytes 491524
  6.0 6.4 %collective-permute-start.2 = (bf16[128,640]{1,0:T(8,128)(2,1)S(1)}, bf16[128,640]{1,0:T(8,128)(2,1)S(1)}, u32[]{:S(2)}, u32[]{:S(2)}) collective-permute-start(bf16[128,640]{1,0:T(8,128)(2,1)S(1)} %collective-permute-done.y_x_ref), channel_id=1, source_target_pairs={{0,1},{1,0},{2,3},{3,2},{4,5},{5,4},{6,7},{7,6},{8,9},{9,8},{10,11... | collective-permute-start | bytes 491528 | tf_op jit(solution)/shard_map/ppermute | solution.py:632
  9.5 2.9 %copy-start.1 = (bf16[128,640]{1,0:T(8,128)(2,1)}, bf16[128,640]{1,0:T(8,128)(2,1)S(1)}, u32[]{:S(2)}) copy-start(bf16[128,640]{1,0:T(8,128)(2,1)S(1)} %collective-permute-done.3.y_t_ref) | copy-start | bytes 491524
  9.5 2.9 %collective-permute-start.5 = (bf16[128,640]{1,0:T(8,128)(2,1)S(1)}, bf16[128,640]{1,0:T(8,128)(2,1)S(1)}, u32[]{:S(2)}, u32[]{:S(2)}) collective-permute-start(bf16[128,640]{1,0:T(8,128)(2,1)S(1)} %collective-permute-done.3.y_t_ref), channel_id=1, source_target_pairs={{0,1},{1,0},{2,3},{3,2},{4,5},{5,4},{6,7},{7,6},{8,9},{9,8},{10,11... | collective-permute-start | bytes 491528 | tf_op jit(solution)/shard_map/ppermute | solution.py:633
  12.4 0.7 copy-start.2
  12.4 0.7 copy-start.3
  12.4 0.7 copy-start.4
  12.4 0.8 copy-start.5
  41.6 47.7 %all-to-all-start = ((bf16[8,80,2176]{2,1,0:T(8,128)(2,1)}), bf16[8,80,2176]{2,1,0:T(8,128)(2,1)S(1)}, u32[]{:S(2)}, u32[]{:S(2)}) async-start(bf16[8,80,2176]{2,1,0:T(8,128)(2,1)} %bitcast.20), calls=%async_computation | async-start | bytes 5570560 | tf_op jit(solution)/shard_map/all_to_all | solution.py:649
  76.7 4.9 %collective-permute-start.6 = (f32[2,640]{1,0:T(2,128)S(1)}, f32[2,640]{1,0:T(2,128)S(1)}, u32[]{:S(2)}, u32[]{:S(2)}) collective-permute-start(f32[2,640]{1,0:T(2,128)S(1)} %psum.7), channel_id=1, source_target_pairs={{0,4},{4,0},{1,5},{5,1},{2,6},{6,2},{3,7},{7,3},{8,12},{12,8},{9,1... | collective-permute-start | bytes 15368 | tf_op jit(solution)/shard_map/ppermute | solution.py:652
  90.7 20.1 %all-to-all-start.1 = ((bf16[8,176,128]{2,1,0:T(8,128)(2,1)}), bf16[8,176,128]{2,1,0:T(8,128)(2,1)S(1)}, u32[]{:S(2)}, u32[]{:S(2)}) async-start(bf16[8,176,128]{2,1,0:T(8,128)(2,1)} %half.1), calls=%async_computation.1 | async-start | bytes 720896 | tf_op jit(solution)/shard_map/all_to_all | solution.py:655
  99.0 2.5 %collective-permute-start.7 = (f32[2,640]{1,0:T(2,128)S(1)}, f32[2,640]{1,0:T(2,128)S(1)}, u32[]{:S(2)}, u32[]{:S(2)}) collective-permute-start(f32[2,640]{1,0:T(2,128)S(1)} %add.24), channel_id=1, source_target_pairs={{0,64},{64,0},{128,192},{192,128},{1,65},{65,1},{129,193},{193,129... | collective-permute-start | bytes 15368 | tf_op jit(solution)/shard_map/ppermute | solution.py:656
  101.4 3.7 %collective-permute-start.8 = (f32[2,640]{1,0:T(2,128)S(1)}, f32[2,640]{1,0:T(2,128)S(1)}, u32[]{:S(2)}, u32[]{:S(2)}) collective-permute-start(f32[2,640]{1,0:T(2,128)S(1)} %add.25), channel_id=1, source_target_pairs={{0,192},{192,0},{64,128},{128,64},{1,193},{193,1},{65,129},{129,65... | collective-permute-start | bytes 15368 | tf_op jit(solution)/shard_map/ppermute | solution.py:657
